TPU v7x, 32 devices: a whole 2x2x4 slice. The times are simulated.
32 devices in a mesh: row: 8 (over y, x, core), col: 4 (over z).
Axes of the slice: x: 2, y: 2, z: 4, core: 2. Of those that a mesh axis runs over, the one named last changes fastest.
Arguments:
- pair_cc: bfloat16 [2, 2048, 6144], P(None, 'row', 'col'), may hold values from -6 to 6
- screened: bfloat16 [2, 6144, 6144], P(None, 'row', 'col'), may hold values from -0.078125 to 0.078125
- pair_vv: bfloat16 [2, 512, 6144], P(None, 'col', 'row'), may hold values from -0.078125 to 0.078125
Outputs:
- kernel: float32 [2, 2048, 512], P(None, 'row', 'col')
All inputs are finite; a program needn't handle non-finite values.
Results may differ from a plain program's by a relative error of at most 0.0003.
Values may be sent and summed in bfloat16 or wider, within the bound.
No kernel may reach another device: no remote copies, remote signals or barrier semaphores. Data moves between devices by JAX's collectives and lax.ppermute only.
A program may use at most 64 MiB of HBM per device.

v0:
```python
import jax
import jax.numpy as jnp
from jax import lax
from jax.sharding import PartitionSpec as P


def half_nt(left, right):
    return lax.dot_general(
        left, right, (((1,), (1,)), ((), ())), preferred_element_type=jnp.float32
    )


def split_parts(values):
    upper = values.astype(jnp.bfloat16)
    lower = (values - upper.astype(jnp.float32)).astype(jnp.bfloat16)
    return (upper, lower)


def mixed_nn(data, inter):
    upper, lower = split_parts(inter)
    return jnp.dot(data, upper, preferred_element_type=jnp.float32) + jnp.dot(
        data, lower, preferred_element_type=jnp.float32
    )


def shards(pair_cc, screened, pair_vv):
    cc_whole = lax.all_gather(pair_cc, "col", axis=2, tiled=True)
    vv_whole = lax.all_gather(pair_vv, "row", axis=2, tiled=True)
    piece = lax.all_gather(screened, "col", axis=2, tiled=True)
    inner_re = half_nt(piece[0], vv_whole[0]) - half_nt(piece[1], vv_whole[1])
    inner_im = half_nt(piece[0], vv_whole[1]) + half_nt(piece[1], vv_whole[0])
    right_block = jnp.stack([inner_re, inner_im])
    piece = lax.all_gather(right_block, "row", axis=1, tiled=True)
    out_re = mixed_nn(cc_whole[0], piece[0]) + mixed_nn(cc_whole[1], piece[1])
    out_im = mixed_nn(cc_whole[0], piece[1]) - mixed_nn(cc_whole[1], piece[0])
    return jnp.stack([out_re, out_im])


def solution(mesh):
    placed = (P(None, "row", "col"), P(None, "row", "col"), P(None, "col", "row"))
    return jax.shard_map(
        shards, mesh=mesh, in_specs=placed, out_specs=P(None, "row", "col"), check_vma=False
    )
```

profile of v0, /device:TPU:0, one launch (start us, length us, event | category | flops | bytes accessed | tf_op | source)
XLA Modules:
  0.0 569.8 jit_solution(13128695449572960410)
XLA Ops:
  6.5 0.0 all-gather.7.cloned.1.call-start
  6.5 0.7 all-gather.7.cloned.1.call-update
  7.3 0.0 all-gather.5.cloned.1.call-start
  7.3 0.7 all-gather.5.cloned.1.call-update
  8.0 0.0 all-gather.9.cloned.1.call-start
  8.1 36.2 %all-gather.7.cloned.1.call-done = bf16[2,128,6144]{2,1,0:T(8,128)(2,1)} async-done(((bf16[2,128,768]{2,1,0:T(8,128)(2,1)}), bf16[2,128,6144]{2,1,0:T(8,128)(2,1)}) %all-gather.7.cloned.1.call-update) | async-done | bytes 3145744 | tf_op jit(solution)/shard_map/all_gather | solution.py:28
  44.2 324.2 %all-gather.5.cloned.1.call-done = bf16[2,768,6144]{2,1,0:T(8,128)(2,1)} async-done(((bf16[2,768,1536]{2,1,0:T(8,128)(2,1)}), bf16[2,768,6144]{2,1,0:T(8,128)(2,1)}) %all-gather.5.cloned.1.call-update) | async-done | bytes 18874384 | tf_op jit(solution)/shard_map/all_gather | solution.py:29
  368.5 6.1 %fusion.1 = f32[768,128]{1,0:T(8,128)S(1)} fusion(bf16[2,768,6144]{2,1,0:T(8,128)(2,1)} %all-gather.5.cloned.1.call-done, bf16[2,128,6144]{2,1,0:T(8,128)(2,1)} %all-gather.7.cloned.1.call-done), kind=kOutput, calls=%fused_computation.3 | convolution fusion | flops 1207959552 | bytes 11403264 | tf_op jit(solution)/shard_map/dot_general | solution.py:8
  374.6 0.0 slice-start.5
  374.6 0.0 slice-start.6
  374.6 5.9 %fusion = f32[768,128]{1,0:T(8,128)S(1)} fusion(bf16[2,768,6144]{2,1,0:T(8,128)(2,1)} %all-gather.5.cloned.1.call-done, bf16[2,128,6144]{2,1,0:T(8,128)(2,1)S(1)} %copy-done.1), kind=kOutput, calls=%fused_computation.2 | convolution fusion | flops 1207959552 | bytes 11403264 | tf_op jit(solution)/shard_map/dot_general | solution.py:8
  380.6 0.5 slice-done.6
  381.1 2.6 fusion.19
  383.7 2.7 fusion.21
  386.4 1.0 pad_maximum_fusion
  387.4 0.0 all-gather.9.cloned.1.call-update
  387.4 0.2 all-gather.11.cloned.1.call-start
  387.7 0.3 all-gather.11.cloned.1.call-update
  388.0 43.9 %all-gather.9.cloned.1.call-done = f32[2,6144,128]{2,1,0:T(8,128)} async-done(((f32[2,768,128]{2,1,0:T(8,128)}), f32[2,6144,128]{2,1,0:T(8,128)}) %all-gather.9.cloned.1.call-update) | async-done | bytes 6291472 | tf_op jit(solution)/shard_map/all_gather | solution.py:33
  432.0 3.3 fusion.34
  435.2 113.6 %all-gather.11.cloned.1.call-done = bf16[2,256,6144]{2,1,0:T(8,128)(2,1)} async-done(((bf16[2,256,1536]{2,1,0:T(8,128)(2,1)}), bf16[2,256,6144]{2,1,0:T(8,128)(2,1)}) %all-gather.11.cloned.1.call-update) | async-done | bytes 6291472 | tf_op jit(solution)/shard_map/all_gather | solution.py:27
  548.8 3.2 fusion.11
  552.0 0.0 slice-start
  552.0 3.2 fusion.5
  555.2 0.0 slice-start.1
  555.2 1.2 fusion.7
  556.4 1.2 fusion.9
  557.6 1.2 fusion.28
  558.8 1.2 fusion.29
  560.0 1.2 fusion.24
  561.2 1.2 fusion.27
  562.4 0.8 copy.4
  (16 shorter events, 0.0 us)
Async XLA Ops:
  6.5 37.7 %all-gather.7.cloned.1.call-start = ((), (), s32[]{:S(2)}) async-start(), calls=%async_computation.1 | async-start | bytes 3538944 | tf_op jit(solution)/shard_map/all_gather | solution.py:28
  7.3 361.2 %all-gather.5.cloned.1.call-start = ((), (), s32[]{:S(2)}) async-start(), calls=%async_computation | async-start | bytes 23592960 | tf_op jit(solution)/shard_map/all_gather | solution.py:29
  8.0 424.0 %all-gather.9.cloned.1.call-start = ((), (), s32[]{:S(2)}) async-start(), calls=%async_computation.2 | async-start | bytes 7077888 | tf_op jit(solution)/shard_map/all_gather | solution.py:33
  44.2 330.3 %copy-start.1 = (bf16[2,128,6144]{2,1,0:T(8,128)(2,1)S(1)}, bf16[2,128,6144]{2,1,0:T(8,128)(2,1)}, u32[]{:S(2)}) copy-start(bf16[2,128,6144]{2,1,0:T(8,128)(2,1)} %all-gather.7.cloned.1.call-done) | copy-start | bytes 9437188
  368.4 12.1 %slice-start.2 = ((s8[18874368]{0:T(1024)(128)(4,1)}), s8[4194304]{0:T(1024)(128)(4,1)S(1)}, s32[]{:S(2)}) async-start(s8[18874368]{0:T(1024)(128)(4,1)} %bitcast.92), calls=%async_computation.6 | async-start | bytes 8388608
  368.4 12.1 %slice-start.3 = ((s8[18874368]{0:T(1024)(128)(4,1)}), s8[4194304]{0:T(1024)(128)(4,1)S(1)}, s32[]{:S(2)}) async-start(s8[18874368]{0:T(1024)(128)(4,1)} %bitcast.92), calls=%async_computation.7 | async-start | bytes 8388608
  368.4 12.1 %slice-start.4 = ((s8[18874368]{0:T(1024)(128)(4,1)}), s8[4194304]{0:T(1024)(128)(4,1)S(1)}, s32[]{:S(2)}) async-start(s8[18874368]{0:T(1024)(128)(4,1)} %bitcast.92), calls=%async_computation.8 | async-start | bytes 8388608
  374.6 5.9 %slice-start.5 = ((s8[18874368]{0:T(1024)(128)(4,1)}), s8[4194304]{0:T(1024)(128)(4,1)S(1)}, s32[]{:S(2)}) async-start(s8[18874368]{0:T(1024)(128)(4,1)} %bitcast.92), calls=%async_computation.9 | async-start | bytes 8388608
  374.6 6.5 %slice-start.6 = ((s8[18874368]{0:T(1024)(128)(4,1)}), s8[2097152]{0:T(1024)(128)(4,1)S(1)}, s32[]{:S(2)}) async-start(s8[18874368]{0:T(1024)(128)(4,1)} %bitcast.92), calls=%async_computation.10 | async-start | bytes 4194304
  387.4 161.3 %all-gather.11.cloned.1.call-start = ((), (), s32[]{:S(2)}) async-start(), calls=%async_computation.3 | async-start | bytes 7864320 | tf_op jit(solution)/shard_map/all_gather | solution.py:27
  548.8 6.4 %copy-start = (bf16[2,256,6144]{2,1,0:T(8,128)(2,1)S(1)}, bf16[2,256,6144]{2,1,0:T(8,128)(2,1)}, u32[]{:S(2)}) copy-start(bf16[2,256,6144]{2,1,0:T(8,128)(2,1)} %all-gather.11.cloned.1.call-done) | copy-start | bytes 18874372
  552.0 5.6 slice-start
  555.2 2.4 slice-start.1
Sparse Core Ops, SparseCore 0:
  9.3 34.9 all-gather.6
  45.8 322.5 all-gather.4
  387.6 44.3 all-gather.8
  433.4 115.3 all-gather.10
where the time goes:
time: 570 us
  waiting for transfers between devices  520 us (91%)
  matrix products  30.8 us (5%)
  between operations  13.3 us (2%)
    all_gather x1, waiting for transfers between devices, shards(): piece = lax.all_gather(screened, 'col', axis=2, tiled=True)  324 us
    all_gather x1, waiting for transfers between devices, shards(): cc_whole = lax.all_gather(pair_cc, 'col', axis=2, tiled=True)  114 us
    all_gather x1, waiting for transfers between devices, shards(): piece = lax.all_gather(right_block, 'row', axis=1, tiled=True)  43.9 us
    all_gather x1, waiting for transfers between devices, shards(): vv_whole = lax.all_gather(pair_vv, 'row', axis=2, tiled=True)  36.2 us
    dot_general x4, matrix products, half_nt(): lax.dot_general(left, right, (((1,), (1,)), ((), ())), preferred_element_...  17.3 us
  transfers between devices with their start and end apart: 4, of which 4 were waited for; matrix products, arithmetic and copies ran while one was open for 1% of the time, Pallas kernels for 0%

commit v1 on v0

--- a/solution.py
+++ b/solution.py
@@ -1,7 +1,18 @@
+import functools
+
 import jax
 import jax.numpy as jnp
 from jax import lax
+from jax.experimental import pallas as pl
+from jax.experimental.pallas import tpu as pltpu
 from jax.sharding import PartitionSpec as P
+
+LANES = 128
+HEAD = 16
+SPAN = 126.0
+CHUNKS = 2
+BF = jnp.bfloat16
+F32 = jnp.float32
 
 
 def half_nt(left, right):
@@ -23,7 +34,7 @@
     )
 
 
-def shards(pair_cc, screened, pair_vv):
+def gathered(pair_cc, screened, pair_vv):
     cc_whole = lax.all_gather(pair_cc, "col", axis=2, tiled=True)
     vv_whole = lax.all_gather(pair_vv, "row", axis=2, tiled=True)
     piece = lax.all_gather(screened, "col", axis=2, tiled=True)
@@ -36,8 +47,322 @@
     return jnp.stack([out_re, out_im])
 
 
+def bound_of(top):
+    top = jnp.max(top, axis=(0, 1), keepdims=True)
+    top = jnp.maximum(top, 1e-30) * (1.0 + 2.0**-7)
+    return top.astype(BF).astype(F32)
+
+
+def fold_top(values):
+    return jnp.max(jnp.abs(values).reshape(-1, 8, LANES), axis=0)
+
+
+def code(values, bound):
+    return jnp.exp2(values * (SPAN / bound)).astype(BF)
+
+
+def decode(coded, bound):
+    return jnp.log2(coded.astype(F32)) * (bound * (1.0 / SPAN))
+
+
+def head_of(ref):
+    return ref[0:1, :].astype(F32)
+
+
+def put_head(ref, bound):
+    ref[0:HEAD, :] = jnp.broadcast_to(bound, (HEAD, LANES)).astype(BF)
+
+
+def call(body, outs, scratch, name, args, flops=0):
+    nbytes = sum(a.size * a.dtype.itemsize for a in args) + sum(
+        functools.reduce(lambda p, q: p * q, o.shape) * o.dtype.itemsize for o in outs
+    )
+    specs = [pl.BlockSpec(memory_space=pltpu.SMEM)] + [
+        pl.BlockSpec(memory_space=pltpu.VMEM)
+    ] * (len(args) - 1)
+    return pl.pallas_call(
+        body,
+        out_shape=outs,
+        in_specs=specs,
+        out_specs=[pl.BlockSpec(memory_space=pltpu.VMEM)] * len(outs),
+        scratch_shapes=scratch,
+        compiler_params=pltpu.CompilerParams(vmem_limit_bytes=48 * 1024 * 1024),
+        cost_estimate=pl.CostEstimate(
+            flops=flops, bytes_accessed=nbytes, transcendentals=0
+        ),
+        name=name,
+    )(*args)
+
+
+def route_body(parts, where_ref, *refs):
+    ins, outs = refs[:parts], refs[parts:]
+    m = where_ref[3]
+    for v in range(parts):
+
+        @pl.when(m == v)
+        def _(v=v):
+            for d in range(parts):
+                outs[d][...] = ins[v ^ d][...]
+
+
+def inner_body(parts, cores, rows, where_ref, w_ref, *refs):
+    n_in = parts * cores
+    ins, outs = refs[:n_in], refs[n_in : n_in + parts]
+    x_ref, t_ref = refs[n_in + parts :]
+    width = ins[0].shape[1]
+    core = where_ref[1]
+    group = ins[0].shape[0]
+    for c in range(cores):
+        at = pl.multiple_of((core ^ c) * width, LANES)
+        for i in range(parts):
+            x_ref[i * group : (i + 1) * group, pl.ds(at, width)] = ins[
+                c * parts + i
+            ][...]
+    n_g = w_ref.shape[1]
+    tops = [jnp.zeros((8, LANES), F32) for _ in range(parts)]
+    tile = 256
+    for g in range(0, n_g, tile):
+        with_re = half_nt(x_ref[...], w_ref[0, g : g + tile, :])
+        with_im = half_nt(x_ref[...], w_ref[1, g : g + tile, :])
+        with_re = with_re.reshape(-1, 2, rows, tile)
+        with_im = with_im.reshape(-1, 2, rows, tile)
+        t_re = with_re[:, 0] - with_im[:, 1]
+        t_im = with_im[:, 0] + with_re[:, 1]
+        both = jnp.stack([t_re, t_im], axis=1).reshape(-1, tile)
+        for i in range(parts):
+            mine = both[i * group : (i + 1) * group]
+            for l in range(0, tile, LANES):
+                block = mine[:, l : l + LANES]
+                tops[i] = jnp.maximum(tops[i], fold_top(block))
+                t_ref[i, (g + l) // LANES] = block
+    for i in range(parts):
+        bound = bound_of(tops[i])
+        put_head(outs[i], bound)
+        for l in range(n_g // LANES):
+            at = HEAD + l * group
+            outs[i][at : at + group, :] = code(t_ref[i, l], bound)
+
+
+def sum_body(parts, where_ref, *refs):
+    ins, out = refs[:parts], refs[parts]
+    t_ref = refs[parts + 1]
+    n_l, group = t_ref.shape[0], t_ref.shape[1]
+    step = group // parts
+    top = jnp.zeros((8, LANES), F32)
+    bounds = [head_of(ins[d]) for d in range(parts)]
+    for l in range(n_l):
+        for s in range(parts):
+            total = None
+            for d in range(parts):
+                at = HEAD + l * group + (s ^ d) * step
+                term = decode(ins[d][at : at + step, :], bounds[d])
+                total = term if total is None else total + term
+            top = jnp.maximum(top, fold_top(total))
+            t_ref[l, s * step : (s + 1) * step, :] = total
+    bound = bound_of(top)
+    put_head(out, bound)
+    for l in range(n_l):
+        at = HEAD + l * group
+        out[at : at + group, :] = code(t_ref[l], bound)
+
+
+def outer_body(parts, cores, rows, where_ref, a_ref, *refs):
+    n_in = parts * cores
+    ins, outs = refs[:n_in], refs[n_in : n_in + parts]
+    hi_ref, lo_ref = refs[n_in + parts :]
+    core = where_ref[1]
+    n_k = hi_ref.shape[1]
+    width = n_k // cores
+    group = (ins[0].shape[0] - HEAD) // (width // LANES)
+    for c in range(cores):
+        for i in range(parts):
+            ref = ins[c * parts + i]
+            bound = head_of(ref)
+            for l in range(width // LANES):
+                at = HEAD + l * group
+                values = decode(ref[at : at + group, :], bound)
+                upper, lower = split_parts(values)
+                lane = pl.multiple_of((core ^ c) * width + l * LANES, LANES)
+                hi_ref[i * group : (i + 1) * group, pl.ds(lane, LANES)] = upper
+                lo_ref[i * group : (i + 1) * group, pl.ds(lane, LANES)] = lower
+    n_p = a_ref.shape[1]
+    with_re = half_nt(hi_ref[...], a_ref[0]) + half_nt(lo_ref[...], a_ref[0])
+    with_im = half_nt(hi_ref[...], a_ref[1]) + half_nt(lo_ref[...], a_ref[1])
+    with_re = with_re.reshape(parts, parts, 2, rows, n_p)
+    with_im = with_im.reshape(parts, parts, 2, rows, n_p)
+    k_re = with_re[:, :, 0] + with_im[:, :, 1]
+    k_im = with_re[:, :, 1] - with_im[:, :, 0]
+    for d in range(parts):
+        both = jnp.stack([k_re[:, d], k_im[:, d]], axis=1).reshape(-1, n_p)
+        if d == 0:
+            outs[0][...] = both
+            continue
+        top = jnp.zeros((8, LANES), F32)
+        for l in range(0, n_p, LANES):
+            top = jnp.maximum(top, fold_top(both[:, l : l + LANES]))
+        bound = bound_of(top)
+        put_head(outs[d], bound)
+        n_r = both.shape[0]
+        for l in range(n_p // LANES):
+            at = HEAD + l * n_r
+            outs[d][at : at + n_r, :] = code(both[:, l * LANES : (l + 1) * LANES], bound)
+
+
+def last_body(parts, chunks, rows, where_ref, *refs):
+    ins, out = refs[: parts * chunks], refs[parts * chunks]
+    k_ref = refs[parts * chunks + 1]
+    t = where_ref[0]
+    n_p = out.shape[1]
+    sub = rows * chunks
+    for e in range(chunks):
+        mine = ins[e * parts]
+        n_r = mine.shape[0]
+        bounds = [None] + [head_of(ins[e * parts + d]) for d in range(1, parts)]
+        for l in range(n_p // LANES):
+            total = mine[:, l * LANES : (l + 1) * LANES]
+            for d in range(1, parts):
+                at = HEAD + l * n_r
+                total = total + decode(ins[e * parts + d][at : at + n_r, :], bounds[d])
+            total = total.reshape(parts, 2, rows, LANES)
+            for i in range(parts):
+                at = pl.multiple_of((t ^ i) * sub + e * rows, 8)
+                for part in range(2):
+                    k_ref[
+                        part, pl.ds(at, rows), l * LANES : (l + 1) * LANES
+                    ] = total[i, part]
+    for part in range(2):
+        out[part] = k_ref[part].T
+
+
+def stationary(n_row, n_col, pair_cc, screened, pair_vv):
+    parts, cores, chunks = n_col, n_row // n_col, CHUNKS
+    n_q, width = pair_vv.shape[1:]
+    n_p, n_k = pair_cc.shape[1:]
+    n_g = screened.shape[1]
+    sub = n_q // parts
+    rows = sub // chunks
+    group = parts * 2 * rows
+    r, z = lax.axis_index("row"), lax.axis_index("col")
+    t, core = r // cores, r % cores
+    where = jnp.stack([t, core, z, t ^ z]).astype(jnp.int32)
+
+    def plane(x, i):
+        pairs = [(a, ((a // cores) ^ i) * cores + a % cores) for a in range(n_row)]
+        return lax.ppermute(x, "row", pairs)
+
+    def twin(x, c):
+        return lax.ppermute(x, "row", [(a, a ^ c) for a in range(n_row)])
+
+    def along(x, d):
+        return lax.ppermute(x, "col", [(a, a ^ d) for a in range(parts)])
+
+    def route(arrays, name):
+        outs = [jax.ShapeDtypeStruct(a.shape, a.dtype) for a in arrays]
+        return call(
+            functools.partial(route_body, parts), outs, [], name, [where, *arrays]
+        )
+
+    def twins(arrays):
+        return list(arrays) + [twin(a, c) for c in range(1, cores) for a in arrays]
+
+    with jax.named_scope("spread_vv"):
+        cut = pair_vv.reshape(2, parts, sub, width)
+        mine = [
+            lax.dynamic_index_in_dim(cut, t ^ i, 1, keepdims=False).reshape(
+                2 * sub, width
+            )
+            for i in range(parts)
+        ]
+        mine = [mine[0]] + [plane(mine[i], i) for i in range(1, parts)]
+        mine = route(mine, "route_vv")
+        mine = [mine[0]] + [along(mine[d], d) for d in range(1, parts)]
+    finals = []
+    for e in range(chunks):
+        with jax.named_scope("gather_vv"):
+            own = jnp.stack(
+                [
+                    m.reshape(2, sub, width)[:, e * rows : (e + 1) * rows]
+                    for m in mine
+                ]
+            ).reshape(group, width)
+            groups = twins([own] + [plane(own, i) for i in range(1, parts)])
+        with jax.named_scope("inner"):
+            coded = jax.ShapeDtypeStruct((HEAD + n_g // LANES * group, LANES), BF)
+            inner = call(
+                functools.partial(inner_body, parts, cores, rows),
+                [coded] * parts,
+                [
+                    pltpu.VMEM((parts * group, cores * width), BF),
+                    pltpu.VMEM((parts, n_g // LANES, group, LANES), F32),
+                ],
+                "inner",
+                [where, screened, *groups],
+                flops=2 * parts * group * cores * width * 2 * n_g,
+            )
+        with jax.named_scope("move_inner"):
+            inner = [inner[0]] + [plane(inner[i], i) for i in range(1, parts)]
+            inner = route(inner, "route_inner")
+            inner = [inner[0]] + [along(inner[d], d) for d in range(1, parts)]
+        with jax.named_scope("sum_inner"):
+            (total,) = call(
+                functools.partial(sum_body, parts),
+                [coded],
+                [pltpu.VMEM((n_g // LANES, group, LANES), F32)],
+                "sum_inner",
+                [where, *inner],
+            )
+        with jax.named_scope("gather_inner"):
+            totals = twins([total] + [plane(total, i) for i in range(1, parts)])
+        with jax.named_scope("outer"):
+            term = jax.ShapeDtypeStruct((HEAD + n_p // LANES * group, LANES), BF)
+            outer = call(
+                functools.partial(outer_body, parts, cores, rows),
+                [jax.ShapeDtypeStruct((group, n_p), F32)] + [term] * (parts - 1),
+                [pltpu.VMEM((parts * group, n_k), BF)] * 2,
+                "outer",
+                [where, pair_cc, *totals],
+                flops=4 * parts * group * n_k * 2 * n_p,
+            )
+        with jax.named_scope("move_outer"):
+            finals += [outer[0]] + [along(outer[d], d) for d in range(1, parts)]
+    with jax.named_scope("sum_outer"):
+        (result,) = call(
+            functools.partial(last_body, parts, chunks, rows),
+            [jax.ShapeDtypeStruct((2, n_p, n_q), F32)],
+            [pltpu.VMEM((2, n_q, n_p), F32)],
+            "sum_outer",
+            [where, *finals],
+        )
+    return result
+
+
+def power_of_two(n):
+    return n > 0 and n & (n - 1) == 0
+
+
 def solution(mesh):
     placed = (P(None, "row", "col"), P(None, "row", "col"), P(None, "col", "row"))
+    n_row, n_col = mesh.shape["row"], mesh.shape["col"]
+
+    def shards(pair_cc, screened, pair_vv):
+        n_q, width = pair_vv.shape[1:]
+        n_p, n_k = pair_cc.shape[1:]
+        n_g = screened.shape[1]
+        fits = (
+            power_of_two(n_row)
+            and power_of_two(n_col)
+            and n_row % n_col == 0
+            and n_q % (n_col * CHUNKS * 16) == 0
+            and width % LANES == 0
+            and n_g == width
+            and n_g % 256 == 0
+            and n_p % LANES == 0
+            and n_k == width * (n_row // n_col)
+        )
+        if not fits:
+            return gathered(pair_cc, screened, pair_vv)
+        return stationary(n_row, n_col, pair_cc, screened, pair_vv)
+
     return jax.shard_map(
         shards, mesh=mesh, in_specs=placed, out_specs=P(None, "row", "col"), check_vma=False
     )

time: 570 us -> 133 us (0.23)
  waiting for transfers between devices: 520 us -> 57.8 us
  starting transfers between devices: 0.3 us -> 50.7 us
  matrix products: 30.8 us -> 0 us
  Pallas kernels: 0 us -> 22.9 us
  between operations: 13.3 us -> 0.16 us
    all_gather x4 -> x0, waiting for transfers between devices: 518 us -> none  [the longest x1 324 us: shards(): piece = lax.all_gather(screened, 'col', axis=2, tiled=True)]
    ppermute x0 -> x52, waiting for transfers between devices: none -> 57.8 us  [the longest x15 29.6 us: along(): return lax.ppermute(x, 'col', [(a, a ^ d) for a in range(parts)])]
    ppermute x0 -> x52, starting transfers between devices: none -> 50.7 us  [the longest x21 24.4 us: plane(): return lax.ppermute(x, 'row', pairs)]
    dot_general x12 -> x0, matrix products: 30.8 us -> none  [the longest x4 17.3 us: half_nt(): lax.dot_general(left, right, (((1,), (1,)), ((), ())), preferred_element_...]
    pallas_call x0 -> x10, Pallas kernels: none -> 22.9 us  [call(): pl.pallas_call(body, out_shape=outs, in_specs=specs, out_specs=[pl.BlockS...]
  transfers between devices with their start and end apart: 4 -> 52, of which waited for: 4 -> 19; matrix products, arithmetic and copies ran while one was open for 1% -> 0% of each run, Pallas kernels for 0% -> 16%
where the time goes in v1:
time: 133 us
  waiting for transfers between devices  57.8 us (43%)
  starting transfers between devices  50.7 us (38%)
  Pallas kernels  22.9 us (17%)
    ppermute x15, waiting for transfers between devices, along(): return lax.ppermute(x, 'col', [(a, a ^ d) for a in range(parts)])  29.6 us
    ppermute x21, waiting for transfers between devices, plane(): return lax.ppermute(x, 'row', pairs)  28.1 us
    ppermute x21, starting transfers between devices, plane(): return lax.ppermute(x, 'row', pairs)  24.4 us
    ppermute x15, starting transfers between devices, along(): return lax.ppermute(x, 'col', [(a, a ^ d) for a in range(parts)])  23.3 us
    pallas_call x10, Pallas kernels, call(): pl.pallas_call(body, out_shape=outs, in_specs=specs, out_specs=[pl.BlockS...  22.9 us
    ppermute x16, starting transfers between devices, twin(): return lax.ppermute(x, 'row', [(a, a ^ c) for a in range(n_row)])  3.07 us
  transfers between devices with their start and end apart: 52, of which 19 were waited for; matrix products, arithmetic and copies ran while one was open for 0% of the time, Pallas kernels for 16%

profile of v1, /device:TPU:0, one launch (start us, length us, event | category | flops | bytes accessed | tf_op | source)
XLA Modules:
  0.0 132.8 jit_solution(8120870474433655085)
XLA Ops:
  1.1 3.0 %collective-permute-start = (bf16[64,768]{1,0:T(8,128)(2,1)S(1)}, bf16[64,768]{1,0:T(8,128)(2,1)S(1)}, u32[]{:S(2)}, u32[]{:S(2)}) collective-permute-start(bf16[64,768]{1,0:T(8,128)(2,1)S(1)} %bitcast.54), channel_id=1, source_target_pairs={{0,8},{4,12},{8,0},{12,4},{16,24},{20,28},{24,16},{28,20},{1,9},{5... | collective-permute-start | bytes 294920 | tf_op jit(solution)/shard_map/spread_vv/ppermute | solution.py:251
  4.1 1.5 %collective-permute-start.1 = (bf16[64,768]{1,0:T(8,128)(2,1)S(1)}, bf16[64,768]{1,0:T(8,128)(2,1)S(1)}, u32[]{:S(2)}, u32[]{:S(2)}) collective-permute-start(bf16[64,768]{1,0:T(8,128)(2,1)S(1)} %bitcast.53), channel_id=1, source_target_pairs={{0,16},{4,20},{8,24},{12,28},{16,0},{20,4},{24,8},{28,12},{1,17},{... | collective-permute-start | bytes 294920 | tf_op jit(solution)/shard_map/spread_vv/ppermute | solution.py:251
  7.1 2.6 %collective-permute-done.1.refs_2_ = bf16[64,768]{1,0:T(8,128)(2,1)S(1)} collective-permute-done((bf16[64,768]{1,0:T(8,128)(2,1)S(1)}, bf16[64,768]{1,0:T(8,128)(2,1)S(1)}, u32[]{:S(2)}, u32[]{:S(2)}) %collective-permute-start.1) | collective-permute-done | bytes 98336 | tf_op jit(solution)/shard_map/spread_vv/ppermute | solution.py:251
  11.7 1.6 %collective-permute-start.3 = (bf16[64,768]{1,0:T(8,128)(2,1)S(1)}, bf16[64,768]{1,0:T(8,128)(2,1)S(1)}, u32[]{:S(2)}, u32[]{:S(2)}) collective-permute-start(bf16[64,768]{1,0:T(8,128)(2,1)S(1)} %get-tuple-element.34), channel_id=1, source_target_pairs={{0,1},{1,0},{2,3},{3,2},{4,5},{5,4},{6,7},{7,6},{8,9},{9,8},{10,11... | collective-permute-start | bytes 294920 | tf_op jit(solution)/shard_map/spread_vv/ppermute | solution.py:257
  13.3 2.6 %collective-permute-start.4 = (bf16[64,768]{1,0:T(8,128)(2,1)S(1)}, bf16[64,768]{1,0:T(8,128)(2,1)S(1)}, u32[]{:S(2)}, u32[]{:S(2)}) collective-permute-start(bf16[64,768]{1,0:T(8,128)(2,1)S(1)} %get-tuple-element.35), channel_id=1, source_target_pairs={{0,2},{1,3},{2,0},{3,1},{4,6},{5,7},{6,4},{7,5},{8,10},{9,11},{10,... | collective-permute-start | bytes 294920 | tf_op jit(solution)/shard_map/spread_vv/ppermute | solution.py:257
  16.8 4.3 %collective-permute-done.4 = bf16[64,768]{1,0:T(8,128)(2,1)S(1)} collective-permute-done((bf16[64,768]{1,0:T(8,128)(2,1)S(1)}, bf16[64,768]{1,0:T(8,128)(2,1)S(1)}, u32[]{:S(2)}, u32[]{:S(2)}) %collective-permute-start.4) | collective-permute-done | bytes 98336 | tf_op jit(solution)/shard_map/spread_vv/ppermute | solution.py:257
  24.3 1.7 %collective-permute-start.31 = (bf16[128,768]{1,0:T(8,128)(2,1)S(1)}, bf16[128,768]{1,0:T(8,128)(2,1)S(1)}, u32[]{:S(2)}, u32[]{:S(2)}) collective-permute-start(bf16[128,768]{1,0:T(8,128)(2,1)S(1)} %bitcast.47), channel_id=1, source_target_pairs={{0,24},{4,28},{8,16},{12,20},{16,8},{20,12},{24,0},{28,4},{1,25},{... | collective-permute-start | bytes 589832 | tf_op jit(solution)/shard_map/gather_vv/ppermute | solution.py:251
  27.4 1.8 %collective-permute-done.29.refs_1_ = bf16[128,768]{1,0:T(8,128)(2,1)S(1)} collective-permute-done((bf16[128,768]{1,0:T(8,128)(2,1)S(1)}, bf16[128,768]{1,0:T(8,128)(2,1)S(1)}, u32[]{:S(2)}, u32[]{:S(2)}) %collective-permute-start.29) | collective-permute-done | bytes 196640 | tf_op jit(solution)/shard_map/gather_vv/ppermute | solution.py:251
  29.9 1.9 %collective-permute-done.30.refs_2_ = bf16[128,768]{1,0:T(8,128)(2,1)S(1)} collective-permute-done((bf16[128,768]{1,0:T(8,128)(2,1)S(1)}, bf16[128,768]{1,0:T(8,128)(2,1)S(1)}, u32[]{:S(2)}, u32[]{:S(2)}) %collective-permute-start.30) | collective-permute-done | bytes 196640 | tf_op jit(solution)/shard_map/gather_vv/ppermute | solution.py:251
  33.7 3.7 %collective-permute-done.6.refs_1_ = bf16[128,768]{1,0:T(8,128)(2,1)S(1)} collective-permute-done((bf16[128,768]{1,0:T(8,128)(2,1)S(1)}, bf16[128,768]{1,0:T(8,128)(2,1)S(1)}, u32[]{:S(2)}, u32[]{:S(2)}) %collective-permute-start.6) | collective-permute-done | bytes 196640 | tf_op jit(solution)/shard_map/gather_vv/ppermute | solution.py:251
  37.5 3.1 %collective-permute-done.7.refs_2_ = bf16[128,768]{1,0:T(8,128)(2,1)S(1)} collective-permute-done((bf16[128,768]{1,0:T(8,128)(2,1)S(1)}, bf16[128,768]{1,0:T(8,128)(2,1)S(1)}, u32[]{:S(2)}, u32[]{:S(2)}) %collective-permute-start.7) | collective-permute-done | bytes 196640 | tf_op jit(solution)/shard_map/gather_vv/ppermute | solution.py:251
  41.6 5.4 %inner.3 = (bf16[784,128]{1,0:T(8,128)(2,1)S(1)}, bf16[784,128]{1,0:T(8,128)(2,1)S(1)}, bf16[784,128]{1,0:T(8,128)(2,1)S(1)}, bf16[784,128]{1,0:T(8,128)(2,1)S(1)}) custom-call(s32[4]{0:T(128)S(1)} %pad_add_fusion.where_ref, bf16[2,768,1536]{2,1,0:T(8,128)(2,1)} %w_ref.3, bf16[128,768]{1,0:T(8,128)(2,1)S(1)} %bitcast.49, ...), custom_call_target="tpu_custom_call" | custom-call | flops 2415919104 | bytes 7094288 | tf_op jit(solution)/shard_map/inner/inner/pallas_call | solution.py:83
  48.5 2.1 %collective-permute-start.38 = (bf16[784,128]{1,0:T(8,128)(2,1)S(1)}, bf16[784,128]{1,0:T(8,128)(2,1)S(1)}, u32[]{:S(2)}, u32[]{:S(2)}) collective-permute-start(bf16[784,128]{1,0:T(8,128)(2,1)S(1)} %get-tuple-element.52), channel_id=1, source_target_pairs={{0,24},{4,28},{8,16},{12,20},{16,8},{20,12},{24,0},{28,4},{1,25},{... | collective-permute-start | bytes 602120 | tf_op jit(solution)/shard_map/move_inner/ppermute | solution.py:251
  50.6 5.4 %inner.2 = (bf16[784,128]{1,0:T(8,128)(2,1)S(1)}, bf16[784,128]{1,0:T(8,128)(2,1)S(1)}, bf16[784,128]{1,0:T(8,128)(2,1)S(1)}, bf16[784,128]{1,0:T(8,128)(2,1)S(1)}) custom-call(s32[4]{0:T(128)S(1)} %pad_add_fusion.where_ref, bf16[2,768,1536]{2,1,0:T(8,128)(2,1)} %w_ref.3, bf16[128,768]{1,0:T(8,128)(2,1)S(1)} %bitcast.44, ...), custom_call_target="tpu_custom_call" | custom-call | flops 2415919104 | bytes 7094288 | tf_op jit(solution)/shard_map/inner/inner/pallas_call | solution.py:83
  57.4 2.1 %collective-permute-start.15 = (bf16[784,128]{1,0:T(8,128)(2,1)S(1)}, bf16[784,128]{1,0:T(8,128)(2,1)S(1)}, u32[]{:S(2)}, u32[]{:S(2)}) collective-permute-start(bf16[784,128]{1,0:T(8,128)(2,1)S(1)} %get-tuple-element.40), channel_id=1, source_target_pairs={{0,24},{4,28},{8,16},{12,20},{16,8},{20,12},{24,0},{28,4},{1,25},{... | collective-permute-start | bytes 602120 | tf_op jit(solution)/shard_map/move_inner/ppermute | solution.py:251
  60.2 2.7 %collective-permute-start.39 = (bf16[784,128]{1,0:T(8,128)(2,1)S(1)}, bf16[784,128]{1,0:T(8,128)(2,1)S(1)}, u32[]{:S(2)}, u32[]{:S(2)}) collective-permute-start(bf16[784,128]{1,0:T(8,128)(2,1)S(1)} %get-tuple-element.54), channel_id=1, source_target_pairs={{0,1},{1,0},{2,3},{3,2},{4,5},{5,4},{6,7},{7,6},{8,9},{9,8},{10,11... | collective-permute-start | bytes 602120 | tf_op jit(solution)/shard_map/move_inner/ppermute | solution.py:257
  64.0 1.9 %collective-permute-start.41 = (bf16[784,128]{1,0:T(8,128)(2,1)S(1)}, bf16[784,128]{1,0:T(8,128)(2,1)S(1)}, u32[]{:S(2)}, u32[]{:S(2)}) collective-permute-start(bf16[784,128]{1,0:T(8,128)(2,1)S(1)} %get-tuple-element.56), channel_id=1, source_target_pairs={{0,3},{1,2},{2,1},{3,0},{4,7},{5,6},{6,5},{7,4},{8,11},{9,10},{10,... | collective-permute-start | bytes 602120 | tf_op jit(solution)/shard_map/move_inner/ppermute | solution.py:257
  65.9 1.7 %collective-permute-done.14.refs_2_ = bf16[784,128]{1,0:T(8,128)(2,1)S(1)} collective-permute-done((bf16[784,128]{1,0:T(8,128)(2,1)S(1)}, bf16[784,128]{1,0:T(8,128)(2,1)S(1)}, u32[]{:S(2)}, u32[]{:S(2)}) %collective-permute-start.14) | collective-permute-done | bytes 200736 | tf_op jit(solution)/shard_map/move_inner/ppermute | solution.py:251
  68.3 2.3 %collective-permute-start.16 = (bf16[784,128]{1,0:T(8,128)(2,1)S(1)}, bf16[784,128]{1,0:T(8,128)(2,1)S(1)}, u32[]{:S(2)}, u32[]{:S(2)}) collective-permute-start(bf16[784,128]{1,0:T(8,128)(2,1)S(1)} %get-tuple-element.42), channel_id=1, source_target_pairs={{0,1},{1,0},{2,3},{3,2},{4,5},{5,4},{6,7},{7,6},{8,9},{9,8},{10,11... | collective-permute-start | bytes 602120 | tf_op jit(solution)/shard_map/move_inner/ppermute | solution.py:257
  71.3 1.7 %collective-permute-start.18 = (bf16[784,128]{1,0:T(8,128)(2,1)S(1)}, bf16[784,128]{1,0:T(8,128)(2,1)S(1)}, u32[]{:S(2)}, u32[]{:S(2)}) collective-permute-start(bf16[784,128]{1,0:T(8,128)(2,1)S(1)} %get-tuple-element.44), channel_id=1, source_target_pairs={{0,3},{1,2},{2,1},{3,0},{4,7},{5,6},{6,5},{7,4},{8,11},{9,10},{10,... | collective-permute-start | bytes 602120 | tf_op jit(solution)/shard_map/move_inner/ppermute | solution.py:257
  73.1 7.3 %collective-permute-done.40.refs_2_ = bf16[784,128]{1,0:T(8,128)(2,1)S(1)} collective-permute-done((bf16[784,128]{1,0:T(8,128)(2,1)S(1)}, bf16[784,128]{1,0:T(8,128)(2,1)S(1)}, u32[]{:S(2)}, u32[]{:S(2)}) %collective-permute-start.40) | collective-permute-done | bytes 200736 | tf_op jit(solution)/shard_map/move_inner/ppermute | solution.py:257
  82.9 1.9 %collective-permute-start.44 = (bf16[784,128]{1,0:T(8,128)(2,1)S(1)}, bf16[784,128]{1,0:T(8,128)(2,1)S(1)}, u32[]{:S(2)}, u32[]{:S(2)}) collective-permute-start(bf16[784,128]{1,0:T(8,128)(2,1)S(1)} %sum_inner.3.refs_0_), channel_id=1, source_target_pairs={{0,24},{4,28},{8,16},{12,20},{16,8},{20,12},{24,0},{28,4},{1,25},{... | collective-permute-start | bytes 602120 | tf_op jit(solution)/shard_map/gather_inner/ppermute | solution.py:251
  84.9 11.7 %collective-permute-done.17.refs_2_ = bf16[784,128]{1,0:T(8,128)(2,1)S(1)} collective-permute-done((bf16[784,128]{1,0:T(8,128)(2,1)S(1)}, bf16[784,128]{1,0:T(8,128)(2,1)S(1)}, u32[]{:S(2)}, u32[]{:S(2)}) %collective-permute-start.17) | collective-permute-done | bytes 200736 | tf_op jit(solution)/shard_map/move_inner/ppermute | solution.py:257
  99.2 1.9 %collective-permute-start.21 = (bf16[784,128]{1,0:T(8,128)(2,1)S(1)}, bf16[784,128]{1,0:T(8,128)(2,1)S(1)}, u32[]{:S(2)}, u32[]{:S(2)}) collective-permute-start(bf16[784,128]{1,0:T(8,128)(2,1)S(1)} %sum_inner.2.refs_0_), channel_id=1, source_target_pairs={{0,24},{4,28},{8,16},{12,20},{16,8},{20,12},{24,0},{28,4},{1,25},{... | collective-permute-start | bytes 602120 | tf_op jit(solution)/shard_map/gather_inner/ppermute | solution.py:251
  101.6 3.8 %collective-permute-done.19.refs_1_ = bf16[784,128]{1,0:T(8,128)(2,1)S(1)} collective-permute-done((bf16[784,128]{1,0:T(8,128)(2,1)S(1)}, bf16[784,128]{1,0:T(8,128)(2,1)S(1)}, u32[]{:S(2)}, u32[]{:S(2)}) %collective-permute-start.19) | collective-permute-done | bytes 200736 | tf_op jit(solution)/shard_map/gather_inner/ppermute | solution.py:251
  105.4 4.8 %collective-permute-done.20.refs_2_ = bf16[784,128]{1,0:T(8,128)(2,1)S(1)} collective-permute-done((bf16[784,128]{1,0:T(8,128)(2,1)S(1)}, bf16[784,128]{1,0:T(8,128)(2,1)S(1)}, u32[]{:S(2)}, u32[]{:S(2)}) %collective-permute-start.20) | collective-permute-done | bytes 200736 | tf_op jit(solution)/shard_map/gather_inner/ppermute | solution.py:251
  111.3 3.4 %outer.3 = (f32[128,256]{1,0:T(8,128)S(1)}, bf16[272,128]{1,0:T(8,128)(2,1)S(1)}, bf16[272,128]{1,0:T(8,128)(2,1)S(1)}, bf16[272,128]{1,0:T(8,128)(2,1)S(1)}) custom-call(s32[4]{0:T(128)S(1)} %pad_add_fusion.where_ref, bf16[2,256,1536]{2,1,0:T(8,128)(2,1)S(1)} %copy-done, bf16[784,128]{1,0:T(8,128)(2,1)S(1)} %sum_inner.3.refs_0_, ...), custom_call_target="tpu_custom_call" | custom-call | flops 1610612736 | bytes 3518480 | tf_op jit(solution)/shard_map/outer/outer/pallas_call | solution.py:83
  117.2 1.9 %collective-permute-start.51 = (bf16[272,128]{1,0:T(8,128)(2,1)S(1)}, bf16[272,128]{1,0:T(8,128)(2,1)S(1)}, u32[]{:S(2)}, u32[]{:S(2)}) collective-permute-start(bf16[272,128]{1,0:T(8,128)(2,1)S(1)} %get-tuple-element.60), channel_id=1, source_target_pairs={{0,3},{1,2},{2,1},{3,0},{4,7},{5,6},{6,5},{7,4},{8,11},{9,10},{10,... | collective-permute-start | bytes 208904 | tf_op jit(solution)/shard_map/move_outer/ppermute | solution.py:257
  119.1 3.4 %outer.2 = (f32[128,256]{1,0:T(8,128)S(1)}, bf16[272,128]{1,0:T(8,128)(2,1)S(1)}, bf16[272,128]{1,0:T(8,128)(2,1)S(1)}, bf16[272,128]{1,0:T(8,128)(2,1)S(1)}) custom-call(s32[4]{0:T(128)S(1)} %pad_add_fusion.where_ref, bf16[2,256,1536]{2,1,0:T(8,128)(2,1)S(1)} %copy-done, bf16[784,128]{1,0:T(8,128)(2,1)S(1)} %sum_inner.2.refs_0_, ...), custom_call_target="tpu_custom_call" | custom-call | flops 1610612736 | bytes 3518480 | tf_op jit(solution)/shard_map/outer/outer/pallas_call | solution.py:83
  123.0 2.1 %collective-permute-start.27 = (bf16[272,128]{1,0:T(8,128)(2,1)S(1)}, bf16[272,128]{1,0:T(8,128)(2,1)S(1)}, u32[]{:S(2)}, u32[]{:S(2)}) collective-permute-start(bf16[272,128]{1,0:T(8,128)(2,1)S(1)} %get-tuple-element.47), channel_id=1, source_target_pairs={{0,2},{1,3},{2,0},{3,1},{4,6},{5,7},{6,4},{7,5},{8,10},{9,11},{10,... | collective-permute-start | bytes 208904 | tf_op jit(solution)/shard_map/move_outer/ppermute | solution.py:257
  125.1 1.9 %collective-permute-start.28 = (bf16[272,128]{1,0:T(8,128)(2,1)S(1)}, bf16[272,128]{1,0:T(8,128)(2,1)S(1)}, u32[]{:S(2)}, u32[]{:S(2)}) collective-permute-start(bf16[272,128]{1,0:T(8,128)(2,1)S(1)} %get-tuple-element.48), channel_id=1, source_target_pairs={{0,3},{1,2},{2,1},{3,0},{4,7},{5,6},{6,5},{7,4},{8,11},{9,10},{10,... | collective-permute-start | bytes 208904 | tf_op jit(solution)/shard_map/move_outer/ppermute | solution.py:257
  127.0 3.0 %collective-permute-done.27.refs_2_ = bf16[272,128]{1,0:T(8,128)(2,1)S(1)} collective-permute-done((bf16[272,128]{1,0:T(8,128)(2,1)S(1)}, bf16[272,128]{1,0:T(8,128)(2,1)S(1)}, u32[]{:S(2)}, u32[]{:S(2)}) %collective-permute-start.27) | collective-permute-done | bytes 69664 | tf_op jit(solution)/shard_map/move_outer/ppermute | solution.py:257
  (92 shorter events, 32.5 us)
Async XLA Ops:
  23.8 8.0 %collective-permute-start.30 = (bf16[128,768]{1,0:T(8,128)(2,1)S(1)}, bf16[128,768]{1,0:T(8,128)(2,1)S(1)}, u32[]{:S(2)}, u32[]{:S(2)}) collective-permute-start(bf16[128,768]{1,0:T(8,128)(2,1)S(1)} %bitcast.46), channel_id=1, source_target_pairs={{0,16},{4,20},{8,24},{12,28},{16,0},{20,4},{24,8},{28,12},{1,17},{... | collective-permute-start | bytes 589832 | tf_op jit(solution)/shard_map/gather_vv/ppermute | solution.py:251
  24.3 8.9 %collective-permute-start.31 = (bf16[128,768]{1,0:T(8,128)(2,1)S(1)}, bf16[128,768]{1,0:T(8,128)(2,1)S(1)}, u32[]{:S(2)}, u32[]{:S(2)}) collective-permute-start(bf16[128,768]{1,0:T(8,128)(2,1)S(1)} %bitcast.47), channel_id=1, source_target_pairs={{0,24},{4,28},{8,16},{12,20},{16,8},{20,12},{24,0},{28,4},{1,25},{... | collective-permute-start | bytes 589832 | tf_op jit(solution)/shard_map/gather_vv/ppermute | solution.py:251
  26.1 11.4 %collective-permute-start.6 = (bf16[128,768]{1,0:T(8,128)(2,1)S(1)}, bf16[128,768]{1,0:T(8,128)(2,1)S(1)}, u32[]{:S(2)}, u32[]{:S(2)}) collective-permute-start(bf16[128,768]{1,0:T(8,128)(2,1)S(1)} %bitcast.40), channel_id=1, source_target_pairs={{0,8},{4,12},{8,0},{12,4},{16,24},{20,28},{24,16},{28,20},{1,9},{5... | collective-permute-start | bytes 589832 | tf_op jit(solution)/shard_map/gather_vv/ppermute | solution.py:251
  29.2 11.4 %collective-permute-start.7 = (bf16[128,768]{1,0:T(8,128)(2,1)S(1)}, bf16[128,768]{1,0:T(8,128)(2,1)S(1)}, u32[]{:S(2)}, u32[]{:S(2)}) collective-permute-start(bf16[128,768]{1,0:T(8,128)(2,1)S(1)} %bitcast.41), channel_id=1, source_target_pairs={{0,16},{4,20},{8,24},{12,28},{16,0},{20,4},{24,8},{28,12},{1,17},{... | collective-permute-start | bytes 589832 | tf_op jit(solution)/shard_map/gather_vv/ppermute | solution.py:251
  31.8 8.8 %collective-permute-start.8 = (bf16[128,768]{1,0:T(8,128)(2,1)S(1)}, bf16[128,768]{1,0:T(8,128)(2,1)S(1)}, u32[]{:S(2)}, u32[]{:S(2)}) collective-permute-start(bf16[128,768]{1,0:T(8,128)(2,1)S(1)} %bitcast.42), channel_id=1, source_target_pairs={{0,24},{4,28},{8,16},{12,20},{16,8},{20,12},{24,0},{28,4},{1,25},{... | collective-permute-start | bytes 589832 | tf_op jit(solution)/shard_map/gather_vv/ppermute | solution.py:251
  33.2 8.0 %collective-permute-start.34 = (bf16[128,768]{1,0:T(8,128)(2,1)S(1)}, bf16[128,768]{1,0:T(8,128)(2,1)S(1)}, u32[]{:S(2)}, u32[]{:S(2)}) collective-permute-start(bf16[128,768]{1,0:T(8,128)(2,1)S(1)} %collective-permute-done.30.refs_2_), channel_id=1, source_target_pairs={{0,4},{4,0},{8,12},{12,8},{16,20},{20,16},{24,28},{28,24},{1,5},{5... | collective-permute-start | bytes 589832 | tf_op jit(solution)/shard_map/gather_vv/ppermute | solution.py:254
  41.1 9.5 %collective-permute-start.11 = (bf16[128,768]{1,0:T(8,128)(2,1)S(1)}, bf16[128,768]{1,0:T(8,128)(2,1)S(1)}, u32[]{:S(2)}, u32[]{:S(2)}) collective-permute-start(bf16[128,768]{1,0:T(8,128)(2,1)S(1)} %collective-permute-done.7.refs_2_), channel_id=1, source_target_pairs={{0,4},{4,0},{8,12},{12,8},{16,20},{20,16},{24,28},{28,24},{1,5},{5... | collective-permute-start | bytes 589832 | tf_op jit(solution)/shard_map/gather_vv/ppermute | solution.py:254
  41.2 9.4 %collective-permute-start.12 = (bf16[128,768]{1,0:T(8,128)(2,1)S(1)}, bf16[128,768]{1,0:T(8,128)(2,1)S(1)}, u32[]{:S(2)}, u32[]{:S(2)}) collective-permute-start(bf16[128,768]{1,0:T(8,128)(2,1)S(1)} %collective-permute-done.8.refs_3_), channel_id=1, source_target_pairs={{0,4},{4,0},{8,12},{12,8},{16,20},{20,16},{24,28},{28,24},{1,5},{5... | collective-permute-start | bytes 589832 | tf_op jit(solution)/shard_map/gather_vv/ppermute | solution.py:254
  47.0 10.4 %collective-permute-start.36 = (bf16[784,128]{1,0:T(8,128)(2,1)S(1)}, bf16[784,128]{1,0:T(8,128)(2,1)S(1)}, u32[]{:S(2)}, u32[]{:S(2)}) collective-permute-start(bf16[784,128]{1,0:T(8,128)(2,1)S(1)} %get-tuple-element.50), channel_id=1, source_target_pairs={{0,8},{4,12},{8,0},{12,4},{16,24},{20,28},{24,16},{28,20},{1,9},{5... | collective-permute-start | bytes 602120 | tf_op jit(solution)/shard_map/move_inner/ppermute | solution.py:251
  48.0 11.6 %collective-permute-start.37 = (bf16[784,128]{1,0:T(8,128)(2,1)S(1)}, bf16[784,128]{1,0:T(8,128)(2,1)S(1)}, u32[]{:S(2)}, u32[]{:S(2)}) collective-permute-start(bf16[784,128]{1,0:T(8,128)(2,1)S(1)} %get-tuple-element.51), channel_id=1, source_target_pairs={{0,16},{4,20},{8,24},{12,28},{16,0},{20,4},{24,8},{28,12},{1,17},{... | collective-permute-start | bytes 602120 | tf_op jit(solution)/shard_map/move_inner/ppermute | solution.py:251
  48.5 11.1 %collective-permute-start.38 = (bf16[784,128]{1,0:T(8,128)(2,1)S(1)}, bf16[784,128]{1,0:T(8,128)(2,1)S(1)}, u32[]{:S(2)}, u32[]{:S(2)}) collective-permute-start(bf16[784,128]{1,0:T(8,128)(2,1)S(1)} %get-tuple-element.52), channel_id=1, source_target_pairs={{0,24},{4,28},{8,16},{12,20},{16,8},{20,12},{24,0},{28,4},{1,25},{... | collective-permute-start | bytes 602120 | tf_op jit(solution)/shard_map/move_inner/ppermute | solution.py:251
  56.0 8.0 %collective-permute-start.13 = (bf16[784,128]{1,0:T(8,128)(2,1)S(1)}, bf16[784,128]{1,0:T(8,128)(2,1)S(1)}, u32[]{:S(2)}, u32[]{:S(2)}) collective-permute-start(bf16[784,128]{1,0:T(8,128)(2,1)S(1)} %get-tuple-element.38), channel_id=1, source_target_pairs={{0,8},{4,12},{8,0},{12,4},{16,24},{20,28},{24,16},{28,20},{1,9},{5... | collective-permute-start | bytes 602120 | tf_op jit(solution)/shard_map/move_inner/ppermute | solution.py:251
  56.9 10.6 %collective-permute-start.14 = (bf16[784,128]{1,0:T(8,128)(2,1)S(1)}, bf16[784,128]{1,0:T(8,128)(2,1)S(1)}, u32[]{:S(2)}, u32[]{:S(2)}) collective-permute-start(bf16[784,128]{1,0:T(8,128)(2,1)S(1)} %get-tuple-element.39), channel_id=1, source_target_pairs={{0,16},{4,20},{8,24},{12,28},{16,0},{20,4},{24,8},{28,12},{1,17},{... | collective-permute-start | bytes 602120 | tf_op jit(solution)/shard_map/move_inner/ppermute | solution.py:251
  57.4 10.1 %collective-permute-start.15 = (bf16[784,128]{1,0:T(8,128)(2,1)S(1)}, bf16[784,128]{1,0:T(8,128)(2,1)S(1)}, u32[]{:S(2)}, u32[]{:S(2)}) collective-permute-start(bf16[784,128]{1,0:T(8,128)(2,1)S(1)} %get-tuple-element.40), channel_id=1, source_target_pairs={{0,24},{4,28},{8,16},{12,20},{16,8},{20,12},{24,0},{28,4},{1,25},{... | collective-permute-start | bytes 602120 | tf_op jit(solution)/shard_map/move_inner/ppermute | solution.py:251
  60.2 11.2 %collective-permute-start.39 = (bf16[784,128]{1,0:T(8,128)(2,1)S(1)}, bf16[784,128]{1,0:T(8,128)(2,1)S(1)}, u32[]{:S(2)}, u32[]{:S(2)}) collective-permute-start(bf16[784,128]{1,0:T(8,128)(2,1)S(1)} %get-tuple-element.54), channel_id=1, source_target_pairs={{0,1},{1,0},{2,3},{3,2},{4,5},{5,4},{6,7},{7,6},{8,9},{9,8},{10,11... | collective-permute-start | bytes 602120 | tf_op jit(solution)/shard_map/move_inner/ppermute | solution.py:257
  62.9 17.5 %collective-permute-start.40 = (bf16[784,128]{1,0:T(8,128)(2,1)S(1)}, bf16[784,128]{1,0:T(8,128)(2,1)S(1)}, u32[]{:S(2)}, u32[]{:S(2)}) collective-permute-start(bf16[784,128]{1,0:T(8,128)(2,1)S(1)} %get-tuple-element.55), channel_id=1, source_target_pairs={{0,2},{1,3},{2,0},{3,1},{4,6},{5,7},{6,4},{7,5},{8,10},{9,11},{10,... | collective-permute-start | bytes 602120 | tf_op jit(solution)/shard_map/move_inner/ppermute | solution.py:257
  64.0 16.4 %collective-permute-start.41 = (bf16[784,128]{1,0:T(8,128)(2,1)S(1)}, bf16[784,128]{1,0:T(8,128)(2,1)S(1)}, u32[]{:S(2)}, u32[]{:S(2)}) collective-permute-start(bf16[784,128]{1,0:T(8,128)(2,1)S(1)} %get-tuple-element.56), channel_id=1, source_target_pairs={{0,3},{1,2},{2,1},{3,0},{4,7},{5,6},{6,5},{7,4},{8,11},{9,10},{10,... | collective-permute-start | bytes 602120 | tf_op jit(solution)/shard_map/move_inner/ppermute | solution.py:257
  68.3 14.6 %collective-permute-start.16 = (bf16[784,128]{1,0:T(8,128)(2,1)S(1)}, bf16[784,128]{1,0:T(8,128)(2,1)S(1)}, u32[]{:S(2)}, u32[]{:S(2)}) collective-permute-start(bf16[784,128]{1,0:T(8,128)(2,1)S(1)} %get-tuple-element.42), channel_id=1, source_target_pairs={{0,1},{1,0},{2,3},{3,2},{4,5},{5,4},{6,7},{7,6},{8,9},{9,8},{10,11... | collective-permute-start | bytes 602120 | tf_op jit(solution)/shard_map/move_inner/ppermute | solution.py:257
  70.6 25.9 %collective-permute-start.17 = (bf16[784,128]{1,0:T(8,128)(2,1)S(1)}, bf16[784,128]{1,0:T(8,128)(2,1)S(1)}, u32[]{:S(2)}, u32[]{:S(2)}) collective-permute-start(bf16[784,128]{1,0:T(8,128)(2,1)S(1)} %get-tuple-element.43), channel_id=1, source_target_pairs={{0,2},{1,3},{2,0},{3,1},{4,6},{5,7},{6,4},{7,5},{8,10},{9,11},{10,... | collective-permute-start | bytes 602120 | tf_op jit(solution)/shard_map/move_inner/ppermute | solution.py:257
  71.3 25.2 %collective-permute-start.18 = (bf16[784,128]{1,0:T(8,128)(2,1)S(1)}, bf16[784,128]{1,0:T(8,128)(2,1)S(1)}, u32[]{:S(2)}, u32[]{:S(2)}) collective-permute-start(bf16[784,128]{1,0:T(8,128)(2,1)S(1)} %get-tuple-element.44), channel_id=1, source_target_pairs={{0,3},{1,2},{2,1},{3,0},{4,7},{5,6},{6,5},{7,4},{8,11},{9,10},{10,... | collective-permute-start | bytes 602120 | tf_op jit(solution)/shard_map/move_inner/ppermute | solution.py:257
  81.3 17.5 %collective-permute-start.42 = (bf16[784,128]{1,0:T(8,128)(2,1)S(1)}, bf16[784,128]{1,0:T(8,128)(2,1)S(1)}, u32[]{:S(2)}, u32[]{:S(2)}) collective-permute-start(bf16[784,128]{1,0:T(8,128)(2,1)S(1)} %sum_inner.3.refs_0_), channel_id=1, source_target_pairs={{0,8},{4,12},{8,0},{12,4},{16,24},{20,28},{24,16},{28,20},{1,9},{5... | collective-permute-start | bytes 602120 | tf_op jit(solution)/shard_map/gather_inner/ppermute | solution.py:251
  82.2 17.1 %collective-permute-start.43 = (bf16[784,128]{1,0:T(8,128)(2,1)S(1)}, bf16[784,128]{1,0:T(8,128)(2,1)S(1)}, u32[]{:S(2)}, u32[]{:S(2)}) collective-permute-start(bf16[784,128]{1,0:T(8,128)(2,1)S(1)} %sum_inner.3.refs_0_), channel_id=1, source_target_pairs={{0,16},{4,20},{8,24},{12,28},{16,0},{20,4},{24,8},{28,12},{1,17},{... | collective-permute-start | bytes 602120 | tf_op jit(solution)/shard_map/gather_inner/ppermute | solution.py:251
  82.9 18.2 %collective-permute-start.44 = (bf16[784,128]{1,0:T(8,128)(2,1)S(1)}, bf16[784,128]{1,0:T(8,128)(2,1)S(1)}, u32[]{:S(2)}, u32[]{:S(2)}) collective-permute-start(bf16[784,128]{1,0:T(8,128)(2,1)S(1)} %sum_inner.3.refs_0_), channel_id=1, source_target_pairs={{0,24},{4,28},{8,16},{12,20},{16,8},{20,12},{24,0},{28,4},{1,25},{... | collective-permute-start | bytes 602120 | tf_op jit(solution)/shard_map/gather_inner/ppermute | solution.py:251
  98.8 11.4 %collective-permute-start.20 = (bf16[784,128]{1,0:T(8,128)(2,1)S(1)}, bf16[784,128]{1,0:T(8,128)(2,1)S(1)}, u32[]{:S(2)}, u32[]{:S(2)}) collective-permute-start(bf16[784,128]{1,0:T(8,128)(2,1)S(1)} %sum_inner.2.refs_0_), channel_id=1, source_target_pairs={{0,16},{4,20},{8,24},{12,28},{16,0},{20,4},{24,8},{28,12},{1,17},{... | collective-permute-start | bytes 602120 | tf_op jit(solution)/shard_map/gather_inner/ppermute | solution.py:251
  99.2 11.0 %collective-permute-start.21 = (bf16[784,128]{1,0:T(8,128)(2,1)S(1)}, bf16[784,128]{1,0:T(8,128)(2,1)S(1)}, u32[]{:S(2)}, u32[]{:S(2)}) collective-permute-start(bf16[784,128]{1,0:T(8,128)(2,1)S(1)} %sum_inner.2.refs_0_), channel_id=1, source_target_pairs={{0,24},{4,28},{8,16},{12,20},{16,8},{20,12},{24,0},{28,4},{1,25},{... | collective-permute-start | bytes 602120 | tf_op jit(solution)/shard_map/gather_inner/ppermute | solution.py:251
  101.1 9.7 %collective-permute-start.46 = (bf16[784,128]{1,0:T(8,128)(2,1)S(1)}, bf16[784,128]{1,0:T(8,128)(2,1)S(1)}, u32[]{:S(2)}, u32[]{:S(2)}) collective-permute-start(bf16[784,128]{1,0:T(8,128)(2,1)S(1)} %collective-permute-done.42.refs_1_), channel_id=1, source_target_pairs={{0,4},{4,0},{8,12},{12,8},{16,20},{20,16},{24,28},{28,24},{1,5},{5... | collective-permute-start | bytes 602120 | tf_op jit(solution)/shard_map/gather_inner/ppermute | solution.py:254
  101.1 9.7 %collective-permute-start.47 = (bf16[784,128]{1,0:T(8,128)(2,1)S(1)}, bf16[784,128]{1,0:T(8,128)(2,1)S(1)}, u32[]{:S(2)}, u32[]{:S(2)}) collective-permute-start(bf16[784,128]{1,0:T(8,128)(2,1)S(1)} %collective-permute-done.43.refs_2_), channel_id=1, source_target_pairs={{0,4},{4,0},{8,12},{12,8},{16,20},{20,16},{24,28},{28,24},{1,5},{5... | collective-permute-start | bytes 602120 | tf_op jit(solution)/shard_map/gather_inner/ppermute | solution.py:254
  110.8 8.4 %collective-permute-start.24 = (bf16[784,128]{1,0:T(8,128)(2,1)S(1)}, bf16[784,128]{1,0:T(8,128)(2,1)S(1)}, u32[]{:S(2)}, u32[]{:S(2)}) collective-permute-start(bf16[784,128]{1,0:T(8,128)(2,1)S(1)} %collective-permute-done.20.refs_2_), channel_id=1, source_target_pairs={{0,4},{4,0},{8,12},{12,8},{16,20},{20,16},{24,28},{28,24},{1,5},{5... | collective-permute-start | bytes 602120 | tf_op jit(solution)/shard_map/gather_inner/ppermute | solution.py:254
  110.8 8.3 %collective-permute-start.25 = (bf16[784,128]{1,0:T(8,128)(2,1)S(1)}, bf16[784,128]{1,0:T(8,128)(2,1)S(1)}, u32[]{:S(2)}, u32[]{:S(2)}) collective-permute-start(bf16[784,128]{1,0:T(8,128)(2,1)S(1)} %collective-permute-done.21.refs_3_), channel_id=1, source_target_pairs={{0,4},{4,0},{8,12},{12,8},{16,20},{20,16},{24,28},{28,24},{1,5},{5... | collective-permute-start | bytes 602120 | tf_op jit(solution)/shard_map/gather_inner/ppermute | solution.py:254
  114.7 10.4 %collective-permute-start.49 = (bf16[272,128]{1,0:T(8,128)(2,1)S(1)}, bf16[272,128]{1,0:T(8,128)(2,1)S(1)}, u32[]{:S(2)}, u32[]{:S(2)}) collective-permute-start(bf16[272,128]{1,0:T(8,128)(2,1)S(1)} %get-tuple-element.58), channel_id=1, source_target_pairs={{0,1},{1,0},{2,3},{3,2},{4,5},{5,4},{6,7},{7,6},{8,9},{9,8},{10,11... | collective-permute-start | bytes 208904 | tf_op jit(solution)/shard_map/move_outer/ppermute | solution.py:257
  116.0 10.9 %collective-permute-start.50 = (bf16[272,128]{1,0:T(8,128)(2,1)S(1)}, bf16[272,128]{1,0:T(8,128)(2,1)S(1)}, u32[]{:S(2)}, u32[]{:S(2)}) collective-permute-start(bf16[272,128]{1,0:T(8,128)(2,1)S(1)} %get-tuple-element.59), channel_id=1, source_target_pairs={{0,2},{1,3},{2,0},{3,1},{4,6},{5,7},{6,4},{7,5},{8,10},{9,11},{10,... | collective-permute-start | bytes 208904 | tf_op jit(solution)/shard_map/move_outer/ppermute | solution.py:257
  117.2 9.7 %collective-permute-start.51 = (bf16[272,128]{1,0:T(8,128)(2,1)S(1)}, bf16[272,128]{1,0:T(8,128)(2,1)S(1)}, u32[]{:S(2)}, u32[]{:S(2)}) collective-permute-start(bf16[272,128]{1,0:T(8,128)(2,1)S(1)} %get-tuple-element.60), channel_id=1, source_target_pairs={{0,3},{1,2},{2,1},{3,0},{4,7},{5,6},{6,5},{7,4},{8,11},{9,10},{10,... | collective-permute-start | bytes 208904 | tf_op jit(solution)/shard_map/move_outer/ppermute | solution.py:257
  (21 other events, 189.3 us)

commit v2 on v0

--- a/solution.py
+++ b/solution.py
@@ -1,7 +1,18 @@
+import functools
+
 import jax
 import jax.numpy as jnp
 from jax import lax
+from jax.experimental import pallas as pl
+from jax.experimental.pallas import tpu as pltpu
 from jax.sharding import PartitionSpec as P
+
+LANES = 128
+HEAD = 16
+SPAN = 126.0
+CHUNKS = 2
+BF = jnp.bfloat16
+F32 = jnp.float32
 
 
 def half_nt(left, right):
@@ -23,7 +34,7 @@
     )
 
 
-def shards(pair_cc, screened, pair_vv):
+def gathered(pair_cc, screened, pair_vv):
     cc_whole = lax.all_gather(pair_cc, "col", axis=2, tiled=True)
     vv_whole = lax.all_gather(pair_vv, "row", axis=2, tiled=True)
     piece = lax.all_gather(screened, "col", axis=2, tiled=True)
@@ -36,8 +47,383 @@
     return jnp.stack([out_re, out_im])
 
 
+def bound_of(top):
+    top = jnp.max(top, axis=(0, 1), keepdims=True)
+    top = jnp.maximum(top, 1e-30) * (1.0 + 2.0**-7)
+    return top.astype(BF).astype(F32)
+
+
+def fold_top(values):
+    return jnp.max(jnp.abs(values).reshape(-1, 8, LANES), axis=0)
+
+
+def code(values, bound):
+    return jnp.exp2(values * (SPAN / bound)).astype(BF)
+
+
+def decode(coded, bound):
+    return jnp.log2(coded.astype(F32)) * (bound * (1.0 / SPAN))
+
+
+def head_of(ref):
+    return ref[0:1, :].astype(F32)
+
+
+def put_head(ref, bound):
+    ref[0:HEAD, :] = jnp.broadcast_to(bound, (HEAD, LANES)).astype(BF)
+
+
+def call(body, outs, scratch, name, args, flops=0):
+    nbytes = sum(a.size * a.dtype.itemsize for a in args) + sum(
+        functools.reduce(lambda p, q: p * q, o.shape) * o.dtype.itemsize for o in outs
+    )
+    specs = [pl.BlockSpec(memory_space=pltpu.SMEM)] + [
+        pl.BlockSpec(memory_space=pltpu.VMEM)
+    ] * (len(args) - 1)
+    return pl.pallas_call(
+        body,
+        out_shape=outs,
+        in_specs=specs,
+        out_specs=[pl.BlockSpec(memory_space=pltpu.VMEM)] * len(outs),
+        scratch_shapes=scratch,
+        compiler_params=pltpu.CompilerParams(vmem_limit_bytes=24 * 1024 * 1024),
+        cost_estimate=pl.CostEstimate(
+            flops=flops, bytes_accessed=nbytes, transcendentals=0
+        ),
+        name=name,
+    )(*args)
+
+
+def spread_body(parts, chunks, where_ref, mine_ref, twin_ref, *outs):
+    t, core = where_ref[0], where_ref[1]
+    half, width = twin_ref.shape[1] // 2, twin_ref.shape[2]
+    sub = half // parts
+    rows = sub // chunks
+    for i in range(parts):
+        at = pl.multiple_of(core * half + (t ^ i) * sub, 16)
+        for source in range(2):
+            lane = pl.multiple_of((core ^ source) * width, LANES)
+            ref = (mine_ref, twin_ref)[source]
+            both = [ref[p, pl.ds(at, sub), :] for p in range(2)]
+            both = [x.astype(F32).reshape(chunks, rows, width) for x in both]
+            both = jnp.stack(both, axis=1).reshape(2 * sub, width)
+            outs[i][:, pl.ds(lane, width)] = both.astype(BF)
+
+
+def route_body(parts, where_ref, *refs):
+    ins, outs = refs[:parts], refs[parts:]
+    m = where_ref[2]
+    for v in range(parts):
+
+        @pl.when(m == v)
+        def _(v=v):
+            for d in range(parts):
+                outs[d][...] = ins[v ^ d][...]
+
+
+def chunk_body(parts, chunks, where_ref, *refs):
+    ins, outs = refs[:parts], refs[parts:]
+    step = outs[0].shape[0] // parts
+    for e in range(chunks):
+        for d in range(parts):
+            outs[e][d * step : (d + 1) * step, :] = ins[d][e * step : (e + 1) * step, :]
+
+
+def inner_body(parts, rows, where_ref, w_own_ref, w_twin_ref, *refs):
+    ins, outs = refs[:parts], refs[parts : 2 * parts]
+    x_ref, t_ref = refs[2 * parts :]
+    group = ins[0].shape[0]
+    for i in range(parts):
+        x_ref[i * group : (i + 1) * group, :] = ins[i][...]
+    n_g = w_own_ref.shape[1]
+    tops = [jnp.zeros((8, LANES), F32) for _ in range(parts)]
+    tile = 256
+    for c, w_ref in enumerate((w_own_ref, w_twin_ref)):
+        for g in range(0, n_g, tile):
+            with_re = half_nt(x_ref[...], w_ref[0, g : g + tile, :])
+            with_im = half_nt(x_ref[...], w_ref[1, g : g + tile, :])
+            with_re = with_re.reshape(-1, 2, rows, tile)
+            with_im = with_im.reshape(-1, 2, rows, tile)
+            t_re = with_re[:, 0] - with_im[:, 1]
+            t_im = with_im[:, 0] + with_re[:, 1]
+            both = jnp.stack([t_re, t_im], axis=1).reshape(-1, tile)
+            for i in range(parts):
+                mine = both[i * group : (i + 1) * group]
+                for l in range(0, tile, LANES):
+                    block = mine[:, l : l + LANES]
+                    tops[i] = jnp.maximum(tops[i], fold_top(block))
+                    t_ref[i, (c * n_g + g + l) // LANES] = block
+    for i in range(parts):
+        bound = bound_of(tops[i])
+        put_head(outs[i], bound)
+        for l in range(2 * n_g // LANES):
+            at = HEAD + l * group
+            outs[i][at : at + group, :] = code(t_ref[i, l], bound)
+
+
+def sum_body(parts, where_ref, *refs):
+    ins, out = refs[:parts], refs[parts]
+    t_ref = refs[parts + 1]
+    n_l, group = t_ref.shape[0], t_ref.shape[1]
+    step = group // parts
+    top = jnp.zeros((8, LANES), F32)
+    bounds = [head_of(ins[d]) for d in range(parts)]
+    for l in range(n_l):
+        for s in range(parts):
+            total = None
+            for d in range(parts):
+                at = HEAD + l * group + (s ^ d) * step
+                term = decode(ins[d][at : at + step, :], bounds[d])
+                total = term if total is None else total + term
+            top = jnp.maximum(top, fold_top(total))
+            t_ref[l, s * step : (s + 1) * step, :] = total
+    bound = bound_of(top)
+    put_head(out, bound)
+    for l in range(n_l):
+        at = HEAD + l * group
+        out[at : at + group, :] = code(t_ref[l], bound)
+
+
+def outer_body(parts, rows, where_ref, a_own_ref, a_twin_ref, *refs):
+    ins, outs = refs[:parts], refs[parts : 2 * parts]
+    hi_ref, lo_ref = refs[2 * parts :]
+    core = where_ref[1]
+    n_l = hi_ref.shape[1] // LANES
+    group = (ins[0].shape[0] - HEAD) // n_l
+    for i in range(parts):
+        bound = head_of(ins[i])
+        for l in range(n_l):
+            at = HEAD + l * group
+            upper, lower = split_parts(decode(ins[i][at : at + group, :], bound))
+            c, rest = divmod(l, n_l // 2)
+            lane = pl.multiple_of(((core ^ c) * (n_l // 2) + rest) * LANES, LANES)
+            hi_ref[i * group : (i + 1) * group, pl.ds(lane, LANES)] = upper
+            lo_ref[i * group : (i + 1) * group, pl.ds(lane, LANES)] = lower
+    n_p = a_own_ref.shape[1]
+    tops = [jnp.zeros((8, LANES), F32) for _ in range(parts)]
+    blocks = [[] for _ in range(parts)]
+    for a_ref in (a_own_ref, a_twin_ref):
+        with_re = half_nt(hi_ref[...], a_ref[0]) + half_nt(lo_ref[...], a_ref[0])
+        with_im = half_nt(hi_ref[...], a_ref[1]) + half_nt(lo_ref[...], a_ref[1])
+        with_re = with_re.reshape(parts, parts, 2, rows, n_p)
+        with_im = with_im.reshape(parts, parts, 2, rows, n_p)
+        k_re = with_re[:, :, 0] + with_im[:, :, 1]
+        k_im = with_re[:, :, 1] - with_im[:, :, 0]
+        for d in range(parts):
+            both = jnp.stack([k_re[:, d], k_im[:, d]], axis=1).reshape(-1, n_p)
+            for l in range(0, n_p, LANES):
+                block = both[:, l : l + LANES]
+                if d:
+                    tops[d] = jnp.maximum(tops[d], fold_top(block))
+                blocks[d].append(block)
+    for d in range(parts):
+        n_r = blocks[d][0].shape[0]
+        if d == 0:
+            for l, block in enumerate(blocks[0]):
+                outs[0][l * n_r : (l + 1) * n_r, :] = block
+            continue
+        bound = bound_of(tops[d])
+        put_head(outs[d], bound)
+        for l, block in enumerate(blocks[d]):
+            at = HEAD + l * n_r
+            outs[d][at : at + n_r, :] = code(block, bound)
+
+
+def last_body(parts, chunks, rows, where_ref, *refs):
+    ins, outs = refs[: parts * chunks], refs[parts * chunks :]
+    t = where_ref[0]
+    sub = rows * chunks
+    n_l = outs[0].shape[2] // LANES
+    for e in range(chunks):
+        mine = ins[e * parts]
+        n_r = mine.shape[0] // (2 * n_l)
+        bounds = [None] + [head_of(ins[e * parts + d]) for d in range(1, parts)]
+        for l in range(2 * n_l):
+            total = mine[l * n_r : (l + 1) * n_r, :]
+            for d in range(1, parts):
+                at = HEAD + l * n_r
+                total = total + decode(ins[e * parts + d][at : at + n_r, :], bounds[d])
+            total = total.reshape(parts, 2, rows, LANES)
+            out, lane = outs[l // n_l], l % n_l * LANES
+            for i in range(parts):
+                at = pl.multiple_of((t ^ i) * sub + e * rows, 8)
+                for part in range(2):
+                    out[part, pl.ds(at, rows), lane : lane + LANES] = total[i, part]
+
+
+def turn_body(where_ref, own_ref, twin_ref, out_ref, k_ref):
+    core = where_ref[1]
+    half = own_ref.shape[1]
+    for c, ref in enumerate((own_ref, twin_ref)):
+        at = pl.multiple_of((core ^ c) * half, 8)
+        k_ref[:, pl.ds(at, half), :] = ref[...]
+    for part in range(2):
+        out_ref[part] = k_ref[part].T
+
+
+def after(values, *earlier):
+    return lax.optimization_barrier((tuple(values), earlier))[0]
+
+
+def stationary(n_row, n_col, pair_cc, screened, pair_vv):
+    parts, chunks = n_col, CHUNKS
+    n_q, width = pair_vv.shape[1:]
+    n_p, n_k = pair_cc.shape[1:]
+    n_g = screened.shape[1]
+    half = n_q // 2
+    sub = half // parts
+    rows = sub // chunks
+    group = parts * 2 * rows
+    r, z = lax.axis_index("row"), lax.axis_index("col")
+    t, core = r // 2, r % 2
+    where = jnp.stack([t, core, t ^ z]).astype(jnp.int32)
+    shape = jax.ShapeDtypeStruct
+    total_g = 2 * n_g
+
+    def plane(x, i):
+        pairs = [(a, a ^ (2 * i)) for a in range(n_row)]
+        return lax.ppermute(x, "row", pairs)
+
+    def twin(x):
+        return lax.ppermute(x, "row", [(a, a ^ 1) for a in range(n_row)])
+
+    def along(x, d):
+        return lax.ppermute(x, "col", [(a, a ^ d) for a in range(parts)])
+
+    def planes(arrays):
+        return [arrays[0]] + [plane(arrays[i], i) for i in range(1, parts)]
+
+    def alongs(arrays):
+        return [arrays[0]] + [along(arrays[d], d) for d in range(1, parts)]
+
+    def route(arrays, name):
+        outs = [shape(a.shape, a.dtype) for a in arrays]
+        return call(
+            functools.partial(route_body, parts), outs, [], name, [where, *arrays]
+        )
+
+    with jax.named_scope("spread_vv"):
+        theirs = twin(pair_vv)
+        cut = call(
+            functools.partial(spread_body, parts, chunks),
+            [shape((2 * sub, 2 * width), BF)] * parts,
+            [],
+            "spread_vv",
+            [where, pair_vv, theirs],
+        )
+        late = after([screened, pair_cc], *cut)
+        screened_twin, pair_cc_twin = twin(late[0]), twin(late[1])
+        cut = alongs(route(planes(cut), "route_vv"))
+        cut = after(cut, screened_twin, pair_cc_twin)
+        own = call(
+            functools.partial(chunk_body, parts, chunks),
+            [shape((group, 2 * width), BF)] * chunks,
+            [],
+            "chunk_vv",
+            [where, *cut],
+        )
+    coded = shape((HEAD + total_g // LANES * group, LANES), BF)
+    term = shape((HEAD + 2 * n_p // LANES * group, LANES), BF)
+
+    def inner_of(groups):
+        return call(
+            functools.partial(inner_body, parts, rows),
+            [coded] * parts,
+            [
+                pltpu.VMEM((parts * group, 2 * width), BF),
+                pltpu.VMEM((parts, total_g // LANES, group, LANES), F32),
+            ],
+            "inner",
+            [where, screened, screened_twin, *groups],
+            flops=2 * parts * group * 2 * width * 2 * total_g,
+        )
+
+    def sum_of(arrays):
+        (total,) = call(
+            functools.partial(sum_body, parts),
+            [coded],
+            [pltpu.VMEM((total_g // LANES, group, LANES), F32)],
+            "sum_inner",
+            [where, *arrays],
+        )
+        return total
+
+    def outer_of(arrays):
+        return call(
+            functools.partial(outer_body, parts, rows),
+            [shape((2 * n_p // LANES * group, LANES), F32)] + [term] * (parts - 1),
+            [pltpu.VMEM((parts * group, n_k), BF)] * 2,
+            "outer",
+            [where, pair_cc, pair_cc_twin, *arrays],
+            flops=4 * parts * group * n_k * 4 * n_p,
+        )
+
+    with jax.named_scope("inner"):
+        groups = [planes([own[e]] * parts) for e in range(chunks)]
+        inner, routed = [], []
+        for e in range(chunks):
+            got = groups[e] if e == 0 else after(groups[e], *inner[e - 1])
+            inner.append(inner_of(got))
+    with jax.named_scope("move_inner"):
+        for e in range(chunks):
+            spread = planes(inner[e])
+            if e + 1 < chunks:
+                spread = after(spread, *inner[e + 1])
+            routed.append(route(spread, "route_inner"))
+        moved = [alongs(x) for x in routed]
+    finals, outer = [], None
+    with jax.named_scope("outer"):
+        for e in range(chunks):
+            got = moved[e] if e == 0 else after(moved[e], *outer)
+            total = sum_of(got)
+            outer = outer_of(planes([total] * parts))
+            finals += alongs(outer)
+    with jax.named_scope("sum_outer"):
+        own, theirs = call(
+            functools.partial(last_body, parts, chunks, rows),
+            [shape((2, half, n_p), F32)] * 2,
+            [],
+            "sum_outer",
+            [where, *finals],
+        )
+        (result,) = call(
+            turn_body,
+            [shape((2, n_p, n_q), F32)],
+            [pltpu.VMEM((2, n_q, n_p), F32)],
+            "turn",
+            [where, own, twin(theirs)],
+        )
+    return result
+
+
+def power_of_two(n):
+    return n > 0 and n & (n - 1) == 0
+
+
 def solution(mesh):
     placed = (P(None, "row", "col"), P(None, "row", "col"), P(None, "col", "row"))
+    n_row, n_col = mesh.shape["row"], mesh.shape["col"]
+
+    def shards(pair_cc, screened, pair_vv):
+        n_q, width = pair_vv.shape[1:]
+        n_p, n_k = pair_cc.shape[1:]
+        n_g = screened.shape[1]
+        fits = (
+            power_of_two(n_row)
+            and power_of_two(n_col)
+            and n_row == 2 * n_col
+            and n_q % (2 * n_col * CHUNKS * 8) == 0
+            and n_q % (2 * n_col * 16) == 0
+            and width % LANES == 0
+            and n_g == width
+            and n_g % 256 == 0
+            and n_p % LANES == 0
+            and n_k == 2 * width
+        )
+        if not fits:
+            return gathered(pair_cc, screened, pair_vv)
+        return stationary(n_row, n_col, pair_cc, screened, pair_vv)
+
     return jax.shard_map(
         shards, mesh=mesh, in_specs=placed, out_specs=P(None, "row", "col"), check_vma=False
     )

time: 570 us -> 124 us (0.22)
  waiting for transfers between devices: 520 us -> 44.2 us
  starting transfers between devices: 0.3 us -> 56.2 us
  matrix products: 30.8 us -> 0 us
  Pallas kernels: 0 us -> 20 us
  between operations: 13.3 us -> 0.16 us
    all_gather x4 -> x0, waiting for transfers between devices: 518 us -> none  [the longest x1 324 us: shards(): piece = lax.all_gather(screened, 'col', axis=2, tiled=True)]
    ppermute x0 -> x40, starting transfers between devices: none -> 56.2 us  [the longest x15 28.1 us: along(): return lax.ppermute(x, 'col', [(a, a ^ d) for a in range(parts)])]
    ppermute x0 -> x40, waiting for transfers between devices: none -> 44.2 us  [the longest x15 28.5 us: along(): return lax.ppermute(x, 'col', [(a, a ^ d) for a in range(parts)])]
    dot_general x12 -> x0, matrix products: 30.8 us -> none  [the longest x4 17.3 us: half_nt(): lax.dot_general(left, right, (((1,), (1,)), ((), ())), preferred_element_...]
    pallas_call x0 -> x13, Pallas kernels: none -> 20 us  [call(): pl.pallas_call(body, out_shape=outs, in_specs=specs, out_specs=[pl.BlockS...]
  transfers between devices with their start and end apart: 4 -> 40, of which waited for: 4 -> 16; matrix products, arithmetic and copies ran while one was open for 1% -> 0% of each run, Pallas kernels for 0% -> 12%
where the time goes in v2:
time: 124 us
  starting transfers between devices  56.2 us (45%)
  waiting for transfers between devices  44.2 us (36%)
  Pallas kernels  20 us (16%)
  local copies, waits for them, and re-layouts  3.34 us (3%)
    ppermute x15, waiting for transfers between devices, along(): return lax.ppermute(x, 'col', [(a, a ^ d) for a in range(parts)])  28.5 us
    ppermute x15, starting transfers between devices, along(): return lax.ppermute(x, 'col', [(a, a ^ d) for a in range(parts)])  28.1 us
    ppermute x21, starting transfers between devices, plane(): return lax.ppermute(x, 'row', pairs)  27 us
    pallas_call x13, Pallas kernels, call(): pl.pallas_call(body, out_shape=outs, in_specs=specs, out_specs=[pl.BlockS...  20 us
    ppermute x21, waiting for transfers between devices, plane(): return lax.ppermute(x, 'row', pairs)  12.8 us
    unnamed x6, local copies, waits for them, and re-layouts  3.34 us
    ppermute x4, waiting for transfers between devices, twin(): return lax.ppermute(x, 'row', [(a, a ^ 1) for a in range(n_row)])  2.82 us
  transfers between devices with their start and end apart: 40, of which 16 were waited for; matrix products, arithmetic and copies ran while one was open for 0% of the time, Pallas kernels for 12%

profile of v2, /device:TPU:0, one launch (start us, length us, event | category | flops | bytes accessed | tf_op | source)
XLA Modules:
  0.0 123.9 jit_solution(13925940368658099381)
XLA Ops:
  4.2 2.9 %collective-permute-start.3 = (bf16[32,1536]{1,0:T(8,128)(2,1)S(1)}, bf16[32,1536]{1,0:T(8,128)(2,1)S(1)}, u32[]{:S(2)}, u32[]{:S(2)}) collective-permute-start(bf16[32,1536]{1,0:T(8,128)(2,1)S(1)} %get-tuple-element.60), channel_id=1, source_target_pairs={{0,8},{4,12},{8,0},{12,4},{16,24},{20,28},{24,16},{28,20},{1,9},{5... | collective-permute-start | bytes 294920 | tf_op jit(solution)/shard_map/spread_vv/ppermute | solution.py:285
  8.6 1.6 %collective-permute-done.3.refs_1_ = bf16[32,1536]{1,0:T(8,128)(2,1)S(1)} collective-permute-done((bf16[32,1536]{1,0:T(8,128)(2,1)S(1)}, bf16[32,1536]{1,0:T(8,128)(2,1)S(1)}, u32[]{:S(2)}, u32[]{:S(2)}) %collective-permute-start.3) | collective-permute-done | bytes 98336 | tf_op jit(solution)/shard_map/spread_vv/ppermute | solution.py:285
  10.2 2.6 %collective-permute-done.4.refs_2_ = bf16[32,1536]{1,0:T(8,128)(2,1)S(1)} collective-permute-done((bf16[32,1536]{1,0:T(8,128)(2,1)S(1)}, bf16[32,1536]{1,0:T(8,128)(2,1)S(1)}, u32[]{:S(2)}, u32[]{:S(2)}) %collective-permute-start.4) | collective-permute-done | bytes 98336 | tf_op jit(solution)/shard_map/spread_vv/ppermute | solution.py:285
  14.7 1.6 %collective-permute-start.6 = (bf16[32,1536]{1,0:T(8,128)(2,1)S(1)}, bf16[32,1536]{1,0:T(8,128)(2,1)S(1)}, u32[]{:S(2)}, u32[]{:S(2)}) collective-permute-start(bf16[32,1536]{1,0:T(8,128)(2,1)S(1)} %get-tuple-element.66), channel_id=1, source_target_pairs={{0,1},{1,0},{2,3},{3,2},{4,5},{5,4},{6,7},{7,6},{8,9},{9,8},{10,11... | collective-permute-start | bytes 294920 | tf_op jit(solution)/shard_map/spread_vv/ppermute | solution.py:291
  16.3 2.6 %collective-permute-start.7 = (bf16[32,1536]{1,0:T(8,128)(2,1)S(1)}, bf16[32,1536]{1,0:T(8,128)(2,1)S(1)}, u32[]{:S(2)}, u32[]{:S(2)}) collective-permute-start(bf16[32,1536]{1,0:T(8,128)(2,1)S(1)} %get-tuple-element.67), channel_id=1, source_target_pairs={{0,2},{1,3},{2,0},{3,1},{4,6},{5,7},{6,4},{7,5},{8,10},{9,11},{10,... | collective-permute-start | bytes 294920 | tf_op jit(solution)/shard_map/spread_vv/ppermute | solution.py:291
  20.0 4.3 %collective-permute-done.7.refs_2_ = bf16[32,1536]{1,0:T(8,128)(2,1)S(1)} collective-permute-done((bf16[32,1536]{1,0:T(8,128)(2,1)S(1)}, bf16[32,1536]{1,0:T(8,128)(2,1)S(1)}, u32[]{:S(2)}, u32[]{:S(2)}) %collective-permute-start.7) | collective-permute-done | bytes 98336 | tf_op jit(solution)/shard_map/spread_vv/ppermute | solution.py:291
  26.0 1.7 %collective-permute-start.11 = (bf16[64,1536]{1,0:T(8,128)(2,1)S(1)}, bf16[64,1536]{1,0:T(8,128)(2,1)S(1)}, u32[]{:S(2)}, u32[]{:S(2)}) collective-permute-start(bf16[64,1536]{1,0:T(8,128)(2,1)S(1)} %get-tuple-element.73.refs_0_), channel_id=1, source_target_pairs={{0,24},{4,28},{8,16},{12,20},{16,8},{20,12},{24,0},{28,4},{1,25},{... | collective-permute-start | bytes 589832 | tf_op jit(solution)/shard_map/inner/ppermute | solution.py:285
  29.5 1.6 %collective-permute-start.17 = (bf16[64,1536]{1,0:T(8,128)(2,1)S(1)}, bf16[64,1536]{1,0:T(8,128)(2,1)S(1)}, u32[]{:S(2)}, u32[]{:S(2)}) collective-permute-start(bf16[64,1536]{1,0:T(8,128)(2,1)S(1)} %get-tuple-element.79.refs_0_), channel_id=1, source_target_pairs={{0,24},{4,28},{8,16},{12,20},{16,8},{20,12},{24,0},{28,4},{1,25},{... | collective-permute-start | bytes 589832 | tf_op jit(solution)/shard_map/inner/ppermute | solution.py:285
  32.7 2.2 %collective-permute-done.11.refs_3_ = bf16[64,1536]{1,0:T(8,128)(2,1)S(1)} collective-permute-done((bf16[64,1536]{1,0:T(8,128)(2,1)S(1)}, bf16[64,1536]{1,0:T(8,128)(2,1)S(1)}, u32[]{:S(2)}, u32[]{:S(2)}) %collective-permute-start.11) | collective-permute-done | bytes 196640 | tf_op jit(solution)/shard_map/inner/ppermute | solution.py:285
  34.9 1.7 %collective-permute-start.15 = (bf16[64,1536]{1,0:T(8,128)(2,1)S(1)}, bf16[64,1536]{1,0:T(8,128)(2,1)S(1)}, u32[]{:S(2)}, u32[]{:S(2)}) collective-permute-start(bf16[64,1536]{1,0:T(8,128)(2,1)S(1)} %get-tuple-element.79.refs_0_), channel_id=1, source_target_pairs={{0,8},{4,12},{8,0},{12,4},{16,24},{20,28},{24,16},{28,20},{1,9},{5... | collective-permute-start | bytes 589832 | tf_op jit(solution)/shard_map/inner/ppermute | solution.py:285
  36.6 3.2 %collective-permute-done.10.refs_2_ = bf16[64,1536]{1,0:T(8,128)(2,1)S(1)} collective-permute-done((bf16[64,1536]{1,0:T(8,128)(2,1)S(1)}, bf16[64,1536]{1,0:T(8,128)(2,1)S(1)}, u32[]{:S(2)}, u32[]{:S(2)}) %collective-permute-start.10) | collective-permute-done | bytes 196640 | tf_op jit(solution)/shard_map/inner/ppermute | solution.py:285
  39.7 2.3 %copy-done = bf16[2,768,1536]{2,1,0:T(8,128)(2,1)S(1)} copy-done((bf16[2,768,1536]{2,1,0:T(8,128)(2,1)S(1)}, bf16[2,768,1536]{2,1,0:T(8,128)(2,1)}, u32[]{:S(2)}) %copy-start) | copy-done | bytes 4718616
  42.1 3.5 %inner.2 = (bf16[784,128]{1,0:T(8,128)(2,1)S(1)}, bf16[784,128]{1,0:T(8,128)(2,1)S(1)}, bf16[784,128]{1,0:T(8,128)(2,1)S(1)}, bf16[784,128]{1,0:T(8,128)(2,1)S(1)}) custom-call(s32[3]{0:T(128)S(1)} %pad_add_fusion.where_ref, bf16[2,768,1536]{2,1,0:T(8,128)(2,1)S(1)} %copy-done, bf16[2,768,1536]{2,1,0:T(8,128)(2,1)S(1)} %collective-permute-done.2.w_twin_ref, ...), custom_call_target="tpu_custom_call" | custom-call | flops 2415919104 | bytes 11026444 | tf_op jit(solution)/shard_map/inner/inner/pallas_call | solution.py:83
  47.5 1.6 %collective-permute-start.14 = (bf16[784,128]{1,0:T(8,128)(2,1)S(1)}, bf16[784,128]{1,0:T(8,128)(2,1)S(1)}, u32[]{:S(2)}, u32[]{:S(2)}) collective-permute-start(bf16[784,128]{1,0:T(8,128)(2,1)S(1)} %get-tuple-element.77), channel_id=1, source_target_pairs={{0,24},{4,28},{8,16},{12,20},{16,8},{20,12},{24,0},{28,4},{1,25},{... | collective-permute-start | bytes 602120 | tf_op jit(solution)/shard_map/move_inner/ppermute | solution.py:285
  49.2 3.5 %inner.3 = (bf16[784,128]{1,0:T(8,128)(2,1)S(1)}, bf16[784,128]{1,0:T(8,128)(2,1)S(1)}, bf16[784,128]{1,0:T(8,128)(2,1)S(1)}, bf16[784,128]{1,0:T(8,128)(2,1)S(1)}) custom-call(s32[3]{0:T(128)S(1)} %pad_add_fusion.where_ref, bf16[2,768,1536]{2,1,0:T(8,128)(2,1)S(1)} %copy-done, bf16[2,768,1536]{2,1,0:T(8,128)(2,1)S(1)} %collective-permute-done.2.w_twin_ref, ...), custom_call_target="tpu_custom_call" | custom-call | flops 2415919104 | bytes 11026444 | tf_op jit(solution)/shard_map/inner/inner/pallas_call | solution.py:83
  52.7 1.9 %collective-permute-done.13.refs_2_ = bf16[784,128]{1,0:T(8,128)(2,1)S(1)} collective-permute-done((bf16[784,128]{1,0:T(8,128)(2,1)S(1)}, bf16[784,128]{1,0:T(8,128)(2,1)S(1)}, u32[]{:S(2)}, u32[]{:S(2)}) %collective-permute-start.13) | collective-permute-done | bytes 200736 | tf_op jit(solution)/shard_map/move_inner/ppermute | solution.py:285
  57.9 1.7 %collective-permute-start.20 = (bf16[784,128]{1,0:T(8,128)(2,1)S(1)}, bf16[784,128]{1,0:T(8,128)(2,1)S(1)}, u32[]{:S(2)}, u32[]{:S(2)}) collective-permute-start(bf16[784,128]{1,0:T(8,128)(2,1)S(1)} %get-tuple-element.94), channel_id=1, source_target_pairs={{0,3},{1,2},{2,1},{3,0},{4,7},{5,6},{6,5},{7,4},{8,11},{9,10},{10,... | collective-permute-start | bytes 602120 | tf_op jit(solution)/shard_map/move_inner/ppermute | solution.py:291
  61.9 2.5 %collective-permute-done.18.refs_1_ = bf16[784,128]{1,0:T(8,128)(2,1)S(1)} collective-permute-done((bf16[784,128]{1,0:T(8,128)(2,1)S(1)}, bf16[784,128]{1,0:T(8,128)(2,1)S(1)}, u32[]{:S(2)}, u32[]{:S(2)}) %collective-permute-start.18) | collective-permute-done | bytes 200736 | tf_op jit(solution)/shard_map/move_inner/ppermute | solution.py:291
  65.7 4.6 %collective-permute-done.19.refs_2_ = bf16[784,128]{1,0:T(8,128)(2,1)S(1)} collective-permute-done((bf16[784,128]{1,0:T(8,128)(2,1)S(1)}, bf16[784,128]{1,0:T(8,128)(2,1)S(1)}, u32[]{:S(2)}, u32[]{:S(2)}) %collective-permute-start.19) | collective-permute-done | bytes 200736 | tf_op jit(solution)/shard_map/move_inner/ppermute | solution.py:291
  72.3 2.2 %collective-permute-start.22 = (bf16[784,128]{1,0:T(8,128)(2,1)S(1)}, bf16[784,128]{1,0:T(8,128)(2,1)S(1)}, u32[]{:S(2)}, u32[]{:S(2)}) collective-permute-start(bf16[784,128]{1,0:T(8,128)(2,1)S(1)} %sum_inner.2.refs_0_), channel_id=1, source_target_pairs={{0,16},{4,20},{8,24},{12,28},{16,0},{20,4},{24,8},{28,12},{1,17},{... | collective-permute-start | bytes 602120 | tf_op jit(solution)/shard_map/outer/ppermute | solution.py:285
  75.6 2.9 %collective-permute-start.30 = (bf16[784,128]{1,0:T(8,128)(2,1)S(1)}, bf16[784,128]{1,0:T(8,128)(2,1)S(1)}, u32[]{:S(2)}, u32[]{:S(2)}) collective-permute-start(bf16[784,128]{1,0:T(8,128)(2,1)S(1)} %get-tuple-element.100), channel_id=1, source_target_pairs={{0,1},{1,0},{2,3},{3,2},{4,5},{5,4},{6,7},{7,6},{8,9},{9,8},{10,11... | collective-permute-start | bytes 602120 | tf_op jit(solution)/shard_map/move_inner/ppermute | solution.py:291
  80.9 3.0 %outer.2 = (f32[256,128]{1,0:T(8,128)S(1)}, bf16[272,128]{1,0:T(8,128)(2,1)S(1)}, bf16[272,128]{1,0:T(8,128)(2,1)S(1)}, bf16[272,128]{1,0:T(8,128)(2,1)S(1)}) custom-call(s32[3]{0:T(128)S(1)} %pad_add_fusion.where_ref, bf16[2,256,1536]{2,1,0:T(8,128)(2,1)S(1)} %copy-done.2, bf16[2,256,1536]{2,1,0:T(8,128)(2,1)S(1)} %collective-permute-done.1.a_twin_ref, ...), custom_call_target="tpu_custom_call" | custom-call | flops 1610612736 | bytes 4288524 | tf_op jit(solution)/shard_map/outer/outer/pallas_call | solution.py:83
  83.9 10.0 %collective-permute-done.31.refs_2_ = bf16[784,128]{1,0:T(8,128)(2,1)S(1)} collective-permute-done((bf16[784,128]{1,0:T(8,128)(2,1)S(1)}, bf16[784,128]{1,0:T(8,128)(2,1)S(1)}, u32[]{:S(2)}, u32[]{:S(2)}) %collective-permute-start.31) | collective-permute-done | bytes 200736 | tf_op jit(solution)/shard_map/move_inner/ppermute | solution.py:291
  96.4 1.7 %collective-permute-start.34 = (bf16[784,128]{1,0:T(8,128)(2,1)S(1)}, bf16[784,128]{1,0:T(8,128)(2,1)S(1)}, u32[]{:S(2)}, u32[]{:S(2)}) collective-permute-start(bf16[784,128]{1,0:T(8,128)(2,1)S(1)} %sum_inner.3.refs_0_), channel_id=1, source_target_pairs={{0,16},{4,20},{8,24},{12,28},{16,0},{20,4},{24,8},{28,12},{1,17},{... | collective-permute-start | bytes 602120 | tf_op jit(solution)/shard_map/outer/ppermute | solution.py:285
  98.4 2.7 %collective-permute-start.24 = (bf16[272,128]{1,0:T(8,128)(2,1)S(1)}, bf16[272,128]{1,0:T(8,128)(2,1)S(1)}, u32[]{:S(2)}, u32[]{:S(2)}) collective-permute-start(bf16[272,128]{1,0:T(8,128)(2,1)S(1)} %get-tuple-element.96), channel_id=1, source_target_pairs={{0,1},{1,0},{2,3},{3,2},{4,5},{5,4},{6,7},{7,6},{8,9},{9,8},{10,11... | collective-permute-start | bytes 208904 | tf_op jit(solution)/shard_map/outer/ppermute | solution.py:291
  101.2 1.8 %collective-permute-start.25 = (bf16[272,128]{1,0:T(8,128)(2,1)S(1)}, bf16[272,128]{1,0:T(8,128)(2,1)S(1)}, u32[]{:S(2)}, u32[]{:S(2)}) collective-permute-start(bf16[272,128]{1,0:T(8,128)(2,1)S(1)} %get-tuple-element.97), channel_id=1, source_target_pairs={{0,2},{1,3},{2,0},{3,1},{4,6},{5,7},{6,4},{7,5},{8,10},{9,11},{10,... | collective-permute-start | bytes 208904 | tf_op jit(solution)/shard_map/outer/ppermute | solution.py:291
  103.0 2.4 %collective-permute-start.26 = (bf16[272,128]{1,0:T(8,128)(2,1)S(1)}, bf16[272,128]{1,0:T(8,128)(2,1)S(1)}, u32[]{:S(2)}, u32[]{:S(2)}) collective-permute-start(bf16[272,128]{1,0:T(8,128)(2,1)S(1)} %get-tuple-element.98), channel_id=1, source_target_pairs={{0,3},{1,2},{2,1},{3,0},{4,7},{5,6},{6,5},{7,4},{8,11},{9,10},{10,... | collective-permute-start | bytes 208904 | tf_op jit(solution)/shard_map/outer/ppermute | solution.py:291
  105.4 3.0 %outer.3 = (f32[256,128]{1,0:T(8,128)S(1)}, bf16[272,128]{1,0:T(8,128)(2,1)S(1)}, bf16[272,128]{1,0:T(8,128)(2,1)S(1)}, bf16[272,128]{1,0:T(8,128)(2,1)S(1)}) custom-call(s32[3]{0:T(128)S(1)} %pad_add_fusion.where_ref, bf16[2,256,1536]{2,1,0:T(8,128)(2,1)S(1)} %copy-done.2, bf16[2,256,1536]{2,1,0:T(8,128)(2,1)S(1)} %collective-permute-done.1.a_twin_ref, ...), custom_call_target="tpu_custom_call" | custom-call | flops 1610612736 | bytes 4288524 | tf_op jit(solution)/shard_map/outer/outer/pallas_call | solution.py:83
  108.4 3.6 %collective-permute-start.36 = (bf16[272,128]{1,0:T(8,128)(2,1)S(1)}, bf16[272,128]{1,0:T(8,128)(2,1)S(1)}, u32[]{:S(2)}, u32[]{:S(2)}) collective-permute-start(bf16[272,128]{1,0:T(8,128)(2,1)S(1)} %get-tuple-element.108), channel_id=1, source_target_pairs={{0,1},{1,0},{2,3},{3,2},{4,5},{5,4},{6,7},{7,6},{8,9},{9,8},{10,11... | collective-permute-start | bytes 208904 | tf_op jit(solution)/shard_map/outer/ppermute | solution.py:291
  112.0 2.0 %collective-permute-start.37 = (bf16[272,128]{1,0:T(8,128)(2,1)S(1)}, bf16[272,128]{1,0:T(8,128)(2,1)S(1)}, u32[]{:S(2)}, u32[]{:S(2)}) collective-permute-start(bf16[272,128]{1,0:T(8,128)(2,1)S(1)} %get-tuple-element.109), channel_id=1, source_target_pairs={{0,2},{1,3},{2,0},{3,1},{4,6},{5,7},{6,4},{7,5},{8,10},{9,11},{10,... | collective-permute-start | bytes 208904 | tf_op jit(solution)/shard_map/outer/ppermute | solution.py:291
  115.4 2.8 %collective-permute-done.37.refs_6_ = bf16[272,128]{1,0:T(8,128)(2,1)S(1)} collective-permute-done((bf16[272,128]{1,0:T(8,128)(2,1)S(1)}, bf16[272,128]{1,0:T(8,128)(2,1)S(1)}, u32[]{:S(2)}, u32[]{:S(2)}) %collective-permute-start.37) | collective-permute-done | bytes 69664 | tf_op jit(solution)/shard_map/outer/ppermute | solution.py:291
  118.2 2.3 %collective-permute-done.38.refs_7_ = bf16[272,128]{1,0:T(8,128)(2,1)S(1)} collective-permute-done((bf16[272,128]{1,0:T(8,128)(2,1)S(1)}, bf16[272,128]{1,0:T(8,128)(2,1)S(1)}, u32[]{:S(2)}, u32[]{:S(2)}) %collective-permute-start.38) | collective-permute-done | bytes 69664 | tf_op jit(solution)/shard_map/outer/ppermute | solution.py:291
  (68 shorter events, 35.8 us)
Async XLA Ops:
  3.6 21.8 %collective-permute-start.2 = (bf16[2,768,1536]{2,1,0:T(8,128)(2,1)}, bf16[2,768,1536]{2,1,0:T(8,128)(2,1)S(1)}, u32[]{:S(2)}, u32[]{:S(2)}) collective-permute-start(bf16[2,768,1536]{2,1,0:T(8,128)(2,1)} %w_own_ref.3), channel_id=1, source_target_pairs={{0,4},{4,0},{8,12},{12,8},{16,20},{20,16},{24,28},{28,24},{1,5},{5... | collective-permute-start | bytes 14155784 | tf_op jit(solution)/shard_map/spread_vv/ppermute | solution.py:288
  4.0 21.4 %collective-permute-start.1 = (bf16[2,256,1536]{2,1,0:T(8,128)(2,1)}, bf16[2,256,1536]{2,1,0:T(8,128)(2,1)S(1)}, u32[]{:S(2)}, u32[]{:S(2)}) collective-permute-start(bf16[2,256,1536]{2,1,0:T(8,128)(2,1)} %a_own_ref.3), channel_id=1, source_target_pairs={{0,4},{4,0},{8,12},{12,8},{16,20},{20,16},{24,28},{28,24},{1,5},{5... | collective-permute-start | bytes 4718600 | tf_op jit(solution)/shard_map/spread_vv/ppermute | solution.py:288
  16.3 8.0 %collective-permute-start.7 = (bf16[32,1536]{1,0:T(8,128)(2,1)S(1)}, bf16[32,1536]{1,0:T(8,128)(2,1)S(1)}, u32[]{:S(2)}, u32[]{:S(2)}) collective-permute-start(bf16[32,1536]{1,0:T(8,128)(2,1)S(1)} %get-tuple-element.67), channel_id=1, source_target_pairs={{0,2},{1,3},{2,0},{3,1},{4,6},{5,7},{6,4},{7,5},{8,10},{9,11},{10,... | collective-permute-start | bytes 294920 | tf_op jit(solution)/shard_map/spread_vv/ppermute | solution.py:291
  18.9 6.5 %collective-permute-start.8 = (bf16[32,1536]{1,0:T(8,128)(2,1)S(1)}, bf16[32,1536]{1,0:T(8,128)(2,1)S(1)}, u32[]{:S(2)}, u32[]{:S(2)}) collective-permute-start(bf16[32,1536]{1,0:T(8,128)(2,1)S(1)} %get-tuple-element.68), channel_id=1, source_target_pairs={{0,3},{1,2},{2,1},{3,0},{4,7},{5,6},{6,5},{7,4},{8,11},{9,10},{10,... | collective-permute-start | bytes 294920 | tf_op jit(solution)/shard_map/spread_vv/ppermute | solution.py:291
  26.0 8.9 %collective-permute-start.11 = (bf16[64,1536]{1,0:T(8,128)(2,1)S(1)}, bf16[64,1536]{1,0:T(8,128)(2,1)S(1)}, u32[]{:S(2)}, u32[]{:S(2)}) collective-permute-start(bf16[64,1536]{1,0:T(8,128)(2,1)S(1)} %get-tuple-element.73.refs_0_), channel_id=1, source_target_pairs={{0,24},{4,28},{8,16},{12,20},{16,8},{20,12},{24,0},{28,4},{1,25},{... | collective-permute-start | bytes 589832 | tf_op jit(solution)/shard_map/inner/ppermute | solution.py:285
  27.7 12.1 %collective-permute-start.10 = (bf16[64,1536]{1,0:T(8,128)(2,1)S(1)}, bf16[64,1536]{1,0:T(8,128)(2,1)S(1)}, u32[]{:S(2)}, u32[]{:S(2)}) collective-permute-start(bf16[64,1536]{1,0:T(8,128)(2,1)S(1)} %get-tuple-element.73.refs_0_), channel_id=1, source_target_pairs={{0,16},{4,20},{8,24},{12,28},{16,0},{20,4},{24,8},{28,12},{1,17},{... | collective-permute-start | bytes 589832 | tf_op jit(solution)/shard_map/inner/ppermute | solution.py:285
  29.2 10.5 %collective-permute-start.9 = (bf16[64,1536]{1,0:T(8,128)(2,1)S(1)}, bf16[64,1536]{1,0:T(8,128)(2,1)S(1)}, u32[]{:S(2)}, u32[]{:S(2)}) collective-permute-start(bf16[64,1536]{1,0:T(8,128)(2,1)S(1)} %get-tuple-element.73.refs_0_), channel_id=1, source_target_pairs={{0,8},{4,12},{8,0},{12,4},{16,24},{20,28},{24,16},{28,20},{1,9},{5... | collective-permute-start | bytes 589832 | tf_op jit(solution)/shard_map/inner/ppermute | solution.py:285
  29.5 18.0 %collective-permute-start.17 = (bf16[64,1536]{1,0:T(8,128)(2,1)S(1)}, bf16[64,1536]{1,0:T(8,128)(2,1)S(1)}, u32[]{:S(2)}, u32[]{:S(2)}) collective-permute-start(bf16[64,1536]{1,0:T(8,128)(2,1)S(1)} %get-tuple-element.79.refs_0_), channel_id=1, source_target_pairs={{0,24},{4,28},{8,16},{12,20},{16,8},{20,12},{24,0},{28,4},{1,25},{... | collective-permute-start | bytes 589832 | tf_op jit(solution)/shard_map/inner/ppermute | solution.py:285
  31.2 18.0 %collective-permute-start.16 = (bf16[64,1536]{1,0:T(8,128)(2,1)S(1)}, bf16[64,1536]{1,0:T(8,128)(2,1)S(1)}, u32[]{:S(2)}, u32[]{:S(2)}) collective-permute-start(bf16[64,1536]{1,0:T(8,128)(2,1)S(1)} %get-tuple-element.79.refs_0_), channel_id=1, source_target_pairs={{0,16},{4,20},{8,24},{12,28},{16,0},{20,4},{24,8},{28,12},{1,17},{... | collective-permute-start | bytes 589832 | tf_op jit(solution)/shard_map/inner/ppermute | solution.py:285
  34.9 14.3 %collective-permute-start.15 = (bf16[64,1536]{1,0:T(8,128)(2,1)S(1)}, bf16[64,1536]{1,0:T(8,128)(2,1)S(1)}, u32[]{:S(2)}, u32[]{:S(2)}) collective-permute-start(bf16[64,1536]{1,0:T(8,128)(2,1)S(1)} %get-tuple-element.79.refs_0_), channel_id=1, source_target_pairs={{0,8},{4,12},{8,0},{12,4},{16,24},{20,28},{24,16},{28,20},{1,9},{5... | collective-permute-start | bytes 589832 | tf_op jit(solution)/shard_map/inner/ppermute | solution.py:285
  45.6 7.1 %collective-permute-start.12 = (bf16[784,128]{1,0:T(8,128)(2,1)S(1)}, bf16[784,128]{1,0:T(8,128)(2,1)S(1)}, u32[]{:S(2)}, u32[]{:S(2)}) collective-permute-start(bf16[784,128]{1,0:T(8,128)(2,1)S(1)} %get-tuple-element.75), channel_id=1, source_target_pairs={{0,8},{4,12},{8,0},{12,4},{16,24},{20,28},{24,16},{28,20},{1,9},{5... | collective-permute-start | bytes 602120 | tf_op jit(solution)/shard_map/move_inner/ppermute | solution.py:285
  46.7 7.9 %collective-permute-start.13 = (bf16[784,128]{1,0:T(8,128)(2,1)S(1)}, bf16[784,128]{1,0:T(8,128)(2,1)S(1)}, u32[]{:S(2)}, u32[]{:S(2)}) collective-permute-start(bf16[784,128]{1,0:T(8,128)(2,1)S(1)} %get-tuple-element.76), channel_id=1, source_target_pairs={{0,16},{4,20},{8,24},{12,28},{16,0},{20,4},{24,8},{28,12},{1,17},{... | collective-permute-start | bytes 602120 | tf_op jit(solution)/shard_map/move_inner/ppermute | solution.py:285
  47.5 7.0 %collective-permute-start.14 = (bf16[784,128]{1,0:T(8,128)(2,1)S(1)}, bf16[784,128]{1,0:T(8,128)(2,1)S(1)}, u32[]{:S(2)}, u32[]{:S(2)}) collective-permute-start(bf16[784,128]{1,0:T(8,128)(2,1)S(1)} %get-tuple-element.77), channel_id=1, source_target_pairs={{0,24},{4,28},{8,16},{12,20},{16,8},{20,12},{24,0},{28,4},{1,25},{... | collective-permute-start | bytes 602120 | tf_op jit(solution)/shard_map/move_inner/ppermute | solution.py:285
  55.2 9.2 %collective-permute-start.18 = (bf16[784,128]{1,0:T(8,128)(2,1)S(1)}, bf16[784,128]{1,0:T(8,128)(2,1)S(1)}, u32[]{:S(2)}, u32[]{:S(2)}) collective-permute-start(bf16[784,128]{1,0:T(8,128)(2,1)S(1)} %get-tuple-element.92), channel_id=1, source_target_pairs={{0,1},{1,0},{2,3},{3,2},{4,5},{5,4},{6,7},{7,6},{8,9},{9,8},{10,11... | collective-permute-start | bytes 602120 | tf_op jit(solution)/shard_map/move_inner/ppermute | solution.py:291
  56.8 13.5 %collective-permute-start.19 = (bf16[784,128]{1,0:T(8,128)(2,1)S(1)}, bf16[784,128]{1,0:T(8,128)(2,1)S(1)}, u32[]{:S(2)}, u32[]{:S(2)}) collective-permute-start(bf16[784,128]{1,0:T(8,128)(2,1)S(1)} %get-tuple-element.93), channel_id=1, source_target_pairs={{0,2},{1,3},{2,0},{3,1},{4,6},{5,7},{6,4},{7,5},{8,10},{9,11},{10,... | collective-permute-start | bytes 602120 | tf_op jit(solution)/shard_map/move_inner/ppermute | solution.py:291
  57.9 12.4 %collective-permute-start.20 = (bf16[784,128]{1,0:T(8,128)(2,1)S(1)}, bf16[784,128]{1,0:T(8,128)(2,1)S(1)}, u32[]{:S(2)}, u32[]{:S(2)}) collective-permute-start(bf16[784,128]{1,0:T(8,128)(2,1)S(1)} %get-tuple-element.94), channel_id=1, source_target_pairs={{0,3},{1,2},{2,1},{3,0},{4,7},{5,6},{6,5},{7,4},{8,11},{9,10},{10,... | collective-permute-start | bytes 602120 | tf_op jit(solution)/shard_map/move_inner/ppermute | solution.py:291
  59.7 14.8 %collective-permute-start.27 = (bf16[784,128]{1,0:T(8,128)(2,1)S(1)}, bf16[784,128]{1,0:T(8,128)(2,1)S(1)}, u32[]{:S(2)}, u32[]{:S(2)}) collective-permute-start(bf16[784,128]{1,0:T(8,128)(2,1)S(1)} %get-tuple-element.84), channel_id=1, source_target_pairs={{0,8},{4,12},{8,0},{12,4},{16,24},{20,28},{24,16},{28,20},{1,9},{5... | collective-permute-start | bytes 602120 | tf_op jit(solution)/shard_map/move_inner/ppermute | solution.py:285
  60.6 14.2 %collective-permute-start.28 = (bf16[784,128]{1,0:T(8,128)(2,1)S(1)}, bf16[784,128]{1,0:T(8,128)(2,1)S(1)}, u32[]{:S(2)}, u32[]{:S(2)}) collective-permute-start(bf16[784,128]{1,0:T(8,128)(2,1)S(1)} %get-tuple-element.85), channel_id=1, source_target_pairs={{0,16},{4,20},{8,24},{12,28},{16,0},{20,4},{24,8},{28,12},{1,17},{... | collective-permute-start | bytes 602120 | tf_op jit(solution)/shard_map/move_inner/ppermute | solution.py:285
  64.4 10.4 %collective-permute-start.29 = (bf16[784,128]{1,0:T(8,128)(2,1)S(1)}, bf16[784,128]{1,0:T(8,128)(2,1)S(1)}, u32[]{:S(2)}, u32[]{:S(2)}) collective-permute-start(bf16[784,128]{1,0:T(8,128)(2,1)S(1)} %get-tuple-element.86), channel_id=1, source_target_pairs={{0,24},{4,28},{8,16},{12,20},{16,8},{20,12},{24,0},{28,4},{1,25},{... | collective-permute-start | bytes 602120 | tf_op jit(solution)/shard_map/move_inner/ppermute | solution.py:285
  71.2 8.1 %collective-permute-start.23 = (bf16[784,128]{1,0:T(8,128)(2,1)S(1)}, bf16[784,128]{1,0:T(8,128)(2,1)S(1)}, u32[]{:S(2)}, u32[]{:S(2)}) collective-permute-start(bf16[784,128]{1,0:T(8,128)(2,1)S(1)} %sum_inner.2.refs_0_), channel_id=1, source_target_pairs={{0,24},{4,28},{8,16},{12,20},{16,8},{20,12},{24,0},{28,4},{1,25},{... | collective-permute-start | bytes 602120 | tf_op jit(solution)/shard_map/outer/ppermute | solution.py:285
  72.3 8.6 %collective-permute-start.22 = (bf16[784,128]{1,0:T(8,128)(2,1)S(1)}, bf16[784,128]{1,0:T(8,128)(2,1)S(1)}, u32[]{:S(2)}, u32[]{:S(2)}) collective-permute-start(bf16[784,128]{1,0:T(8,128)(2,1)S(1)} %sum_inner.2.refs_0_), channel_id=1, source_target_pairs={{0,16},{4,20},{8,24},{12,28},{16,0},{20,4},{24,8},{28,12},{1,17},{... | collective-permute-start | bytes 602120 | tf_op jit(solution)/shard_map/outer/ppermute | solution.py:285
  75.6 8.3 %collective-permute-start.30 = (bf16[784,128]{1,0:T(8,128)(2,1)S(1)}, bf16[784,128]{1,0:T(8,128)(2,1)S(1)}, u32[]{:S(2)}, u32[]{:S(2)}) collective-permute-start(bf16[784,128]{1,0:T(8,128)(2,1)S(1)} %get-tuple-element.100), channel_id=1, source_target_pairs={{0,1},{1,0},{2,3},{3,2},{4,5},{5,4},{6,7},{7,6},{8,9},{9,8},{10,11... | collective-permute-start | bytes 602120 | tf_op jit(solution)/shard_map/move_inner/ppermute | solution.py:291
  78.5 15.5 %collective-permute-start.31 = (bf16[784,128]{1,0:T(8,128)(2,1)S(1)}, bf16[784,128]{1,0:T(8,128)(2,1)S(1)}, u32[]{:S(2)}, u32[]{:S(2)}) collective-permute-start(bf16[784,128]{1,0:T(8,128)(2,1)S(1)} %get-tuple-element.101), channel_id=1, source_target_pairs={{0,2},{1,3},{2,0},{3,1},{4,6},{5,7},{6,4},{7,5},{8,10},{9,11},{10,... | collective-permute-start | bytes 602120 | tf_op jit(solution)/shard_map/move_inner/ppermute | solution.py:291
  79.4 14.5 %collective-permute-start.32 = (bf16[784,128]{1,0:T(8,128)(2,1)S(1)}, bf16[784,128]{1,0:T(8,128)(2,1)S(1)}, u32[]{:S(2)}, u32[]{:S(2)}) collective-permute-start(bf16[784,128]{1,0:T(8,128)(2,1)S(1)} %get-tuple-element.102), channel_id=1, source_target_pairs={{0,3},{1,2},{2,1},{3,0},{4,7},{5,6},{6,5},{7,4},{8,11},{9,10},{10,... | collective-permute-start | bytes 602120 | tf_op jit(solution)/shard_map/move_inner/ppermute | solution.py:291
  94.9 8.1 %collective-permute-start.35 = (bf16[784,128]{1,0:T(8,128)(2,1)S(1)}, bf16[784,128]{1,0:T(8,128)(2,1)S(1)}, u32[]{:S(2)}, u32[]{:S(2)}) collective-permute-start(bf16[784,128]{1,0:T(8,128)(2,1)S(1)} %sum_inner.3.refs_0_), channel_id=1, source_target_pairs={{0,24},{4,28},{8,16},{12,20},{16,8},{20,12},{24,0},{28,4},{1,25},{... | collective-permute-start | bytes 602120 | tf_op jit(solution)/shard_map/outer/ppermute | solution.py:285
  96.4 9.0 %collective-permute-start.34 = (bf16[784,128]{1,0:T(8,128)(2,1)S(1)}, bf16[784,128]{1,0:T(8,128)(2,1)S(1)}, u32[]{:S(2)}, u32[]{:S(2)}) collective-permute-start(bf16[784,128]{1,0:T(8,128)(2,1)S(1)} %sum_inner.3.refs_0_), channel_id=1, source_target_pairs={{0,16},{4,20},{8,24},{12,28},{16,0},{20,4},{24,8},{28,12},{1,17},{... | collective-permute-start | bytes 602120 | tf_op jit(solution)/shard_map/outer/ppermute | solution.py:285
  98.1 7.3 %collective-permute-start.33 = (bf16[784,128]{1,0:T(8,128)(2,1)S(1)}, bf16[784,128]{1,0:T(8,128)(2,1)S(1)}, u32[]{:S(2)}, u32[]{:S(2)}) collective-permute-start(bf16[784,128]{1,0:T(8,128)(2,1)S(1)} %sum_inner.3.refs_0_), channel_id=1, source_target_pairs={{0,8},{4,12},{8,0},{12,4},{16,24},{20,28},{24,16},{28,20},{1,9},{5... | collective-permute-start | bytes 602120 | tf_op jit(solution)/shard_map/outer/ppermute | solution.py:285
  98.4 15.5 %collective-permute-start.24 = (bf16[272,128]{1,0:T(8,128)(2,1)S(1)}, bf16[272,128]{1,0:T(8,128)(2,1)S(1)}, u32[]{:S(2)}, u32[]{:S(2)}) collective-permute-start(bf16[272,128]{1,0:T(8,128)(2,1)S(1)} %get-tuple-element.96), channel_id=1, source_target_pairs={{0,1},{1,0},{2,3},{3,2},{4,5},{5,4},{6,7},{7,6},{8,9},{9,8},{10,11... | collective-permute-start | bytes 208904 | tf_op jit(solution)/shard_map/outer/ppermute | solution.py:291
  101.2 14.2 %collective-permute-start.25 = (bf16[272,128]{1,0:T(8,128)(2,1)S(1)}, bf16[272,128]{1,0:T(8,128)(2,1)S(1)}, u32[]{:S(2)}, u32[]{:S(2)}) collective-permute-start(bf16[272,128]{1,0:T(8,128)(2,1)S(1)} %get-tuple-element.97), channel_id=1, source_target_pairs={{0,2},{1,3},{2,0},{3,1},{4,6},{5,7},{6,4},{7,5},{8,10},{9,11},{10,... | collective-permute-start | bytes 208904 | tf_op jit(solution)/shard_map/outer/ppermute | solution.py:291
  103.0 12.4 %collective-permute-start.26 = (bf16[272,128]{1,0:T(8,128)(2,1)S(1)}, bf16[272,128]{1,0:T(8,128)(2,1)S(1)}, u32[]{:S(2)}, u32[]{:S(2)}) collective-permute-start(bf16[272,128]{1,0:T(8,128)(2,1)S(1)} %get-tuple-element.98), channel_id=1, source_target_pairs={{0,3},{1,2},{2,1},{3,0},{4,7},{5,6},{6,5},{7,4},{8,11},{9,10},{10,... | collective-permute-start | bytes 208904 | tf_op jit(solution)/shard_map/outer/ppermute | solution.py:291
  108.4 7.0 %collective-permute-start.36 = (bf16[272,128]{1,0:T(8,128)(2,1)S(1)}, bf16[272,128]{1,0:T(8,128)(2,1)S(1)}, u32[]{:S(2)}, u32[]{:S(2)}) collective-permute-start(bf16[272,128]{1,0:T(8,128)(2,1)S(1)} %get-tuple-element.108), channel_id=1, source_target_pairs={{0,1},{1,0},{2,3},{3,2},{4,5},{5,4},{6,7},{7,6},{8,9},{9,8},{10,11... | collective-permute-start | bytes 208904 | tf_op jit(solution)/shard_map/outer/ppermute | solution.py:291
  114.0 6.5 %collective-permute-start.38 = (bf16[272,128]{1,0:T(8,128)(2,1)S(1)}, bf16[272,128]{1,0:T(8,128)(2,1)S(1)}, u32[]{:S(2)}, u32[]{:S(2)}) collective-permute-start(bf16[272,128]{1,0:T(8,128)(2,1)S(1)} %get-tuple-element.110), channel_id=1, source_target_pairs={{0,3},{1,2},{2,1},{3,0},{4,7},{5,6},{6,5},{7,4},{8,11},{9,10},{10,... | collective-permute-start | bytes 208904 | tf_op jit(solution)/shard_map/outer/ppermute | solution.py:291
  (11 other events, 73.8 us)

commit v3 on v2

--- a/solution.py
+++ b/solution.py
@@ -11,6 +11,11 @@
 HEAD = 16
 SPAN = 126.0
 CHUNKS = 2
+MERGE = True
+BATCHES = ((0, 1, 2), (3,))
+ORDER = {"out_1": ["out_0"]}
+FORWARD = {"p3_0": False, "p3_1": False, "q3_0": False, "q3_1": False}
+HALVE = {"q2_0": True, "q2_1": True, "o_0": False, "o_1": True}
 BF = jnp.bfloat16
 F32 = jnp.float32
 
@@ -69,17 +74,20 @@
     return ref[0:1, :].astype(F32)
 
 
+def spread_head(bound):
+    return jnp.broadcast_to(bound, (HEAD, LANES)).astype(BF)
+
+
 def put_head(ref, bound):
-    ref[0:HEAD, :] = jnp.broadcast_to(bound, (HEAD, LANES)).astype(BF)
-
-
-def call(body, outs, scratch, name, args, flops=0):
-    nbytes = sum(a.size * a.dtype.itemsize for a in args) + sum(
-        functools.reduce(lambda p, q: p * q, o.shape) * o.dtype.itemsize for o in outs
+    ref[0:HEAD, :] = spread_head(bound)
+
+
+def call(body, outs, scratch, name, args, flops=0, far=0):
+    specs = (
+        [pl.BlockSpec(memory_space=pltpu.SMEM)]
+        + [pl.BlockSpec(memory_space=pltpu.HBM)] * far
+        + [pl.BlockSpec(memory_space=pltpu.VMEM)] * (len(args) - 1 - far)
     )
-    specs = [pl.BlockSpec(memory_space=pltpu.SMEM)] + [
-        pl.BlockSpec(memory_space=pltpu.VMEM)
-    ] * (len(args) - 1)
     return pl.pallas_call(
         body,
         out_shape=outs,
@@ -88,7 +96,7 @@
         scratch_shapes=scratch,
         compiler_params=pltpu.CompilerParams(vmem_limit_bytes=24 * 1024 * 1024),
         cost_estimate=pl.CostEstimate(
-            flops=flops, bytes_accessed=nbytes, transcendentals=0
+            flops=1, bytes_accessed=1, transcendentals=0
         ),
         name=name,
     )(*args)
@@ -123,20 +131,30 @@
 
 def chunk_body(parts, chunks, where_ref, *refs):
     ins, outs = refs[:parts], refs[parts:]
-    step = outs[0].shape[0] // parts
+    step = ins[0].shape[0] // chunks
+    size = parts * step * chunks // len(outs)
     for e in range(chunks):
         for d in range(parts):
-            outs[e][d * step : (d + 1) * step, :] = ins[d][e * step : (e + 1) * step, :]
-
-
-def inner_body(parts, rows, where_ref, w_own_ref, w_twin_ref, *refs):
-    ins, outs = refs[:parts], refs[parts : 2 * parts]
-    x_ref, t_ref = refs[2 * parts :]
-    group = ins[0].shape[0]
-    for i in range(parts):
-        x_ref[i * group : (i + 1) * group, :] = ins[i][...]
+            at = (e * parts + d) * step
+            out = outs[at // size]
+            out[at % size : at % size + step, :] = ins[d][e * step : (e + 1) * step, :]
+
+
+def fetch_body(where_ref, far_ref, near_ref, sem):
+    copy = pltpu.make_async_copy(far_ref, near_ref, sem)
+    copy.start()
+    copy.wait()
+
+
+def inner_body(n, chunks, rows, where_ref, w_own_ref, w_twin_ref, *refs):
+    ins, outs = refs[:n], refs[n : n + n * chunks]
+    x_ref, t_ref = refs[n + n * chunks :]
+    size = ins[0].shape[0]
+    group = size // chunks
+    for i in range(n):
+        x_ref[i * size : (i + 1) * size, :] = ins[i][...]
     n_g = w_own_ref.shape[1]
-    tops = [jnp.zeros((8, LANES), F32) for _ in range(parts)]
+    tops = [jnp.zeros((8, LANES), F32) for _ in range(n * chunks)]
     tile = 256
     for c, w_ref in enumerate((w_own_ref, w_twin_ref)):
         for g in range(0, n_g, tile):
@@ -147,13 +165,13 @@
             t_re = with_re[:, 0] - with_im[:, 1]
             t_im = with_im[:, 0] + with_re[:, 1]
             both = jnp.stack([t_re, t_im], axis=1).reshape(-1, tile)
-            for i in range(parts):
+            for i in range(n * chunks):
                 mine = both[i * group : (i + 1) * group]
                 for l in range(0, tile, LANES):
                     block = mine[:, l : l + LANES]
                     tops[i] = jnp.maximum(tops[i], fold_top(block))
                     t_ref[i, (c * n_g + g + l) // LANES] = block
-    for i in range(parts):
+    for i in range(n * chunks):
         bound = bound_of(tops[i])
         put_head(outs[i], bound)
         for l in range(2 * n_g // LANES):
@@ -161,9 +179,70 @@
             outs[i][at : at + group, :] = code(t_ref[i, l], bound)
 
 
-def sum_body(parts, where_ref, *refs):
-    ins, out = refs[:parts], refs[parts]
-    t_ref = refs[parts + 1]
+def deal_body(parts, where_ref, *refs):
+    ins, (own_ref, far_ref, sent_ref) = refs[:parts], refs[parts:]
+    size = own_ref.shape[0]
+    m = where_ref[2]
+    for v in range(parts):
+
+        @pl.when(m == v)
+        def _(v=v):
+            own_ref[...] = ins[v][...]
+            far_ref[...] = ins[v ^ 2][...]
+            sent_ref[0:size, :] = ins[v ^ 1][...]
+            sent_ref[size:, :] = ins[v ^ 3][...]
+
+
+def fold_body(parts, where_ref, own_ref, far_ref, got_ref, kept_ref, sent_ref, t_ref):
+    n_l, group, _ = kept_ref.shape
+    step = group // parts
+    size = own_ref.shape[0]
+    own_bound, far_bound = head_of(own_ref), head_of(far_ref)
+    near_bound = head_of(got_ref)
+    next_bound = got_ref[size : size + 1, :].astype(F32)
+    top = jnp.zeros((8, LANES), F32)
+    for l in range(n_l):
+        for s in range(parts):
+            here = HEAD + l * group + s * step
+            there = HEAD + l * group + (s ^ 1) * step
+            to = slice(s * step, (s + 1) * step)
+            kept_ref[l, to, :] = decode(
+                own_ref[here : here + step, :], own_bound
+            ) + decode(got_ref[there : there + step, :], near_bound)
+            there += size
+            total = decode(far_ref[here : here + step, :], far_bound) + decode(
+                got_ref[there : there + step, :], next_bound
+            )
+            top = jnp.maximum(top, fold_top(total))
+            t_ref[l, to, :] = total
+    bound = bound_of(top)
+    put_head(sent_ref, bound)
+    for l in range(n_l):
+        at = HEAD + l * group
+        sent_ref[at : at + group, :] = code(t_ref[l], bound)
+
+
+def sum_body(parts, where_ref, kept_ref, got_ref, out_ref, t_ref):
+    n_l, group, _ = kept_ref.shape
+    step = group // parts
+    bound = head_of(got_ref)
+    top = jnp.zeros((8, LANES), F32)
+    for l in range(n_l):
+        for s in range(parts):
+            there = HEAD + l * group + (s ^ 2) * step
+            to = slice(s * step, (s + 1) * step)
+            total = kept_ref[l, to, :] + decode(got_ref[there : there + step, :], bound)
+            top = jnp.maximum(top, fold_top(total))
+            t_ref[l, to, :] = total
+    bound = bound_of(top)
+    put_head(out_ref, bound)
+    for l in range(n_l):
+        at = HEAD + l * group
+        out_ref[at : at + group, :] = code(t_ref[l], bound)
+
+
+def add_body(parts, where_ref, *refs):
+    ins, out, t_ref = refs[:parts], refs[parts], refs[parts + 1]
     n_l, group = t_ref.shape[0], t_ref.shape[1]
     step = group // parts
     top = jnp.zeros((8, LANES), F32)
@@ -184,9 +263,9 @@
         out[at : at + group, :] = code(t_ref[l], bound)
 
 
-def outer_body(parts, rows, where_ref, a_own_ref, a_twin_ref, *refs):
-    ins, outs = refs[:parts], refs[parts : 2 * parts]
-    hi_ref, lo_ref = refs[2 * parts :]
+def outer_body(parts, rows, plain, n_out, where_ref, a_own_ref, a_twin_ref, *refs):
+    ins, outs = refs[:parts], refs[parts : parts + n_out]
+    hi_ref, lo_ref = refs[parts + n_out :]
     core = where_ref[1]
     n_l = hi_ref.shape[1] // LANES
     group = (ins[0].shape[0] - HEAD) // n_l
@@ -213,36 +292,49 @@
             both = jnp.stack([k_re[:, d], k_im[:, d]], axis=1).reshape(-1, n_p)
             for l in range(0, n_p, LANES):
                 block = both[:, l : l + LANES]
-                if d:
+                if d >= plain:
                     tops[d] = jnp.maximum(tops[d], fold_top(block))
                 blocks[d].append(block)
     for d in range(parts):
         n_r = blocks[d][0].shape[0]
-        if d == 0:
-            for l, block in enumerate(blocks[0]):
-                outs[0][l * n_r : (l + 1) * n_r, :] = block
+        if d < plain:
+            for l, block in enumerate(blocks[d]):
+                outs[d][l * n_r : (l + 1) * n_r, :] = block
             continue
         bound = bound_of(tops[d])
-        put_head(outs[d], bound)
+        out = outs[min(d, len(outs) - 1)]
+        start = (d - min(d, len(outs) - 1)) * (HEAD + len(blocks[d]) * n_r)
+        out[start : start + HEAD, :] = spread_head(bound)
         for l, block in enumerate(blocks[d]):
-            at = HEAD + l * n_r
-            outs[d][at : at + n_r, :] = code(block, bound)
-
-
-def last_body(parts, chunks, rows, where_ref, *refs):
-    ins, outs = refs[: parts * chunks], refs[parts * chunks :]
+            at = start + HEAD + l * n_r
+            out[at : at + n_r, :] = code(block, bound)
+
+
+def halve_body(where_ref, own_ref, near_ref, got_ref, kept_ref, sent_ref):
+    n_r = own_ref.shape[0]
+    kept_ref[...] = own_ref[...] + decode(got_ref[HEAD : HEAD + n_r, :], head_of(got_ref))
+    start = HEAD + n_r
+    bound = got_ref[start : start + 1, :].astype(F32)
+    near = near_ref[...] + decode(got_ref[start + HEAD :, :], bound)
+    bound = bound_of(fold_top(near))
+    sent_ref[0:HEAD, :] = spread_head(bound)
+    sent_ref[HEAD:, :] = code(near, bound)
+
+
+def last_body(parts, counts, rows, where_ref, *refs):
+    ins, outs = list(refs[: sum(counts)]), refs[sum(counts) :]
     t = where_ref[0]
-    sub = rows * chunks
+    sub = rows * len(counts)
     n_l = outs[0].shape[2] // LANES
-    for e in range(chunks):
-        mine = ins[e * parts]
+    for e, count in enumerate(counts):
+        mine, *others = [ins.pop(0) for _ in range(count)]
         n_r = mine.shape[0] // (2 * n_l)
-        bounds = [None] + [head_of(ins[e * parts + d]) for d in range(1, parts)]
+        bounds = [head_of(x) for x in others]
         for l in range(2 * n_l):
             total = mine[l * n_r : (l + 1) * n_r, :]
-            for d in range(1, parts):
-                at = HEAD + l * n_r
-                total = total + decode(ins[e * parts + d][at : at + n_r, :], bounds[d])
+            at = HEAD + l * n_r
+            for x, bound in zip(others, bounds):
+                total = total + decode(x[at : at + n_r, :], bound)
             total = total.reshape(parts, 2, rows, LANES)
             out, lane = outs[l // n_l], l % n_l * LANES
             for i in range(parts):
@@ -302,22 +394,30 @@
             functools.partial(route_body, parts), outs, [], name, [where, *arrays]
         )
 
+    def fetch(x):
+        outs, scratch = [shape(x.shape, x.dtype)], [pltpu.SemaphoreType.DMA]
+        return call(fetch_body, outs, scratch, "fetch", [where, x], far=1)[0]
+
     with jax.named_scope("spread_vv"):
         theirs = twin(pair_vv)
+        mine = fetch(pair_vv)
         cut = call(
             functools.partial(spread_body, parts, chunks),
             [shape((2 * sub, 2 * width), BF)] * parts,
             [],
             "spread_vv",
-            [where, pair_vv, theirs],
+            [where, mine, theirs],
         )
         late = after([screened, pair_cc], *cut)
         screened_twin, pair_cc_twin = twin(late[0]), twin(late[1])
         cut = alongs(route(planes(cut), "route_vv"))
-        cut = after(cut, screened_twin, pair_cc_twin)
+        screened_own = fetch(late[0])
+        cut = after(cut, screened_own, screened_twin, pair_cc_twin)
         own = call(
             functools.partial(chunk_body, parts, chunks),
-            [shape((group, 2 * width), BF)] * chunks,
+            [shape((group * chunks, 2 * width), BF)]
+            if MERGE
+            else [shape((group, 2 * width), BF)] * chunks,
             [],
             "chunk_vv",
             [where, *cut],
@@ -326,61 +426,164 @@
     term = shape((HEAD + 2 * n_p // LANES * group, LANES), BF)
 
     def inner_of(groups):
+        n = len(groups)
         return call(
-            functools.partial(inner_body, parts, rows),
-            [coded] * parts,
+            functools.partial(inner_body, n, chunks, rows),
+            [coded] * (n * chunks),
             [
-                pltpu.VMEM((parts * group, 2 * width), BF),
-                pltpu.VMEM((parts, total_g // LANES, group, LANES), F32),
+                pltpu.VMEM((n * chunks * group, 2 * width), BF),
+                pltpu.VMEM((n * chunks, total_g // LANES, group, LANES), F32),
             ],
             "inner",
-            [where, screened, screened_twin, *groups],
-            flops=2 * parts * group * 2 * width * 2 * total_g,
-        )
-
-    def sum_of(arrays):
-        (total,) = call(
-            functools.partial(sum_body, parts),
-            [coded],
-            [pltpu.VMEM((total_g // LANES, group, LANES), F32)],
-            "sum_inner",
-            [where, *arrays],
-        )
-        return total
-
-    def outer_of(arrays):
+            [where, screened_own, screened_twin, *groups],
+        )
+
+    summed = pltpu.VMEM((total_g // LANES, group, LANES), F32)
+
+    def deal(arrays):
+        outs = [coded, coded, shape((2 * coded.shape[0], LANES), BF)]
+        body = functools.partial(deal_body, parts)
+        return call(body, outs, [], "deal_inner", [where, *arrays])
+
+    def fold(own, far, got):
+        outs = [shape((total_g // LANES, group, LANES), F32), coded]
+        body = functools.partial(fold_body, parts)
+        return call(body, outs, [summed], "fold_inner", [where, own, far, got])
+
+    def sum_of(kept, got):
+        body = functools.partial(sum_body, parts)
+        return call(body, [coded], [summed], "sum_inner", [where, kept, got])[0]
+
+    def outer_of(arrays, halving):
+        n_r = 2 * n_p // LANES * group
+        whole = shape((n_r, LANES), F32)
+        if halving:
+            outs = [whole, whole, shape((2 * (HEAD + n_r), LANES), BF)]
+        else:
+            outs = [whole] + [term] * (parts - 1)
+        plain = 2 if halving else 1
         return call(
-            functools.partial(outer_body, parts, rows),
-            [shape((2 * n_p // LANES * group, LANES), F32)] + [term] * (parts - 1),
+            functools.partial(outer_body, parts, rows, plain, len(outs)),
+            outs,
             [pltpu.VMEM((parts * group, n_k), BF)] * 2,
             "outer",
             [where, pair_cc, pair_cc_twin, *arrays],
-            flops=4 * parts * group * n_k * 4 * n_p,
-        )
-
-    with jax.named_scope("inner"):
-        groups = [planes([own[e]] * parts) for e in range(chunks)]
-        inner, routed = [], []
+        )
+
+    done = {}
+
+    def step(name, arrays):
+        late = [a for other in ORDER.get(name, ()) for a in done[other]]
+        return after(arrays, *late) if late else tuple(arrays)
+
+    def tell(name, arrays):
+        done[name] = list(arrays)
+        return arrays
+
+    def gathered_of(x, forward):
+        if not forward:
+            return planes([x] * parts)
+        near = plane(x, 1)
+        return [x, near, plane(x, 2), plane(near, 2)]
+
+    def add(arrays):
+        body = functools.partial(add_body, parts)
+        return call(body, [coded], [summed], "add_inner", [where, *arrays])[0]
+
+    def gather_vv(e):
+        if MERGE and e:
+            return tell(f"p3_{e}", done["p3_0"])
+        (x,) = step(f"p3_{e}", [own[e]])
+        return tell(f"p3_{e}", gathered_of(x, FORWARD[f"p3_{e}"]))
+
+    def inner_step(e, groups):
+        if e == 0:
+            found = []
+            for batch in BATCHES:
+                found += inner_of([groups[i] for i in batch])
+            tell("inner", found)
+        return done["inner"][e::chunks]
+
+    def spread_step(e, arrays):
+        mine, *sent = step(f"q1_{e}", arrays)
+        return tell(f"q1_{e}", planes([mine, *sent]))
+
+    def deal_step(e, arrays):
+        arrays = step(f"deal_{e}", arrays)
+        if HALVE[f"q2_{e}"]:
+            return tell(f"deal_{e}", deal(arrays))
+        return tell(f"deal_{e}", route(arrays, "route_inner"))
+
+    def move_step(e, arrays):
+        arrays = step(f"s1_{e}", arrays)
+        if not HALVE[f"q2_{e}"]:
+            got = tell(f"s1_{e}", alongs(arrays))
+            return tell(f"sum_{e}", [add(step(f"sum_{e}", got))])[0]
+        mine, far, sent = arrays
+        (got,) = tell(f"s1_{e}", [along(sent, 1)])
+        kept, sent = tell(f"fold_{e}", fold(*step(f"fold_{e}", [mine, far, got])))
+        (sent,) = step(f"s2_{e}", [sent])
+        (got,) = tell(f"s2_{e}", [along(sent, 2)])
+        return tell(f"sum_{e}", [sum_of(*step(f"sum_{e}", [kept, got]))])[0]
+
+    def gather_step(e, x):
+        (x,) = step(f"q3_{e}", [x])
+        return tell(f"q3_{e}", gathered_of(x, FORWARD[f"q3_{e}"]))
+
+    def outer_step(e, arrays):
+        return tell(f"out_{e}", outer_of(step(f"out_{e}", arrays), HALVE[f"o_{e}"]))
+
+    def final_step(e, arrays):
+        arrays = step(f"o_{e}", arrays)
+        if not HALVE[f"o_{e}"]:
+            return tell(f"o_{e}", alongs(arrays))
+        kept, near, sent = arrays
+        kept, sent = call(
+            halve_body,
+            [shape(kept.shape, F32), term],
+            [],
+            "halve",
+            [where, *step(f"half_{e}", [kept, near, along(sent, 2)])],
+        )
+        done[f"half_{e}"] = [kept, sent]
+        return tell(f"o_{e}", [kept, along(sent, 1)])
+
+    state = [None] * chunks
+    stages = (
+        lambda e, x: gather_vv(e),
+        inner_step,
+        spread_step,
+        deal_step,
+        move_step,
+        gather_step,
+        outer_step,
+        final_step,
+    )
+    names = ("p3", "in", "q1", "deal", "s1", "q3", "out", "o")
+    pending = [0] * chunks
+    while min(pending) < len(stages):
+        moved = False
         for e in range(chunks):
-            got = groups[e] if e == 0 else after(groups[e], *inner[e - 1])
-            inner.append(inner_of(got))
-    with jax.named_scope("move_inner"):
-        for e in range(chunks):
-            spread = planes(inner[e])
-            if e + 1 < chunks:
-                spread = after(spread, *inner[e + 1])
-            routed.append(route(spread, "route_inner"))
-        moved = [alongs(x) for x in routed]
-    finals, outer = [], None
-    with jax.named_scope("outer"):
-        for e in range(chunks):
-            got = moved[e] if e == 0 else after(moved[e], *outer)
-            total = sum_of(got)
-            outer = outer_of(planes([total] * parts))
-            finals += alongs(outer)
+            n = pending[e]
+            if n == len(stages):
+                continue
+            needs = [f"{names[n]}_{e}"]
+            if names[n] == "s1":
+                needs += [f"fold_{e}", f"s2_{e}", f"sum_{e}"]
+            if names[n] == "o":
+                needs += [f"half_{e}"]
+            wanted = [o for name in needs for o in ORDER.get(name, ())]
+            if any(o not in done and not o.endswith(f"_{e}") for o in wanted):
+                continue
+            state[e] = stages[n](e, state[e])
+            pending[e] += 1
+            moved = True
+        assert moved
+    finals = [x for e in range(chunks) for x in state[e]]
+    counts = tuple(len(x) for x in state)
     with jax.named_scope("sum_outer"):
         own, theirs = call(
-            functools.partial(last_body, parts, chunks, rows),
+            functools.partial(last_body, parts, counts, rows),
             [shape((2, half, n_p), F32)] * 2,
             [],
             "sum_outer",
@@ -412,6 +615,7 @@
             power_of_two(n_row)
             and power_of_two(n_col)
             and n_row == 2 * n_col
+            and n_col == 4
             and n_q % (2 * n_col * CHUNKS * 8) == 0
             and n_q % (2 * n_col * 16) == 0
             and width % LANES == 0

time: 124 us -> 118 us (0.952)
  starting transfers between devices: 56.2 us -> 42.3 us
  Pallas kernels: 20 us -> 25.5 us
  waiting for transfers between devices: 44.2 us -> 46.5 us
    ppermute x21 -> x18, waiting for transfers between devices: 12.8 us -> 21.9 us  [plane(): return lax.ppermute(x, 'row', pairs)]
    ppermute x15 -> x12, starting transfers between devices: 28.1 us -> 19.2 us  [along(): return lax.ppermute(x, 'col', [(a, a ^ d) for a in range(parts)])]
    pallas_call x13 -> x18, Pallas kernels: 20 us -> 25.5 us  [call(): pl.pallas_call(body, out_shape=outs, in_specs=specs, out_specs=[pl.BlockS...]
    ppermute x15 -> x12, waiting for transfers between devices: 28.5 us -> 23.2 us  [along(): return lax.ppermute(x, 'col', [(a, a ^ d) for a in range(parts)])]
    ppermute x21 -> x18, starting transfers between devices: 27 us -> 22 us  [plane(): return lax.ppermute(x, 'row', pairs)]
    ppermute x4, waiting for transfers between devices: 2.82 us -> 1.34 us  [twin(): return lax.ppermute(x, 'row', [(a, a ^ 1) for a in range(n_row)])]
  transfers between devices with their start and end apart: 40 -> 34, of which waited for: 16 -> 18; matrix products, arithmetic and copies ran while one was open for 0% -> 0% of each run, Pallas kernels for 12% -> 16%
where the time goes in v3:
time: 118 us
  waiting for transfers between devices  46.5 us (39%)
  starting transfers between devices  42.3 us (36%)
  Pallas kernels  25.5 us (22%)
  local copies, waits for them, and re-layouts  3.34 us (3%)
    pallas_call x18, Pallas kernels, call(): pl.pallas_call(body, out_shape=outs, in_specs=specs, out_specs=[pl.BlockS...  25.5 us
    ppermute x12, waiting for transfers between devices, along(): return lax.ppermute(x, 'col', [(a, a ^ d) for a in range(parts)])  23.2 us
    ppermute x18, starting transfers between devices, plane(): return lax.ppermute(x, 'row', pairs)  22 us
    ppermute x18, waiting for transfers between devices, plane(): return lax.ppermute(x, 'row', pairs)  21.9 us
    ppermute x12, starting transfers between devices, along(): return lax.ppermute(x, 'col', [(a, a ^ d) for a in range(parts)])  19.2 us
    unnamed x6, local copies, waits for them, and re-layouts  3.34 us
  transfers between devices with their start and end apart: 34, of which 18 were waited for; matrix products, arithmetic and copies ran while one was open for 0% of the time, Pallas kernels for 16%

profile of v3, /device:TPU:0, one launch (start us, length us, event | category | flops | bytes accessed | tf_op | source)
XLA Modules:
  0.0 117.9 jit_solution(6079133296662391053)
XLA Ops:
  3.4 2.6 %collective-permute-start.3 = (bf16[32,1536]{1,0:T(8,128)(2,1)S(1)}, bf16[32,1536]{1,0:T(8,128)(2,1)S(1)}, u32[]{:S(2)}, u32[]{:S(2)}) collective-permute-start(bf16[32,1536]{1,0:T(8,128)(2,1)S(1)} %get-tuple-element.53), channel_id=1, source_target_pairs={{0,8},{4,12},{8,0},{12,4},{16,24},{20,28},{24,16},{28,20},{1,9},{5... | collective-permute-start | bytes 294920 | tf_op jit(solution)/shard_map/spread_vv/ppermute | solution.py:377
  6.0 1.5 %collective-permute-start.4 = (bf16[32,1536]{1,0:T(8,128)(2,1)S(1)}, bf16[32,1536]{1,0:T(8,128)(2,1)S(1)}, u32[]{:S(2)}, u32[]{:S(2)}) collective-permute-start(bf16[32,1536]{1,0:T(8,128)(2,1)S(1)} %get-tuple-element.54), channel_id=1, source_target_pairs={{0,16},{4,20},{8,24},{12,28},{16,0},{20,4},{24,8},{28,12},{1,17},{... | collective-permute-start | bytes 294920 | tf_op jit(solution)/shard_map/spread_vv/ppermute | solution.py:377
  7.6 1.8 %collective-permute-done.3.refs_1_ = bf16[32,1536]{1,0:T(8,128)(2,1)S(1)} collective-permute-done((bf16[32,1536]{1,0:T(8,128)(2,1)S(1)}, bf16[32,1536]{1,0:T(8,128)(2,1)S(1)}, u32[]{:S(2)}, u32[]{:S(2)}) %collective-permute-start.3) | collective-permute-done | bytes 98336 | tf_op jit(solution)/shard_map/spread_vv/ppermute | solution.py:377
  9.4 2.6 %collective-permute-done.4.refs_2_ = bf16[32,1536]{1,0:T(8,128)(2,1)S(1)} collective-permute-done((bf16[32,1536]{1,0:T(8,128)(2,1)S(1)}, bf16[32,1536]{1,0:T(8,128)(2,1)S(1)}, u32[]{:S(2)}, u32[]{:S(2)}) %collective-permute-start.4) | collective-permute-done | bytes 98336 | tf_op jit(solution)/shard_map/spread_vv/ppermute | solution.py:377
  13.7 1.6 %collective-permute-start.6 = (bf16[32,1536]{1,0:T(8,128)(2,1)S(1)}, bf16[32,1536]{1,0:T(8,128)(2,1)S(1)}, u32[]{:S(2)}, u32[]{:S(2)}) collective-permute-start(bf16[32,1536]{1,0:T(8,128)(2,1)S(1)} %get-tuple-element.59), channel_id=1, source_target_pairs={{0,1},{1,0},{2,3},{3,2},{4,5},{5,4},{6,7},{7,6},{8,9},{9,8},{10,11... | collective-permute-start | bytes 294920 | tf_op jit(solution)/shard_map/spread_vv/ppermute | solution.py:383
  15.3 2.6 %collective-permute-start.7 = (bf16[32,1536]{1,0:T(8,128)(2,1)S(1)}, bf16[32,1536]{1,0:T(8,128)(2,1)S(1)}, u32[]{:S(2)}, u32[]{:S(2)}) collective-permute-start(bf16[32,1536]{1,0:T(8,128)(2,1)S(1)} %get-tuple-element.60), channel_id=1, source_target_pairs={{0,2},{1,3},{2,0},{3,1},{4,6},{5,7},{6,4},{7,5},{8,10},{9,11},{10,... | collective-permute-start | bytes 294920 | tf_op jit(solution)/shard_map/spread_vv/ppermute | solution.py:383
  18.1 2.3 %copy-done.1 = bf16[2,768,1536]{2,1,0:T(8,128)(2,1)S(1)} copy-done((bf16[2,768,1536]{2,1,0:T(8,128)(2,1)S(1)}, bf16[2,768,1536]{2,1,0:T(8,128)(2,1)}, u32[]{:S(2)}) %copy-start.1) | copy-done | bytes 4718616
  21.3 3.3 %collective-permute-done.7.refs_2_ = bf16[32,1536]{1,0:T(8,128)(2,1)S(1)} collective-permute-done((bf16[32,1536]{1,0:T(8,128)(2,1)S(1)}, bf16[32,1536]{1,0:T(8,128)(2,1)S(1)}, u32[]{:S(2)}, u32[]{:S(2)}) %collective-permute-start.7) | collective-permute-done | bytes 98336 | tf_op jit(solution)/shard_map/spread_vv/ppermute | solution.py:383
  25.2 2.1 %collective-permute-start.9 = (bf16[128,1536]{1,0:T(8,128)(2,1)S(1)}, bf16[128,1536]{1,0:T(8,128)(2,1)S(1)}, u32[]{:S(2)}, u32[]{:S(2)}) collective-permute-start(bf16[128,1536]{1,0:T(8,128)(2,1)S(1)} %chunk_vv.1.refs_0_), channel_id=1, source_target_pairs={{0,8},{4,12},{8,0},{12,4},{16,24},{20,28},{24,16},{28,20},{1,9},{5... | collective-permute-start | bytes 1179656 | tf_op jit(solution)/shard_map/ppermute | solution.py:377
  28.9 8.5 %collective-permute-done.9.refs_1_ = bf16[128,1536]{1,0:T(8,128)(2,1)S(1)} collective-permute-done((bf16[128,1536]{1,0:T(8,128)(2,1)S(1)}, bf16[128,1536]{1,0:T(8,128)(2,1)S(1)}, u32[]{:S(2)}, u32[]{:S(2)}) %collective-permute-start.9) | collective-permute-done | bytes 393248 | tf_op jit(solution)/shard_map/ppermute | solution.py:377
  37.4 3.5 %collective-permute-done.10.refs_2_ = bf16[128,1536]{1,0:T(8,128)(2,1)S(1)} collective-permute-done((bf16[128,1536]{1,0:T(8,128)(2,1)S(1)}, bf16[128,1536]{1,0:T(8,128)(2,1)S(1)}, u32[]{:S(2)}, u32[]{:S(2)}) %collective-permute-start.10) | collective-permute-done | bytes 393248 | tf_op jit(solution)/shard_map/ppermute | solution.py:377
  40.9 4.8 %inner.2 = (bf16[784,128]{1,0:T(8,128)(2,1)S(1)}, bf16[784,128]{1,0:T(8,128)(2,1)S(1)}, bf16[784,128]{1,0:T(8,128)(2,1)S(1)}, bf16[784,128]{1,0:T(8,128)(2,1)S(1...) custom-call(s32[3]{0:T(128)S(1)} %pad_add_fusion.where_ref, bf16[2,768,1536]{2,1,0:T(8,128)(2,1)S(1)} %fetch.3.w_own_ref, ...), custom_call_target="tpu_custom_call" | custom-call | flops 1 | bytes 1 | tf_op jit(solution)/shard_map/inner/pallas_call | solution.py:91
  45.8 2.4 %collective-permute-start.12 = (bf16[784,128]{1,0:T(8,128)(2,1)S(1)}, bf16[784,128]{1,0:T(8,128)(2,1)S(1)}, u32[]{:S(2)}, u32[]{:S(2)}) collective-permute-start(bf16[784,128]{1,0:T(8,128)(2,1)S(1)} %get-tuple-element.68), channel_id=1, source_target_pairs={{0,16},{4,20},{8,24},{12,28},{16,0},{20,4},{24,8},{28,12},{1,17},{... | collective-permute-start | bytes 602120 | tf_op jit(solution)/shard_map/ppermute | solution.py:377
  48.2 3.9 %inner.3 = (bf16[784,128]{1,0:T(8,128)(2,1)S(1)}, bf16[784,128]{1,0:T(8,128)(2,1)S(1)}) custom-call(s32[3]{0:T(128)S(1)} %pad_add_fusion.where_ref, bf16[2,768,1536]{2,1,0:T(8,128)(2,1)S(1)} %fetch.3.w_own_ref, bf16[2,768,1536]{2,1,0:T(8,128)(2,1)S(1)} %collective-permute-done.2.w_twin_ref, bf16[128,1536]{1,0:T(8,128)(2,1)S(1)} %collective-permute-done.13.refs_0_), custom_call_target="tpu_custom_call" | custom-call | flops 1 | bytes 1 | tf_op jit(solution)/shard_map/inner/pallas_call | solution.py:91
  53.6 2.0 %collective-permute-start.24 = (bf16[784,128]{1,0:T(8,128)(2,1)S(1)}, bf16[784,128]{1,0:T(8,128)(2,1)S(1)}, u32[]{:S(2)}, u32[]{:S(2)}) collective-permute-start(bf16[784,128]{1,0:T(8,128)(2,1)S(1)} %get-tuple-element.81), channel_id=1, source_target_pairs={{0,16},{4,20},{8,24},{12,28},{16,0},{20,4},{24,8},{28,12},{1,17},{... | collective-permute-start | bytes 602120 | tf_op jit(solution)/shard_map/ppermute | solution.py:377
  56.7 2.2 %collective-permute-done.14.refs_3_ = bf16[784,128]{1,0:T(8,128)(2,1)S(1)} collective-permute-done((bf16[784,128]{1,0:T(8,128)(2,1)S(1)}, bf16[784,128]{1,0:T(8,128)(2,1)S(1)}, u32[]{:S(2)}, u32[]{:S(2)}) %collective-permute-start.14) | collective-permute-done | bytes 200736 | tf_op jit(solution)/shard_map/ppermute | solution.py:377
  59.5 3.7 %collective-permute-start.15 = (bf16[1568,128]{1,0:T(8,128)(2,1)S(1)}, bf16[1568,128]{1,0:T(8,128)(2,1)S(1)}, u32[]{:S(2)}, u32[]{:S(2)}) collective-permute-start(bf16[1568,128]{1,0:T(8,128)(2,1)S(1)} %get-tuple-element.72), channel_id=1, source_target_pairs={{0,1},{1,0},{2,3},{3,2},{4,5},{5,4},{6,7},{7,6},{8,9},{9,8},{10,11... | collective-permute-start | bytes 1204232 | tf_op jit(solution)/shard_map/ppermute | solution.py:383
  64.1 3.6 %collective-permute-start.26 = (bf16[1568,128]{1,0:T(8,128)(2,1)S(1)}, bf16[1568,128]{1,0:T(8,128)(2,1)S(1)}, u32[]{:S(2)}, u32[]{:S(2)}) collective-permute-start(bf16[1568,128]{1,0:T(8,128)(2,1)S(1)} %get-tuple-element.85), channel_id=1, source_target_pairs={{0,1},{1,0},{2,3},{3,2},{4,5},{5,4},{6,7},{7,6},{8,9},{9,8},{10,11... | collective-permute-start | bytes 1204232 | tf_op jit(solution)/shard_map/ppermute | solution.py:383
  67.7 5.4 %collective-permute-done.15.got_ref = bf16[1568,128]{1,0:T(8,128)(2,1)S(1)} collective-permute-done((bf16[1568,128]{1,0:T(8,128)(2,1)S(1)}, bf16[1568,128]{1,0:T(8,128)(2,1)S(1)}, u32[]{:S(2)}, u32[]{:S(2)}) %collective-permute-start.15) | collective-permute-done | bytes 401440 | tf_op jit(solution)/shard_map/ppermute | solution.py:383
  74.0 2.4 %collective-permute-start.16 = (bf16[784,128]{1,0:T(8,128)(2,1)S(1)}, bf16[784,128]{1,0:T(8,128)(2,1)S(1)}, u32[]{:S(2)}, u32[]{:S(2)}) collective-permute-start(bf16[784,128]{1,0:T(8,128)(2,1)S(1)} %get-tuple-element.74), channel_id=1, source_target_pairs={{0,2},{1,3},{2,0},{3,1},{4,6},{5,7},{6,4},{7,5},{8,10},{9,11},{10,... | collective-permute-start | bytes 602120 | tf_op jit(solution)/shard_map/ppermute | solution.py:383
  76.4 5.2 %collective-permute-done.26.got_ref = bf16[1568,128]{1,0:T(8,128)(2,1)S(1)} collective-permute-done((bf16[1568,128]{1,0:T(8,128)(2,1)S(1)}, bf16[1568,128]{1,0:T(8,128)(2,1)S(1)}, u32[]{:S(2)}, u32[]{:S(2)}) %collective-permute-start.26) | collective-permute-done | bytes 401440 | tf_op jit(solution)/shard_map/ppermute | solution.py:383
  84.2 1.5 %collective-permute-start.18 = (bf16[784,128]{1,0:T(8,128)(2,1)S(1)}, bf16[784,128]{1,0:T(8,128)(2,1)S(1)}, u32[]{:S(2)}, u32[]{:S(2)}) collective-permute-start(bf16[784,128]{1,0:T(8,128)(2,1)S(1)} %sum_inner.2.refs_0_), channel_id=1, source_target_pairs={{0,16},{4,20},{8,24},{12,28},{16,0},{20,4},{24,8},{28,12},{1,17},{... | collective-permute-start | bytes 602120 | tf_op jit(solution)/shard_map/ppermute | solution.py:377
  85.7 2.0 %collective-permute-start.19 = (bf16[784,128]{1,0:T(8,128)(2,1)S(1)}, bf16[784,128]{1,0:T(8,128)(2,1)S(1)}, u32[]{:S(2)}, u32[]{:S(2)}) collective-permute-start(bf16[784,128]{1,0:T(8,128)(2,1)S(1)} %sum_inner.2.refs_0_), channel_id=1, source_target_pairs={{0,24},{4,28},{8,16},{12,20},{16,8},{20,12},{24,0},{28,4},{1,25},{... | collective-permute-start | bytes 602120 | tf_op jit(solution)/shard_map/ppermute | solution.py:377
  87.7 2.8 %collective-permute-done.27.got_ref = bf16[784,128]{1,0:T(8,128)(2,1)S(1)} collective-permute-done((bf16[784,128]{1,0:T(8,128)(2,1)S(1)}, bf16[784,128]{1,0:T(8,128)(2,1)S(1)}, u32[]{:S(2)}, u32[]{:S(2)}) %collective-permute-start.27) | collective-permute-done | bytes 200736 | tf_op jit(solution)/shard_map/ppermute | solution.py:383
  91.5 1.8 %collective-permute-start.29 = (bf16[784,128]{1,0:T(8,128)(2,1)S(1)}, bf16[784,128]{1,0:T(8,128)(2,1)S(1)}, u32[]{:S(2)}, u32[]{:S(2)}) collective-permute-start(bf16[784,128]{1,0:T(8,128)(2,1)S(1)} %sum_inner.3.refs_0_), channel_id=1, source_target_pairs={{0,16},{4,20},{8,24},{12,28},{16,0},{20,4},{24,8},{28,12},{1,17},{... | collective-permute-start | bytes 602120 | tf_op jit(solution)/shard_map/ppermute | solution.py:377
  93.3 1.5 %collective-permute-start.30 = (bf16[784,128]{1,0:T(8,128)(2,1)S(1)}, bf16[784,128]{1,0:T(8,128)(2,1)S(1)}, u32[]{:S(2)}, u32[]{:S(2)}) collective-permute-start(bf16[784,128]{1,0:T(8,128)(2,1)S(1)} %sum_inner.3.refs_0_), channel_id=1, source_target_pairs={{0,24},{4,28},{8,16},{12,20},{16,8},{20,12},{24,0},{28,4},{1,25},{... | collective-permute-start | bytes 602120 | tf_op jit(solution)/shard_map/ppermute | solution.py:377
  94.8 2.9 %outer.2 = (f32[256,128]{1,0:T(8,128)S(1)}, bf16[272,128]{1,0:T(8,128)(2,1)S(1)}, bf16[272,128]{1,0:T(8,128)(2,1)S(1)}, bf16[272,128]{1,0:T(8,128)(2,1)S(1)}) custom-call(s32[3]{0:T(128)S(1)} %pad_add_fusion.where_ref, bf16[2,256,1536]{2,1,0:T(8,128)(2,1)S(1)} %copy-done, bf16[2,256,1536]{2,1,0:T(8,128)(2,1)S(1)} %collective-permute-done.1.a_twin_ref, ...), custom_call_target="tpu_custom_call" | custom-call | flops 1 | bytes 1 | tf_op jit(solution)/shard_map/outer/pallas_call | solution.py:91
  99.9 2.9 %outer.3 = (f32[256,128]{1,0:T(8,128)S(1)}, f32[256,128]{1,0:T(8,128)S(1)}, bf16[544,128]{1,0:T(8,128)(2,1)S(1)}) custom-call(s32[3]{0:T(128)S(1)} %pad_add_fusion.where_ref, bf16[2,256,1536]{2,1,0:T(8,128)(2,1)S(1)} %copy-done, bf16[2,256,1536]{2,1,0:T(8,128)(2,1)S(1)} %collective-permute-done.1.a_twin_ref, bf16[784,128]{1,0:T(8,128)(2,1)S(1)} %sum_inner.3.refs_0_, ...), custom_call_target="tpu_custom_call" | custom-call | flops 1 | bytes 1 | tf_op jit(solution)/shard_map/outer/pallas_call | solution.py:91
  102.9 2.5 %collective-permute-start.20 = (bf16[272,128]{1,0:T(8,128)(2,1)S(1)}, bf16[272,128]{1,0:T(8,128)(2,1)S(1)}, u32[]{:S(2)}, u32[]{:S(2)}) collective-permute-start(bf16[272,128]{1,0:T(8,128)(2,1)S(1)} %get-tuple-element.76), channel_id=1, source_target_pairs={{0,1},{1,0},{2,3},{3,2},{4,5},{5,4},{6,7},{7,6},{8,9},{9,8},{10,11... | collective-permute-start | bytes 208904 | tf_op jit(solution)/shard_map/ppermute | solution.py:383
  105.8 1.9 %collective-permute-start.22 = (bf16[272,128]{1,0:T(8,128)(2,1)S(1)}, bf16[272,128]{1,0:T(8,128)(2,1)S(1)}, u32[]{:S(2)}, u32[]{:S(2)}) collective-permute-start(bf16[272,128]{1,0:T(8,128)(2,1)S(1)} %get-tuple-element.78), channel_id=1, source_target_pairs={{0,3},{1,2},{2,1},{3,0},{4,7},{5,6},{6,5},{7,4},{8,11},{9,10},{10,... | collective-permute-start | bytes 208904 | tf_op jit(solution)/shard_map/ppermute | solution.py:383
  107.8 1.6 %collective-permute-done.31.got_ref = bf16[544,128]{1,0:T(8,128)(2,1)S(1)} collective-permute-done((bf16[544,128]{1,0:T(8,128)(2,1)S(1)}, bf16[544,128]{1,0:T(8,128)(2,1)S(1)}, u32[]{:S(2)}, u32[]{:S(2)}) %collective-permute-start.31) | collective-permute-done | bytes 139296 | tf_op jit(solution)/shard_map/ppermute | solution.py:383
  112.0 2.4 %collective-permute-done.32.refs_5_ = bf16[272,128]{1,0:T(8,128)(2,1)S(1)} collective-permute-done((bf16[272,128]{1,0:T(8,128)(2,1)S(1)}, bf16[272,128]{1,0:T(8,128)(2,1)S(1)}, u32[]{:S(2)}, u32[]{:S(2)}) %collective-permute-start.32) | collective-permute-done | bytes 69664 | tf_op jit(solution)/shard_map/ppermute | solution.py:383
  (61 shorter events, 25.6 us)
Async XLA Ops:
  2.9 21.7 %collective-permute-start.2 = (bf16[2,768,1536]{2,1,0:T(8,128)(2,1)}, bf16[2,768,1536]{2,1,0:T(8,128)(2,1)S(1)}, u32[]{:S(2)}, u32[]{:S(2)}) collective-permute-start(bf16[2,768,1536]{2,1,0:T(8,128)(2,1)} %far_ref.2), channel_id=1, source_target_pairs={{0,4},{4,0},{8,12},{12,8},{16,20},{20,16},{24,28},{28,24},{1,5},{5... | collective-permute-start | bytes 14155784 | tf_op jit(solution)/shard_map/spread_vv/ppermute | solution.py:380
  3.0 21.6 %collective-permute-start.1 = (bf16[2,256,1536]{2,1,0:T(8,128)(2,1)}, bf16[2,256,1536]{2,1,0:T(8,128)(2,1)S(1)}, u32[]{:S(2)}, u32[]{:S(2)}) collective-permute-start(bf16[2,256,1536]{2,1,0:T(8,128)(2,1)} %a_own_ref.3), channel_id=1, source_target_pairs={{0,4},{4,0},{8,12},{12,8},{16,20},{20,16},{24,28},{28,24},{1,5},{5... | collective-permute-start | bytes 4718600 | tf_op jit(solution)/shard_map/spread_vv/ppermute | solution.py:380
  3.4 6.0 %collective-permute-start.3 = (bf16[32,1536]{1,0:T(8,128)(2,1)S(1)}, bf16[32,1536]{1,0:T(8,128)(2,1)S(1)}, u32[]{:S(2)}, u32[]{:S(2)}) collective-permute-start(bf16[32,1536]{1,0:T(8,128)(2,1)S(1)} %get-tuple-element.53), channel_id=1, source_target_pairs={{0,8},{4,12},{8,0},{12,4},{16,24},{20,28},{24,16},{28,20},{1,9},{5... | collective-permute-start | bytes 294920 | tf_op jit(solution)/shard_map/spread_vv/ppermute | solution.py:377
  6.0 6.0 %collective-permute-start.4 = (bf16[32,1536]{1,0:T(8,128)(2,1)S(1)}, bf16[32,1536]{1,0:T(8,128)(2,1)S(1)}, u32[]{:S(2)}, u32[]{:S(2)}) collective-permute-start(bf16[32,1536]{1,0:T(8,128)(2,1)S(1)} %get-tuple-element.54), channel_id=1, source_target_pairs={{0,16},{4,20},{8,24},{12,28},{16,0},{20,4},{24,8},{28,12},{1,17},{... | collective-permute-start | bytes 294920 | tf_op jit(solution)/shard_map/spread_vv/ppermute | solution.py:377
  7.6 5.5 %collective-permute-start.5 = (bf16[32,1536]{1,0:T(8,128)(2,1)S(1)}, bf16[32,1536]{1,0:T(8,128)(2,1)S(1)}, u32[]{:S(2)}, u32[]{:S(2)}) collective-permute-start(bf16[32,1536]{1,0:T(8,128)(2,1)S(1)} %get-tuple-element.55), channel_id=1, source_target_pairs={{0,24},{4,28},{8,16},{12,20},{16,8},{20,12},{24,0},{28,4},{1,25},{... | collective-permute-start | bytes 294920 | tf_op jit(solution)/shard_map/spread_vv/ppermute | solution.py:377
  13.7 7.7 %collective-permute-start.6 = (bf16[32,1536]{1,0:T(8,128)(2,1)S(1)}, bf16[32,1536]{1,0:T(8,128)(2,1)S(1)}, u32[]{:S(2)}, u32[]{:S(2)}) collective-permute-start(bf16[32,1536]{1,0:T(8,128)(2,1)S(1)} %get-tuple-element.59), channel_id=1, source_target_pairs={{0,1},{1,0},{2,3},{3,2},{4,5},{5,4},{6,7},{7,6},{8,9},{9,8},{10,11... | collective-permute-start | bytes 294920 | tf_op jit(solution)/shard_map/spread_vv/ppermute | solution.py:383
  15.3 9.3 %collective-permute-start.7 = (bf16[32,1536]{1,0:T(8,128)(2,1)S(1)}, bf16[32,1536]{1,0:T(8,128)(2,1)S(1)}, u32[]{:S(2)}, u32[]{:S(2)}) collective-permute-start(bf16[32,1536]{1,0:T(8,128)(2,1)S(1)} %get-tuple-element.60), channel_id=1, source_target_pairs={{0,2},{1,3},{2,0},{3,1},{4,6},{5,7},{6,4},{7,5},{8,10},{9,11},{10,... | collective-permute-start | bytes 294920 | tf_op jit(solution)/shard_map/spread_vv/ppermute | solution.py:383
  17.9 6.7 %collective-permute-start.8 = (bf16[32,1536]{1,0:T(8,128)(2,1)S(1)}, bf16[32,1536]{1,0:T(8,128)(2,1)S(1)}, u32[]{:S(2)}, u32[]{:S(2)}) collective-permute-start(bf16[32,1536]{1,0:T(8,128)(2,1)S(1)} %get-tuple-element.61), channel_id=1, source_target_pairs={{0,3},{1,2},{2,1},{3,0},{4,7},{5,6},{6,5},{7,4},{8,11},{9,10},{10,... | collective-permute-start | bytes 294920 | tf_op jit(solution)/shard_map/spread_vv/ppermute | solution.py:383
  25.2 12.2 %collective-permute-start.9 = (bf16[128,1536]{1,0:T(8,128)(2,1)S(1)}, bf16[128,1536]{1,0:T(8,128)(2,1)S(1)}, u32[]{:S(2)}, u32[]{:S(2)}) collective-permute-start(bf16[128,1536]{1,0:T(8,128)(2,1)S(1)} %chunk_vv.1.refs_0_), channel_id=1, source_target_pairs={{0,8},{4,12},{8,0},{12,4},{16,24},{20,28},{24,16},{28,20},{1,9},{5... | collective-permute-start | bytes 1179656 | tf_op jit(solution)/shard_map/ppermute | solution.py:377
  27.3 13.6 %collective-permute-start.10 = (bf16[128,1536]{1,0:T(8,128)(2,1)S(1)}, bf16[128,1536]{1,0:T(8,128)(2,1)S(1)}, u32[]{:S(2)}, u32[]{:S(2)}) collective-permute-start(bf16[128,1536]{1,0:T(8,128)(2,1)S(1)} %chunk_vv.1.refs_0_), channel_id=1, source_target_pairs={{0,16},{4,20},{8,24},{12,28},{16,0},{20,4},{24,8},{28,12},{1,17},{... | collective-permute-start | bytes 1179656 | tf_op jit(solution)/shard_map/ppermute | solution.py:377
  27.9 20.3 %collective-permute-start.13 = (bf16[128,1536]{1,0:T(8,128)(2,1)S(1)}, bf16[128,1536]{1,0:T(8,128)(2,1)S(1)}, u32[]{:S(2)}, u32[]{:S(2)}) collective-permute-start(bf16[128,1536]{1,0:T(8,128)(2,1)S(1)} %chunk_vv.1.refs_0_), channel_id=1, source_target_pairs={{0,24},{4,28},{8,16},{12,20},{16,8},{20,12},{24,0},{28,4},{1,25},{... | collective-permute-start | bytes 1179656 | tf_op jit(solution)/shard_map/ppermute | solution.py:377
  45.7 9.9 %collective-permute-start.11 = (bf16[784,128]{1,0:T(8,128)(2,1)S(1)}, bf16[784,128]{1,0:T(8,128)(2,1)S(1)}, u32[]{:S(2)}, u32[]{:S(2)}) collective-permute-start(bf16[784,128]{1,0:T(8,128)(2,1)S(1)} %get-tuple-element.67), channel_id=1, source_target_pairs={{0,8},{4,12},{8,0},{12,4},{16,24},{20,28},{24,16},{28,20},{1,9},{5... | collective-permute-start | bytes 602120 | tf_op jit(solution)/shard_map/ppermute | solution.py:377
  45.8 10.9 %collective-permute-start.12 = (bf16[784,128]{1,0:T(8,128)(2,1)S(1)}, bf16[784,128]{1,0:T(8,128)(2,1)S(1)}, u32[]{:S(2)}, u32[]{:S(2)}) collective-permute-start(bf16[784,128]{1,0:T(8,128)(2,1)S(1)} %get-tuple-element.68), channel_id=1, source_target_pairs={{0,16},{4,20},{8,24},{12,28},{16,0},{20,4},{24,8},{28,12},{1,17},{... | collective-permute-start | bytes 602120 | tf_op jit(solution)/shard_map/ppermute | solution.py:377
  52.1 6.8 %collective-permute-start.14 = (bf16[784,128]{1,0:T(8,128)(2,1)S(1)}, bf16[784,128]{1,0:T(8,128)(2,1)S(1)}, u32[]{:S(2)}, u32[]{:S(2)}) collective-permute-start(bf16[784,128]{1,0:T(8,128)(2,1)S(1)} %get-tuple-element.69), channel_id=1, source_target_pairs={{0,24},{4,28},{8,16},{12,20},{16,8},{20,12},{24,0},{28,4},{1,25},{... | collective-permute-start | bytes 602120 | tf_op jit(solution)/shard_map/ppermute | solution.py:377
  53.2 10.1 %collective-permute-start.23 = (bf16[784,128]{1,0:T(8,128)(2,1)S(1)}, bf16[784,128]{1,0:T(8,128)(2,1)S(1)}, u32[]{:S(2)}, u32[]{:S(2)}) collective-permute-start(bf16[784,128]{1,0:T(8,128)(2,1)S(1)} %get-tuple-element.80), channel_id=1, source_target_pairs={{0,8},{4,12},{8,0},{12,4},{16,24},{20,28},{24,16},{28,20},{1,9},{5... | collective-permute-start | bytes 602120 | tf_op jit(solution)/shard_map/ppermute | solution.py:377
  53.6 9.7 %collective-permute-start.24 = (bf16[784,128]{1,0:T(8,128)(2,1)S(1)}, bf16[784,128]{1,0:T(8,128)(2,1)S(1)}, u32[]{:S(2)}, u32[]{:S(2)}) collective-permute-start(bf16[784,128]{1,0:T(8,128)(2,1)S(1)} %get-tuple-element.81), channel_id=1, source_target_pairs={{0,16},{4,20},{8,24},{12,28},{16,0},{20,4},{24,8},{28,12},{1,17},{... | collective-permute-start | bytes 602120 | tf_op jit(solution)/shard_map/ppermute | solution.py:377
  55.6 7.6 %collective-permute-start.25 = (bf16[784,128]{1,0:T(8,128)(2,1)S(1)}, bf16[784,128]{1,0:T(8,128)(2,1)S(1)}, u32[]{:S(2)}, u32[]{:S(2)}) collective-permute-start(bf16[784,128]{1,0:T(8,128)(2,1)S(1)} %get-tuple-element.82), channel_id=1, source_target_pairs={{0,24},{4,28},{8,16},{12,20},{16,8},{20,12},{24,0},{28,4},{1,25},{... | collective-permute-start | bytes 602120 | tf_op jit(solution)/shard_map/ppermute | solution.py:377
  59.5 13.5 %collective-permute-start.15 = (bf16[1568,128]{1,0:T(8,128)(2,1)S(1)}, bf16[1568,128]{1,0:T(8,128)(2,1)S(1)}, u32[]{:S(2)}, u32[]{:S(2)}) collective-permute-start(bf16[1568,128]{1,0:T(8,128)(2,1)S(1)} %get-tuple-element.72), channel_id=1, source_target_pairs={{0,1},{1,0},{2,3},{3,2},{4,5},{5,4},{6,7},{7,6},{8,9},{9,8},{10,11... | collective-permute-start | bytes 1204232 | tf_op jit(solution)/shard_map/ppermute | solution.py:383
  64.1 17.5 %collective-permute-start.26 = (bf16[1568,128]{1,0:T(8,128)(2,1)S(1)}, bf16[1568,128]{1,0:T(8,128)(2,1)S(1)}, u32[]{:S(2)}, u32[]{:S(2)}) collective-permute-start(bf16[1568,128]{1,0:T(8,128)(2,1)S(1)} %get-tuple-element.85), channel_id=1, source_target_pairs={{0,1},{1,0},{2,3},{3,2},{4,5},{5,4},{6,7},{7,6},{8,9},{9,8},{10,11... | collective-permute-start | bytes 1204232 | tf_op jit(solution)/shard_map/ppermute | solution.py:383
  74.0 9.3 %collective-permute-start.16 = (bf16[784,128]{1,0:T(8,128)(2,1)S(1)}, bf16[784,128]{1,0:T(8,128)(2,1)S(1)}, u32[]{:S(2)}, u32[]{:S(2)}) collective-permute-start(bf16[784,128]{1,0:T(8,128)(2,1)S(1)} %get-tuple-element.74), channel_id=1, source_target_pairs={{0,2},{1,3},{2,0},{3,1},{4,6},{5,7},{6,4},{7,5},{8,10},{9,11},{10,... | collective-permute-start | bytes 602120 | tf_op jit(solution)/shard_map/ppermute | solution.py:383
  82.5 7.9 %collective-permute-start.27 = (bf16[784,128]{1,0:T(8,128)(2,1)S(1)}, bf16[784,128]{1,0:T(8,128)(2,1)S(1)}, u32[]{:S(2)}, u32[]{:S(2)}) collective-permute-start(bf16[784,128]{1,0:T(8,128)(2,1)S(1)} %get-tuple-element.87), channel_id=1, source_target_pairs={{0,2},{1,3},{2,0},{3,1},{4,6},{5,7},{6,4},{7,5},{8,10},{9,11},{10,... | collective-permute-start | bytes 602120 | tf_op jit(solution)/shard_map/ppermute | solution.py:383
  84.1 9.2 %collective-permute-start.17 = (bf16[784,128]{1,0:T(8,128)(2,1)S(1)}, bf16[784,128]{1,0:T(8,128)(2,1)S(1)}, u32[]{:S(2)}, u32[]{:S(2)}) collective-permute-start(bf16[784,128]{1,0:T(8,128)(2,1)S(1)} %sum_inner.2.refs_0_), channel_id=1, source_target_pairs={{0,8},{4,12},{8,0},{12,4},{16,24},{20,28},{24,16},{28,20},{1,9},{5... | collective-permute-start | bytes 602120 | tf_op jit(solution)/shard_map/ppermute | solution.py:377
  84.2 10.6 %collective-permute-start.18 = (bf16[784,128]{1,0:T(8,128)(2,1)S(1)}, bf16[784,128]{1,0:T(8,128)(2,1)S(1)}, u32[]{:S(2)}, u32[]{:S(2)}) collective-permute-start(bf16[784,128]{1,0:T(8,128)(2,1)S(1)} %sum_inner.2.refs_0_), channel_id=1, source_target_pairs={{0,16},{4,20},{8,24},{12,28},{16,0},{20,4},{24,8},{28,12},{1,17},{... | collective-permute-start | bytes 602120 | tf_op jit(solution)/shard_map/ppermute | solution.py:377
  85.7 9.1 %collective-permute-start.19 = (bf16[784,128]{1,0:T(8,128)(2,1)S(1)}, bf16[784,128]{1,0:T(8,128)(2,1)S(1)}, u32[]{:S(2)}, u32[]{:S(2)}) collective-permute-start(bf16[784,128]{1,0:T(8,128)(2,1)S(1)} %sum_inner.2.refs_0_), channel_id=1, source_target_pairs={{0,24},{4,28},{8,16},{12,20},{16,8},{20,12},{24,0},{28,4},{1,25},{... | collective-permute-start | bytes 602120 | tf_op jit(solution)/shard_map/ppermute | solution.py:377
  91.3 6.5 %collective-permute-start.28 = (bf16[784,128]{1,0:T(8,128)(2,1)S(1)}, bf16[784,128]{1,0:T(8,128)(2,1)S(1)}, u32[]{:S(2)}, u32[]{:S(2)}) collective-permute-start(bf16[784,128]{1,0:T(8,128)(2,1)S(1)} %sum_inner.3.refs_0_), channel_id=1, source_target_pairs={{0,8},{4,12},{8,0},{12,4},{16,24},{20,28},{24,16},{28,20},{1,9},{5... | collective-permute-start | bytes 602120 | tf_op jit(solution)/shard_map/ppermute | solution.py:377
  91.5 7.3 %collective-permute-start.29 = (bf16[784,128]{1,0:T(8,128)(2,1)S(1)}, bf16[784,128]{1,0:T(8,128)(2,1)S(1)}, u32[]{:S(2)}, u32[]{:S(2)}) collective-permute-start(bf16[784,128]{1,0:T(8,128)(2,1)S(1)} %sum_inner.3.refs_0_), channel_id=1, source_target_pairs={{0,16},{4,20},{8,24},{12,28},{16,0},{20,4},{24,8},{28,12},{1,17},{... | collective-permute-start | bytes 602120 | tf_op jit(solution)/shard_map/ppermute | solution.py:377
  93.3 6.6 %collective-permute-start.30 = (bf16[784,128]{1,0:T(8,128)(2,1)S(1)}, bf16[784,128]{1,0:T(8,128)(2,1)S(1)}, u32[]{:S(2)}, u32[]{:S(2)}) collective-permute-start(bf16[784,128]{1,0:T(8,128)(2,1)S(1)} %sum_inner.3.refs_0_), channel_id=1, source_target_pairs={{0,24},{4,28},{8,16},{12,20},{16,8},{20,12},{24,0},{28,4},{1,25},{... | collective-permute-start | bytes 602120 | tf_op jit(solution)/shard_map/ppermute | solution.py:377
  102.8 6.5 %collective-permute-start.31 = (bf16[544,128]{1,0:T(8,128)(2,1)S(1)}, bf16[544,128]{1,0:T(8,128)(2,1)S(1)}, u32[]{:S(2)}, u32[]{:S(2)}) collective-permute-start(bf16[544,128]{1,0:T(8,128)(2,1)S(1)} %get-tuple-element.94), channel_id=1, source_target_pairs={{0,2},{1,3},{2,0},{3,1},{4,6},{5,7},{6,4},{7,5},{8,10},{9,11},{10,... | collective-permute-start | bytes 417800 | tf_op jit(solution)/shard_map/ppermute | solution.py:383
  102.9 7.3 %collective-permute-start.20 = (bf16[272,128]{1,0:T(8,128)(2,1)S(1)}, bf16[272,128]{1,0:T(8,128)(2,1)S(1)}, u32[]{:S(2)}, u32[]{:S(2)}) collective-permute-start(bf16[272,128]{1,0:T(8,128)(2,1)S(1)} %get-tuple-element.76), channel_id=1, source_target_pairs={{0,1},{1,0},{2,3},{3,2},{4,5},{5,4},{6,7},{7,6},{8,9},{9,8},{10,11... | collective-permute-start | bytes 208904 | tf_op jit(solution)/shard_map/ppermute | solution.py:383
  105.4 5.7 %collective-permute-start.21 = (bf16[272,128]{1,0:T(8,128)(2,1)S(1)}, bf16[272,128]{1,0:T(8,128)(2,1)S(1)}, u32[]{:S(2)}, u32[]{:S(2)}) collective-permute-start(bf16[272,128]{1,0:T(8,128)(2,1)S(1)} %get-tuple-element.77), channel_id=1, source_target_pairs={{0,2},{1,3},{2,0},{3,1},{4,6},{5,7},{6,4},{7,5},{8,10},{9,11},{10,... | collective-permute-start | bytes 208904 | tf_op jit(solution)/shard_map/ppermute | solution.py:383
  105.8 6.2 %collective-permute-start.22 = (bf16[272,128]{1,0:T(8,128)(2,1)S(1)}, bf16[272,128]{1,0:T(8,128)(2,1)S(1)}, u32[]{:S(2)}, u32[]{:S(2)}) collective-permute-start(bf16[272,128]{1,0:T(8,128)(2,1)S(1)} %get-tuple-element.78), channel_id=1, source_target_pairs={{0,3},{1,2},{2,1},{3,0},{4,7},{5,6},{6,5},{7,4},{8,11},{9,10},{10,... | collective-permute-start | bytes 208904 | tf_op jit(solution)/shard_map/ppermute | solution.py:383
  110.1 4.4 %collective-permute-start.32 = (bf16[272,128]{1,0:T(8,128)(2,1)S(1)}, bf16[272,128]{1,0:T(8,128)(2,1)S(1)}, u32[]{:S(2)}, u32[]{:S(2)}) collective-permute-start(bf16[272,128]{1,0:T(8,128)(2,1)S(1)} %get-tuple-element.96), channel_id=1, source_target_pairs={{0,1},{1,0},{2,3},{3,2},{4,5},{5,4},{6,7},{7,6},{8,9},{9,8},{10,11... | collective-permute-start | bytes 208904 | tf_op jit(solution)/shard_map/ppermute | solution.py:383
  (5 other events, 49.8 us)

commit v4 on v3

--- a/solution.py
+++ b/solution.py
@@ -12,10 +12,11 @@
 SPAN = 126.0
 CHUNKS = 2
 MERGE = True
+CHAIN = False
 BATCHES = ((0, 1, 2), (3,))
-ORDER = {"out_1": ["out_0"]}
+ORDER = {}
 FORWARD = {"p3_0": False, "p3_1": False, "q3_0": False, "q3_1": False}
-HALVE = {"q2_0": True, "q2_1": True, "o_0": False, "o_1": True}
+HALVE = {"q2_0": True, "q2_1": True}
 BF = jnp.bfloat16
 F32 = jnp.float32
 
@@ -80,6 +81,17 @@
 
 def put_head(ref, bound):
     ref[0:HEAD, :] = spread_head(bound)
+
+
+COSTS = {"inner": 4.0, "outer": 3.0, "sum_inner": 0.8, "fold_inner": 0.9, "deal_inner": 0.7, "fetch": 0.9, "turn": 1.4}
+SCALE = None
+
+
+def guess(name):
+    if SCALE is None:
+        return None
+    flops = int(COSTS.get(name, 0.6) * SCALE * 1.1e9)
+    return pl.CostEstimate(flops=flops, bytes_accessed=0, transcendentals=0)
 
 
 def call(body, outs, scratch, name, args, flops=0, far=0):
@@ -95,9 +107,7 @@
         out_specs=[pl.BlockSpec(memory_space=pltpu.VMEM)] * len(outs),
         scratch_shapes=scratch,
         compiler_params=pltpu.CompilerParams(vmem_limit_bytes=24 * 1024 * 1024),
-        cost_estimate=pl.CostEstimate(
-            flops=1, bytes_accessed=1, transcendentals=0
-        ),
+        cost_estimate=guess(name),
         name=name,
     )(*args)
 
@@ -263,11 +273,11 @@
         out[at : at + group, :] = code(t_ref[l], bound)
 
 
-def outer_body(parts, rows, plain, n_out, where_ref, a_own_ref, a_twin_ref, *refs):
-    ins, outs = refs[:parts], refs[parts : parts + n_out]
-    hi_ref, lo_ref = refs[parts + n_out :]
+def outer_body(parts, rows, n_early, where_ref, a_own_ref, a_twin_ref, *refs):
+    ins, early = refs[:parts], refs[parts : parts + n_early]
+    outs, t_ref = refs[parts + n_early : -1], refs[-1]
     core = where_ref[1]
-    n_l = hi_ref.shape[1] // LANES
+    n_l = t_ref.shape[1] // LANES
     group = (ins[0].shape[0] - HEAD) // n_l
     for i in range(parts):
         bound = head_of(ins[i])
@@ -276,14 +286,17 @@
             upper, lower = split_parts(decode(ins[i][at : at + group, :], bound))
             c, rest = divmod(l, n_l // 2)
             lane = pl.multiple_of(((core ^ c) * (n_l // 2) + rest) * LANES, LANES)
-            hi_ref[i * group : (i + 1) * group, pl.ds(lane, LANES)] = upper
-            lo_ref[i * group : (i + 1) * group, pl.ds(lane, LANES)] = lower
+            for at, half in ((i, upper), (parts + i, lower)):
+                t_ref[at * group : (at + 1) * group, pl.ds(lane, LANES)] = half
     n_p = a_own_ref.shape[1]
     tops = [jnp.zeros((8, LANES), F32) for _ in range(parts)]
     blocks = [[] for _ in range(parts)]
     for a_ref in (a_own_ref, a_twin_ref):
-        with_re = half_nt(hi_ref[...], a_ref[0]) + half_nt(lo_ref[...], a_ref[0])
-        with_im = half_nt(hi_ref[...], a_ref[1]) + half_nt(lo_ref[...], a_ref[1])
+        with_re = half_nt(t_ref[...], a_ref[0])
+        with_im = half_nt(t_ref[...], a_ref[1])
+        n_t = parts * group
+        with_re = with_re[:n_t] + with_re[n_t:]
+        with_im = with_im[:n_t] + with_im[n_t:]
         with_re = with_re.reshape(parts, parts, 2, rows, n_p)
         with_im = with_im.reshape(parts, parts, 2, rows, n_p)
         k_re = with_re[:, :, 0] + with_im[:, :, 1]
@@ -292,47 +305,40 @@
             both = jnp.stack([k_re[:, d], k_im[:, d]], axis=1).reshape(-1, n_p)
             for l in range(0, n_p, LANES):
                 block = both[:, l : l + LANES]
-                if d >= plain:
+                if d:
                     tops[d] = jnp.maximum(tops[d], fold_top(block))
                 blocks[d].append(block)
     for d in range(parts):
         n_r = blocks[d][0].shape[0]
-        if d < plain:
+        if d == 0:
             for l, block in enumerate(blocks[d]):
                 outs[d][l * n_r : (l + 1) * n_r, :] = block
             continue
         bound = bound_of(tops[d])
-        out = outs[min(d, len(outs) - 1)]
-        start = (d - min(d, len(outs) - 1)) * (HEAD + len(blocks[d]) * n_r)
+        out, start = outs[d], 0
+        if early:
+            start = early[d - 1].shape[0]
+            out[:start, :] = early[d - 1][...]
         out[start : start + HEAD, :] = spread_head(bound)
         for l, block in enumerate(blocks[d]):
             at = start + HEAD + l * n_r
             out[at : at + n_r, :] = code(block, bound)
 
 
-def halve_body(where_ref, own_ref, near_ref, got_ref, kept_ref, sent_ref):
-    n_r = own_ref.shape[0]
-    kept_ref[...] = own_ref[...] + decode(got_ref[HEAD : HEAD + n_r, :], head_of(got_ref))
-    start = HEAD + n_r
-    bound = got_ref[start : start + 1, :].astype(F32)
-    near = near_ref[...] + decode(got_ref[start + HEAD :, :], bound)
-    bound = bound_of(fold_top(near))
-    sent_ref[0:HEAD, :] = spread_head(bound)
-    sent_ref[HEAD:, :] = code(near, bound)
-
-
-def last_body(parts, counts, rows, where_ref, *refs):
-    ins, outs = list(refs[: sum(counts)]), refs[sum(counts) :]
+def last_body(parts, chunks, rows, where_ref, *refs):
+    own, others = refs[:chunks], refs[chunks : chunks + parts - 1]
+    outs = refs[chunks + parts - 1 :]
     t = where_ref[0]
-    sub = rows * len(counts)
+    sub = rows * chunks
     n_l = outs[0].shape[2] // LANES
-    for e, count in enumerate(counts):
-        mine, *others = [ins.pop(0) for _ in range(count)]
-        n_r = mine.shape[0] // (2 * n_l)
-        bounds = [head_of(x) for x in others]
+    size = others[0].shape[0] // chunks
+    for e in range(chunks):
+        n_r = own[e].shape[0] // (2 * n_l)
+        start = e * size
+        bounds = [x[start : start + 1, :].astype(F32) for x in others]
         for l in range(2 * n_l):
-            total = mine[l * n_r : (l + 1) * n_r, :]
-            at = HEAD + l * n_r
+            total = own[e][l * n_r : (l + 1) * n_r, :]
+            at = start + HEAD + l * n_r
             for x, bound in zip(others, bounds):
                 total = total + decode(x[at : at + n_r, :], bound)
             total = total.reshape(parts, 2, rows, LANES)
@@ -454,20 +460,15 @@
         body = functools.partial(sum_body, parts)
         return call(body, [coded], [summed], "sum_inner", [where, kept, got])[0]
 
-    def outer_of(arrays, halving):
+    def outer_of(arrays, early):
         n_r = 2 * n_p // LANES * group
-        whole = shape((n_r, LANES), F32)
-        if halving:
-            outs = [whole, whole, shape((2 * (HEAD + n_r), LANES), BF)]
-        else:
-            outs = [whole] + [term] * (parts - 1)
-        plain = 2 if halving else 1
+        sent = shape(((HEAD + n_r) * (2 if early else 1), LANES), BF)
         return call(
-            functools.partial(outer_body, parts, rows, plain, len(outs)),
-            outs,
-            [pltpu.VMEM((parts * group, n_k), BF)] * 2,
+            functools.partial(outer_body, parts, rows, len(early)),
+            [shape((n_r, LANES), F32)] + [sent] * (parts - 1),
+            [pltpu.VMEM((2 * parts * group, n_k), BF)],
             "outer",
-            [where, pair_cc, pair_cc_twin, *arrays],
+            [where, pair_cc, pair_cc_twin, *arrays, *early],
         )
 
     done = {}
@@ -500,7 +501,10 @@
         if e == 0:
             found = []
             for batch in BATCHES:
-                found += inner_of([groups[i] for i in batch])
+                picked = [groups[i] for i in batch]
+                if found and CHAIN:
+                    picked = after(picked, *found)
+                found += inner_of(picked)
             tell("inner", found)
         return done["inner"][e::chunks]
 
@@ -531,22 +535,8 @@
         return tell(f"q3_{e}", gathered_of(x, FORWARD[f"q3_{e}"]))
 
     def outer_step(e, arrays):
-        return tell(f"out_{e}", outer_of(step(f"out_{e}", arrays), HALVE[f"o_{e}"]))
-
-    def final_step(e, arrays):
-        arrays = step(f"o_{e}", arrays)
-        if not HALVE[f"o_{e}"]:
-            return tell(f"o_{e}", alongs(arrays))
-        kept, near, sent = arrays
-        kept, sent = call(
-            halve_body,
-            [shape(kept.shape, F32), term],
-            [],
-            "halve",
-            [where, *step(f"half_{e}", [kept, near, along(sent, 2)])],
-        )
-        done[f"half_{e}"] = [kept, sent]
-        return tell(f"o_{e}", [kept, along(sent, 1)])
+        early = done["out_0"][1:] if e else []
+        return tell(f"out_{e}", outer_of(step(f"out_{e}", arrays), early))
 
     state = [None] * chunks
     stages = (
@@ -557,9 +547,8 @@
         move_step,
         gather_step,
         outer_step,
-        final_step,
     )
-    names = ("p3", "in", "q1", "deal", "s1", "q3", "out", "o")
+    names = ("p3", "in", "q1", "deal", "s1", "q3", "out")
     pending = [0] * chunks
     while min(pending) < len(stages):
         moved = False
@@ -570,8 +559,6 @@
             needs = [f"{names[n]}_{e}"]
             if names[n] == "s1":
                 needs += [f"fold_{e}", f"s2_{e}", f"sum_{e}"]
-            if names[n] == "o":
-                needs += [f"half_{e}"]
             wanted = [o for name in needs for o in ORDER.get(name, ())]
             if any(o not in done and not o.endswith(f"_{e}") for o in wanted):
                 continue
@@ -579,11 +566,10 @@
             pending[e] += 1
             moved = True
         assert moved
-    finals = [x for e in range(chunks) for x in state[e]]
-    counts = tuple(len(x) for x in state)
+    finals = [x[0] for x in state] + alongs(state[-1])[1:]
     with jax.named_scope("sum_outer"):
         own, theirs = call(
-            functools.partial(last_body, parts, counts, rows),
+            functools.partial(last_body, parts, chunks, rows),
             [shape((2, half, n_p), F32)] * 2,
             [],
             "sum_outer",

time: 118 us -> 116 us (0.983)
    ppermute x12 -> x10, waiting for transfers between devices: 23.2 us -> 22.2 us  [along(): return lax.ppermute(x, 'col', [(a, a ^ d) for a in range(parts)])]
    pallas_call x18 -> x17, Pallas kernels: 25.5 us -> 24.6 us  [call(): pl.pallas_call(body, out_shape=outs, in_specs=specs, out_specs=[pl.BlockS...]
    ppermute x12 -> x10, starting transfers between devices: 19.2 us -> 18.8 us  [along(): return lax.ppermute(x, 'col', [(a, a ^ d) for a in range(parts)])]
  transfers between devices with their start and end apart: 34 -> 32, of which waited for: 18 -> 16; matrix products, arithmetic and copies ran while one was open for 0% -> 0% of each run, Pallas kernels for 16% -> 16%
where the time goes in v4:
time: 116 us
  waiting for transfers between devices  45.5 us (39%)
  starting transfers between devices  41.9 us (36%)
  Pallas kernels  24.6 us (21%)
  local copies, waits for them, and re-layouts  3.34 us (3%)
    pallas_call x17, Pallas kernels, call(): pl.pallas_call(body, out_shape=outs, in_specs=specs, out_specs=[pl.BlockS...  24.6 us
    ppermute x10, waiting for transfers between devices, along(): return lax.ppermute(x, 'col', [(a, a ^ d) for a in range(parts)])  22.2 us
    ppermute x18, starting transfers between devices, plane(): return lax.ppermute(x, 'row', pairs)  22 us
    ppermute x18, waiting for transfers between devices, plane(): return lax.ppermute(x, 'row', pairs)  22 us
    ppermute x10, starting transfers between devices, along(): return lax.ppermute(x, 'col', [(a, a ^ d) for a in range(parts)])  18.8 us
    unnamed x6, local copies, waits for them, and re-layouts  3.34 us
  transfers between devices with their start and end apart: 32, of which 16 were waited for; matrix products, arithmetic and copies ran while one was open for 0% of the time, Pallas kernels for 16%

profile of v4, /device:TPU:0, one launch (start us, length us, event | category | flops | bytes accessed | tf_op | source)
XLA Modules:
  0.0 115.6 jit_solution(7925444960901315956)
XLA Ops:
  3.4 2.6 %collective-permute-start.3 = (bf16[32,1536]{1,0:T(8,128)(2,1)S(1)}, bf16[32,1536]{1,0:T(8,128)(2,1)S(1)}, u32[]{:S(2)}, u32[]{:S(2)}) collective-permute-start(bf16[32,1536]{1,0:T(8,128)(2,1)S(1)} %get-tuple-element.48), channel_id=1, source_target_pairs={{0,8},{4,12},{8,0},{12,4},{16,24},{20,28},{24,16},{28,20},{1,9},{5... | collective-permute-start | bytes 294920 | tf_op jit(solution)/shard_map/spread_vv/ppermute | solution.py:383
  6.0 1.5 %collective-permute-start.4 = (bf16[32,1536]{1,0:T(8,128)(2,1)S(1)}, bf16[32,1536]{1,0:T(8,128)(2,1)S(1)}, u32[]{:S(2)}, u32[]{:S(2)}) collective-permute-start(bf16[32,1536]{1,0:T(8,128)(2,1)S(1)} %get-tuple-element.49), channel_id=1, source_target_pairs={{0,16},{4,20},{8,24},{12,28},{16,0},{20,4},{24,8},{28,12},{1,17},{... | collective-permute-start | bytes 294920 | tf_op jit(solution)/shard_map/spread_vv/ppermute | solution.py:383
  7.6 1.8 %collective-permute-done.3.refs_1_ = bf16[32,1536]{1,0:T(8,128)(2,1)S(1)} collective-permute-done((bf16[32,1536]{1,0:T(8,128)(2,1)S(1)}, bf16[32,1536]{1,0:T(8,128)(2,1)S(1)}, u32[]{:S(2)}, u32[]{:S(2)}) %collective-permute-start.3) | collective-permute-done | bytes 98336 | tf_op jit(solution)/shard_map/spread_vv/ppermute | solution.py:383
  9.4 2.6 %collective-permute-done.4.refs_2_ = bf16[32,1536]{1,0:T(8,128)(2,1)S(1)} collective-permute-done((bf16[32,1536]{1,0:T(8,128)(2,1)S(1)}, bf16[32,1536]{1,0:T(8,128)(2,1)S(1)}, u32[]{:S(2)}, u32[]{:S(2)}) %collective-permute-start.4) | collective-permute-done | bytes 98336 | tf_op jit(solution)/shard_map/spread_vv/ppermute | solution.py:383
  13.7 1.6 %collective-permute-start.6 = (bf16[32,1536]{1,0:T(8,128)(2,1)S(1)}, bf16[32,1536]{1,0:T(8,128)(2,1)S(1)}, u32[]{:S(2)}, u32[]{:S(2)}) collective-permute-start(bf16[32,1536]{1,0:T(8,128)(2,1)S(1)} %get-tuple-element.54), channel_id=1, source_target_pairs={{0,1},{1,0},{2,3},{3,2},{4,5},{5,4},{6,7},{7,6},{8,9},{9,8},{10,11... | collective-permute-start | bytes 294920 | tf_op jit(solution)/shard_map/spread_vv/ppermute | solution.py:389
  15.3 2.6 %collective-permute-start.7 = (bf16[32,1536]{1,0:T(8,128)(2,1)S(1)}, bf16[32,1536]{1,0:T(8,128)(2,1)S(1)}, u32[]{:S(2)}, u32[]{:S(2)}) collective-permute-start(bf16[32,1536]{1,0:T(8,128)(2,1)S(1)} %get-tuple-element.55), channel_id=1, source_target_pairs={{0,2},{1,3},{2,0},{3,1},{4,6},{5,7},{6,4},{7,5},{8,10},{9,11},{10,... | collective-permute-start | bytes 294920 | tf_op jit(solution)/shard_map/spread_vv/ppermute | solution.py:389
  18.1 2.3 %copy-done.1 = bf16[2,768,1536]{2,1,0:T(8,128)(2,1)S(1)} copy-done((bf16[2,768,1536]{2,1,0:T(8,128)(2,1)S(1)}, bf16[2,768,1536]{2,1,0:T(8,128)(2,1)}, u32[]{:S(2)}) %copy-start.1) | copy-done | bytes 4718616
  21.3 3.3 %collective-permute-done.7.refs_2_ = bf16[32,1536]{1,0:T(8,128)(2,1)S(1)} collective-permute-done((bf16[32,1536]{1,0:T(8,128)(2,1)S(1)}, bf16[32,1536]{1,0:T(8,128)(2,1)S(1)}, u32[]{:S(2)}, u32[]{:S(2)}) %collective-permute-start.7) | collective-permute-done | bytes 98336 | tf_op jit(solution)/shard_map/spread_vv/ppermute | solution.py:389
  25.2 2.1 %collective-permute-start.9 = (bf16[128,1536]{1,0:T(8,128)(2,1)S(1)}, bf16[128,1536]{1,0:T(8,128)(2,1)S(1)}, u32[]{:S(2)}, u32[]{:S(2)}) collective-permute-start(bf16[128,1536]{1,0:T(8,128)(2,1)S(1)} %chunk_vv.1.refs_0_), channel_id=1, source_target_pairs={{0,8},{4,12},{8,0},{12,4},{16,24},{20,28},{24,16},{28,20},{1,9},{5... | collective-permute-start | bytes 1179656 | tf_op jit(solution)/shard_map/ppermute | solution.py:383
  28.9 8.5 %collective-permute-done.9.refs_1_ = bf16[128,1536]{1,0:T(8,128)(2,1)S(1)} collective-permute-done((bf16[128,1536]{1,0:T(8,128)(2,1)S(1)}, bf16[128,1536]{1,0:T(8,128)(2,1)S(1)}, u32[]{:S(2)}, u32[]{:S(2)}) %collective-permute-start.9) | collective-permute-done | bytes 393248 | tf_op jit(solution)/shard_map/ppermute | solution.py:383
  37.4 3.5 %collective-permute-done.10.refs_2_ = bf16[128,1536]{1,0:T(8,128)(2,1)S(1)} collective-permute-done((bf16[128,1536]{1,0:T(8,128)(2,1)S(1)}, bf16[128,1536]{1,0:T(8,128)(2,1)S(1)}, u32[]{:S(2)}, u32[]{:S(2)}) %collective-permute-start.10) | collective-permute-done | bytes 393248 | tf_op jit(solution)/shard_map/ppermute | solution.py:383
  40.9 4.8 %inner.2 = (bf16[784,128]{1,0:T(8,128)(2,1)S(1)}, bf16[784,128]{1,0:T(8,128)(2,1)S(1)}, bf16[784,128]{1,0:T(8,128)(2,1)S(1)}, bf16[784,128]{1,0:T(8,128)(2,1)S(1...) custom-call(s32[3]{0:T(128)S(1)} %pad_add_fusion.where_ref, bf16[2,768,1536]{2,1,0:T(8,128)(2,1)S(1)} %fetch.3.w_own_ref, ...), custom_call_target="tpu_custom_call" | custom-call | tf_op jit(solution)/shard_map/inner/pallas_call | solution.py:103
  45.8 2.4 %collective-permute-start.12 = (bf16[784,128]{1,0:T(8,128)(2,1)S(1)}, bf16[784,128]{1,0:T(8,128)(2,1)S(1)}, u32[]{:S(2)}, u32[]{:S(2)}) collective-permute-start(bf16[784,128]{1,0:T(8,128)(2,1)S(1)} %get-tuple-element.63), channel_id=1, source_target_pairs={{0,16},{4,20},{8,24},{12,28},{16,0},{20,4},{24,8},{28,12},{1,17},{... | collective-permute-start | bytes 602120 | tf_op jit(solution)/shard_map/ppermute | solution.py:383
  48.2 3.9 %inner.3 = (bf16[784,128]{1,0:T(8,128)(2,1)S(1)}, bf16[784,128]{1,0:T(8,128)(2,1)S(1)}) custom-call(s32[3]{0:T(128)S(1)} %pad_add_fusion.where_ref, bf16[2,768,1536]{2,1,0:T(8,128)(2,1)S(1)} %fetch.3.w_own_ref, bf16[2,768,1536]{2,1,0:T(8,128)(2,1)S(1)} %collective-permute-done.2.w_twin_ref, bf16[128,1536]{1,0:T(8,128)(2,1)S(1)} %collective-permute-done.13.refs_0_), custom_call_target="tpu_custom_call" | custom-call | tf_op jit(solution)/shard_map/inner/pallas_call | solution.py:103
  53.6 2.0 %collective-permute-start.21 = (bf16[784,128]{1,0:T(8,128)(2,1)S(1)}, bf16[784,128]{1,0:T(8,128)(2,1)S(1)}, u32[]{:S(2)}, u32[]{:S(2)}) collective-permute-start(bf16[784,128]{1,0:T(8,128)(2,1)S(1)} %get-tuple-element.73), channel_id=1, source_target_pairs={{0,16},{4,20},{8,24},{12,28},{16,0},{20,4},{24,8},{28,12},{1,17},{... | collective-permute-start | bytes 602120 | tf_op jit(solution)/shard_map/ppermute | solution.py:383
  56.7 2.2 %collective-permute-done.14.refs_3_ = bf16[784,128]{1,0:T(8,128)(2,1)S(1)} collective-permute-done((bf16[784,128]{1,0:T(8,128)(2,1)S(1)}, bf16[784,128]{1,0:T(8,128)(2,1)S(1)}, u32[]{:S(2)}, u32[]{:S(2)}) %collective-permute-start.14) | collective-permute-done | bytes 200736 | tf_op jit(solution)/shard_map/ppermute | solution.py:383
  59.6 3.7 %collective-permute-start.15 = (bf16[1568,128]{1,0:T(8,128)(2,1)S(1)}, bf16[1568,128]{1,0:T(8,128)(2,1)S(1)}, u32[]{:S(2)}, u32[]{:S(2)}) collective-permute-start(bf16[1568,128]{1,0:T(8,128)(2,1)S(1)} %get-tuple-element.67), channel_id=1, source_target_pairs={{0,1},{1,0},{2,3},{3,2},{4,5},{5,4},{6,7},{7,6},{8,9},{9,8},{10,11... | collective-permute-start | bytes 1204232 | tf_op jit(solution)/shard_map/ppermute | solution.py:389
  63.9 3.6 %collective-permute-start.23 = (bf16[1568,128]{1,0:T(8,128)(2,1)S(1)}, bf16[1568,128]{1,0:T(8,128)(2,1)S(1)}, u32[]{:S(2)}, u32[]{:S(2)}) collective-permute-start(bf16[1568,128]{1,0:T(8,128)(2,1)S(1)} %get-tuple-element.77), channel_id=1, source_target_pairs={{0,1},{1,0},{2,3},{3,2},{4,5},{5,4},{6,7},{7,6},{8,9},{9,8},{10,11... | collective-permute-start | bytes 1204232 | tf_op jit(solution)/shard_map/ppermute | solution.py:389
  67.5 5.4 %collective-permute-done.15.got_ref = bf16[1568,128]{1,0:T(8,128)(2,1)S(1)} collective-permute-done((bf16[1568,128]{1,0:T(8,128)(2,1)S(1)}, bf16[1568,128]{1,0:T(8,128)(2,1)S(1)}, u32[]{:S(2)}, u32[]{:S(2)}) %collective-permute-start.15) | collective-permute-done | bytes 401440 | tf_op jit(solution)/shard_map/ppermute | solution.py:389
  73.8 2.5 %collective-permute-start.16 = (bf16[784,128]{1,0:T(8,128)(2,1)S(1)}, bf16[784,128]{1,0:T(8,128)(2,1)S(1)}, u32[]{:S(2)}, u32[]{:S(2)}) collective-permute-start(bf16[784,128]{1,0:T(8,128)(2,1)S(1)} %get-tuple-element.69), channel_id=1, source_target_pairs={{0,2},{1,3},{2,0},{3,1},{4,6},{5,7},{6,4},{7,5},{8,10},{9,11},{10,... | collective-permute-start | bytes 602120 | tf_op jit(solution)/shard_map/ppermute | solution.py:389
  76.4 5.1 %collective-permute-done.23.got_ref = bf16[1568,128]{1,0:T(8,128)(2,1)S(1)} collective-permute-done((bf16[1568,128]{1,0:T(8,128)(2,1)S(1)}, bf16[1568,128]{1,0:T(8,128)(2,1)S(1)}, u32[]{:S(2)}, u32[]{:S(2)}) %collective-permute-start.23) | collective-permute-done | bytes 401440 | tf_op jit(solution)/shard_map/ppermute | solution.py:389
  83.5 1.9 %collective-permute-start.18 = (bf16[784,128]{1,0:T(8,128)(2,1)S(1)}, bf16[784,128]{1,0:T(8,128)(2,1)S(1)}, u32[]{:S(2)}, u32[]{:S(2)}) collective-permute-start(bf16[784,128]{1,0:T(8,128)(2,1)S(1)} %sum_inner.2.refs_0_), channel_id=1, source_target_pairs={{0,16},{4,20},{8,24},{12,28},{16,0},{20,4},{24,8},{28,12},{1,17},{... | collective-permute-start | bytes 602120 | tf_op jit(solution)/shard_map/ppermute | solution.py:383
  85.4 1.5 %collective-permute-start.19 = (bf16[784,128]{1,0:T(8,128)(2,1)S(1)}, bf16[784,128]{1,0:T(8,128)(2,1)S(1)}, u32[]{:S(2)}, u32[]{:S(2)}) collective-permute-start(bf16[784,128]{1,0:T(8,128)(2,1)S(1)} %sum_inner.2.refs_0_), channel_id=1, source_target_pairs={{0,24},{4,28},{8,16},{12,20},{16,8},{20,12},{24,0},{28,4},{1,25},{... | collective-permute-start | bytes 602120 | tf_op jit(solution)/shard_map/ppermute | solution.py:383
  86.9 3.4 %collective-permute-done.24.got_ref = bf16[784,128]{1,0:T(8,128)(2,1)S(1)} collective-permute-done((bf16[784,128]{1,0:T(8,128)(2,1)S(1)}, bf16[784,128]{1,0:T(8,128)(2,1)S(1)}, u32[]{:S(2)}, u32[]{:S(2)}) %collective-permute-start.24) | collective-permute-done | bytes 200736 | tf_op jit(solution)/shard_map/ppermute | solution.py:389
  91.3 1.8 %collective-permute-start.26 = (bf16[784,128]{1,0:T(8,128)(2,1)S(1)}, bf16[784,128]{1,0:T(8,128)(2,1)S(1)}, u32[]{:S(2)}, u32[]{:S(2)}) collective-permute-start(bf16[784,128]{1,0:T(8,128)(2,1)S(1)} %sum_inner.3.refs_0_), channel_id=1, source_target_pairs={{0,16},{4,20},{8,24},{12,28},{16,0},{20,4},{24,8},{28,12},{1,17},{... | collective-permute-start | bytes 602120 | tf_op jit(solution)/shard_map/ppermute | solution.py:383
  93.1 1.5 %collective-permute-start.27 = (bf16[784,128]{1,0:T(8,128)(2,1)S(1)}, bf16[784,128]{1,0:T(8,128)(2,1)S(1)}, u32[]{:S(2)}, u32[]{:S(2)}) collective-permute-start(bf16[784,128]{1,0:T(8,128)(2,1)S(1)} %sum_inner.3.refs_0_), channel_id=1, source_target_pairs={{0,24},{4,28},{8,16},{12,20},{16,8},{20,12},{24,0},{28,4},{1,25},{... | collective-permute-start | bytes 602120 | tf_op jit(solution)/shard_map/ppermute | solution.py:383
  94.7 2.9 %outer.2 = (f32[256,128]{1,0:T(8,128)S(1)}, bf16[272,128]{1,0:T(8,128)(2,1)S(1)}, bf16[272,128]{1,0:T(8,128)(2,1)S(1)}, bf16[272,128]{1,0:T(8,128)(2,1)S(1)}) custom-call(s32[3]{0:T(128)S(1)} %pad_add_fusion.where_ref, bf16[2,256,1536]{2,1,0:T(8,128)(2,1)S(1)} %copy-done, bf16[2,256,1536]{2,1,0:T(8,128)(2,1)S(1)} %collective-permute-done.1.a_twin_ref, ...), custom_call_target="tpu_custom_call" | custom-call | tf_op jit(solution)/shard_map/outer/pallas_call | solution.py:103
  99.7 2.9 %outer.3 = (f32[256,128]{1,0:T(8,128)S(1)}, bf16[544,128]{1,0:T(8,128)(2,1)S(1)}, bf16[544,128]{1,0:T(8,128)(2,1)S(1)}, bf16[544,128]{1,0:T(8,128)(2,1)S(1)}) custom-call(s32[3]{0:T(128)S(1)} %pad_add_fusion.where_ref, bf16[2,256,1536]{2,1,0:T(8,128)(2,1)S(1)} %copy-done, bf16[2,256,1536]{2,1,0:T(8,128)(2,1)S(1)} %collective-permute-done.1.a_twin_ref, ...), custom_call_target="tpu_custom_call" | custom-call | tf_op jit(solution)/shard_map/outer/pallas_call | solution.py:103
  102.7 2.5 %collective-permute-start.29 = (bf16[544,128]{1,0:T(8,128)(2,1)S(1)}, bf16[544,128]{1,0:T(8,128)(2,1)S(1)}, u32[]{:S(2)}, u32[]{:S(2)}) collective-permute-start(bf16[544,128]{1,0:T(8,128)(2,1)S(1)} %get-tuple-element.85), channel_id=1, source_target_pairs={{0,2},{1,3},{2,0},{3,1},{4,6},{5,7},{6,4},{7,5},{8,10},{9,11},{10,... | collective-permute-start | bytes 417800 | tf_op jit(solution)/shard_map/ppermute | solution.py:389
  105.2 1.9 %collective-permute-start.30 = (bf16[544,128]{1,0:T(8,128)(2,1)S(1)}, bf16[544,128]{1,0:T(8,128)(2,1)S(1)}, u32[]{:S(2)}, u32[]{:S(2)}) collective-permute-start(bf16[544,128]{1,0:T(8,128)(2,1)S(1)} %get-tuple-element.86), channel_id=1, source_target_pairs={{0,3},{1,2},{2,1},{3,0},{4,7},{5,6},{6,5},{7,4},{8,11},{9,10},{10,... | collective-permute-start | bytes 417800 | tf_op jit(solution)/shard_map/ppermute | solution.py:389
  107.1 2.1 %collective-permute-done.28.refs_2_ = bf16[544,128]{1,0:T(8,128)(2,1)S(1)} collective-permute-done((bf16[544,128]{1,0:T(8,128)(2,1)S(1)}, bf16[544,128]{1,0:T(8,128)(2,1)S(1)}, u32[]{:S(2)}, u32[]{:S(2)}) %collective-permute-start.28) | collective-permute-done | bytes 139296 | tf_op jit(solution)/shard_map/ppermute | solution.py:389
  110.3 1.8 %collective-permute-done.30.refs_4_ = bf16[544,128]{1,0:T(8,128)(2,1)S(1)} collective-permute-done((bf16[544,128]{1,0:T(8,128)(2,1)S(1)}, bf16[544,128]{1,0:T(8,128)(2,1)S(1)}, u32[]{:S(2)}, u32[]{:S(2)}) %collective-permute-start.30) | collective-permute-done | bytes 139296 | tf_op jit(solution)/shard_map/ppermute | solution.py:389
  (56 shorter events, 22.8 us)
Async XLA Ops:
  0.0 2.3 %collective-permute-start = (bf16[2,128,768]{2,1,0:T(8,128)(2,1)}, bf16[2,128,768]{2,1,0:T(8,128)(2,1)S(1)}, u32[]{:S(2)}, u32[]{:S(2)}) collective-permute-start(bf16[2,128,768]{2,1,0:T(8,128)(2,1)} %far_ref.1), channel_id=1, source_target_pairs={{0,4},{4,0},{8,12},{12,8},{16,20},{20,16},{24,28},{28,24},{1,5},{5... | collective-permute-start | bytes 1179656 | tf_op jit(solution)/shard_map/spread_vv/ppermute | solution.py:386
  2.9 21.7 %collective-permute-start.2 = (bf16[2,768,1536]{2,1,0:T(8,128)(2,1)}, bf16[2,768,1536]{2,1,0:T(8,128)(2,1)S(1)}, u32[]{:S(2)}, u32[]{:S(2)}) collective-permute-start(bf16[2,768,1536]{2,1,0:T(8,128)(2,1)} %far_ref.2), channel_id=1, source_target_pairs={{0,4},{4,0},{8,12},{12,8},{16,20},{20,16},{24,28},{28,24},{1,5},{5... | collective-permute-start | bytes 14155784 | tf_op jit(solution)/shard_map/spread_vv/ppermute | solution.py:386
  3.0 21.6 %collective-permute-start.1 = (bf16[2,256,1536]{2,1,0:T(8,128)(2,1)}, bf16[2,256,1536]{2,1,0:T(8,128)(2,1)S(1)}, u32[]{:S(2)}, u32[]{:S(2)}) collective-permute-start(bf16[2,256,1536]{2,1,0:T(8,128)(2,1)} %a_own_ref.3), channel_id=1, source_target_pairs={{0,4},{4,0},{8,12},{12,8},{16,20},{20,16},{24,28},{28,24},{1,5},{5... | collective-permute-start | bytes 4718600 | tf_op jit(solution)/shard_map/spread_vv/ppermute | solution.py:386
  3.4 6.0 %collective-permute-start.3 = (bf16[32,1536]{1,0:T(8,128)(2,1)S(1)}, bf16[32,1536]{1,0:T(8,128)(2,1)S(1)}, u32[]{:S(2)}, u32[]{:S(2)}) collective-permute-start(bf16[32,1536]{1,0:T(8,128)(2,1)S(1)} %get-tuple-element.48), channel_id=1, source_target_pairs={{0,8},{4,12},{8,0},{12,4},{16,24},{20,28},{24,16},{28,20},{1,9},{5... | collective-permute-start | bytes 294920 | tf_op jit(solution)/shard_map/spread_vv/ppermute | solution.py:383
  6.0 6.0 %collective-permute-start.4 = (bf16[32,1536]{1,0:T(8,128)(2,1)S(1)}, bf16[32,1536]{1,0:T(8,128)(2,1)S(1)}, u32[]{:S(2)}, u32[]{:S(2)}) collective-permute-start(bf16[32,1536]{1,0:T(8,128)(2,1)S(1)} %get-tuple-element.49), channel_id=1, source_target_pairs={{0,16},{4,20},{8,24},{12,28},{16,0},{20,4},{24,8},{28,12},{1,17},{... | collective-permute-start | bytes 294920 | tf_op jit(solution)/shard_map/spread_vv/ppermute | solution.py:383
  7.6 5.5 %collective-permute-start.5 = (bf16[32,1536]{1,0:T(8,128)(2,1)S(1)}, bf16[32,1536]{1,0:T(8,128)(2,1)S(1)}, u32[]{:S(2)}, u32[]{:S(2)}) collective-permute-start(bf16[32,1536]{1,0:T(8,128)(2,1)S(1)} %get-tuple-element.50), channel_id=1, source_target_pairs={{0,24},{4,28},{8,16},{12,20},{16,8},{20,12},{24,0},{28,4},{1,25},{... | collective-permute-start | bytes 294920 | tf_op jit(solution)/shard_map/spread_vv/ppermute | solution.py:383
  13.7 7.7 %collective-permute-start.6 = (bf16[32,1536]{1,0:T(8,128)(2,1)S(1)}, bf16[32,1536]{1,0:T(8,128)(2,1)S(1)}, u32[]{:S(2)}, u32[]{:S(2)}) collective-permute-start(bf16[32,1536]{1,0:T(8,128)(2,1)S(1)} %get-tuple-element.54), channel_id=1, source_target_pairs={{0,1},{1,0},{2,3},{3,2},{4,5},{5,4},{6,7},{7,6},{8,9},{9,8},{10,11... | collective-permute-start | bytes 294920 | tf_op jit(solution)/shard_map/spread_vv/ppermute | solution.py:389
  15.3 9.3 %collective-permute-start.7 = (bf16[32,1536]{1,0:T(8,128)(2,1)S(1)}, bf16[32,1536]{1,0:T(8,128)(2,1)S(1)}, u32[]{:S(2)}, u32[]{:S(2)}) collective-permute-start(bf16[32,1536]{1,0:T(8,128)(2,1)S(1)} %get-tuple-element.55), channel_id=1, source_target_pairs={{0,2},{1,3},{2,0},{3,1},{4,6},{5,7},{6,4},{7,5},{8,10},{9,11},{10,... | collective-permute-start | bytes 294920 | tf_op jit(solution)/shard_map/spread_vv/ppermute | solution.py:389
  17.9 6.7 %collective-permute-start.8 = (bf16[32,1536]{1,0:T(8,128)(2,1)S(1)}, bf16[32,1536]{1,0:T(8,128)(2,1)S(1)}, u32[]{:S(2)}, u32[]{:S(2)}) collective-permute-start(bf16[32,1536]{1,0:T(8,128)(2,1)S(1)} %get-tuple-element.56), channel_id=1, source_target_pairs={{0,3},{1,2},{2,1},{3,0},{4,7},{5,6},{6,5},{7,4},{8,11},{9,10},{10,... | collective-permute-start | bytes 294920 | tf_op jit(solution)/shard_map/spread_vv/ppermute | solution.py:389
  25.2 12.2 %collective-permute-start.9 = (bf16[128,1536]{1,0:T(8,128)(2,1)S(1)}, bf16[128,1536]{1,0:T(8,128)(2,1)S(1)}, u32[]{:S(2)}, u32[]{:S(2)}) collective-permute-start(bf16[128,1536]{1,0:T(8,128)(2,1)S(1)} %chunk_vv.1.refs_0_), channel_id=1, source_target_pairs={{0,8},{4,12},{8,0},{12,4},{16,24},{20,28},{24,16},{28,20},{1,9},{5... | collective-permute-start | bytes 1179656 | tf_op jit(solution)/shard_map/ppermute | solution.py:383
  27.3 13.6 %collective-permute-start.10 = (bf16[128,1536]{1,0:T(8,128)(2,1)S(1)}, bf16[128,1536]{1,0:T(8,128)(2,1)S(1)}, u32[]{:S(2)}, u32[]{:S(2)}) collective-permute-start(bf16[128,1536]{1,0:T(8,128)(2,1)S(1)} %chunk_vv.1.refs_0_), channel_id=1, source_target_pairs={{0,16},{4,20},{8,24},{12,28},{16,0},{20,4},{24,8},{28,12},{1,17},{... | collective-permute-start | bytes 1179656 | tf_op jit(solution)/shard_map/ppermute | solution.py:383
  27.9 20.3 %collective-permute-start.13 = (bf16[128,1536]{1,0:T(8,128)(2,1)S(1)}, bf16[128,1536]{1,0:T(8,128)(2,1)S(1)}, u32[]{:S(2)}, u32[]{:S(2)}) collective-permute-start(bf16[128,1536]{1,0:T(8,128)(2,1)S(1)} %chunk_vv.1.refs_0_), channel_id=1, source_target_pairs={{0,24},{4,28},{8,16},{12,20},{16,8},{20,12},{24,0},{28,4},{1,25},{... | collective-permute-start | bytes 1179656 | tf_op jit(solution)/shard_map/ppermute | solution.py:383
  45.7 9.9 %collective-permute-start.11 = (bf16[784,128]{1,0:T(8,128)(2,1)S(1)}, bf16[784,128]{1,0:T(8,128)(2,1)S(1)}, u32[]{:S(2)}, u32[]{:S(2)}) collective-permute-start(bf16[784,128]{1,0:T(8,128)(2,1)S(1)} %get-tuple-element.62), channel_id=1, source_target_pairs={{0,8},{4,12},{8,0},{12,4},{16,24},{20,28},{24,16},{28,20},{1,9},{5... | collective-permute-start | bytes 602120 | tf_op jit(solution)/shard_map/ppermute | solution.py:383
  45.8 10.9 %collective-permute-start.12 = (bf16[784,128]{1,0:T(8,128)(2,1)S(1)}, bf16[784,128]{1,0:T(8,128)(2,1)S(1)}, u32[]{:S(2)}, u32[]{:S(2)}) collective-permute-start(bf16[784,128]{1,0:T(8,128)(2,1)S(1)} %get-tuple-element.63), channel_id=1, source_target_pairs={{0,16},{4,20},{8,24},{12,28},{16,0},{20,4},{24,8},{28,12},{1,17},{... | collective-permute-start | bytes 602120 | tf_op jit(solution)/shard_map/ppermute | solution.py:383
  52.1 6.8 %collective-permute-start.14 = (bf16[784,128]{1,0:T(8,128)(2,1)S(1)}, bf16[784,128]{1,0:T(8,128)(2,1)S(1)}, u32[]{:S(2)}, u32[]{:S(2)}) collective-permute-start(bf16[784,128]{1,0:T(8,128)(2,1)S(1)} %get-tuple-element.64), channel_id=1, source_target_pairs={{0,24},{4,28},{8,16},{12,20},{16,8},{20,12},{24,0},{28,4},{1,25},{... | collective-permute-start | bytes 602120 | tf_op jit(solution)/shard_map/ppermute | solution.py:383
  53.2 10.1 %collective-permute-start.20 = (bf16[784,128]{1,0:T(8,128)(2,1)S(1)}, bf16[784,128]{1,0:T(8,128)(2,1)S(1)}, u32[]{:S(2)}, u32[]{:S(2)}) collective-permute-start(bf16[784,128]{1,0:T(8,128)(2,1)S(1)} %get-tuple-element.72), channel_id=1, source_target_pairs={{0,8},{4,12},{8,0},{12,4},{16,24},{20,28},{24,16},{28,20},{1,9},{5... | collective-permute-start | bytes 602120 | tf_op jit(solution)/shard_map/ppermute | solution.py:383
  53.6 9.7 %collective-permute-start.21 = (bf16[784,128]{1,0:T(8,128)(2,1)S(1)}, bf16[784,128]{1,0:T(8,128)(2,1)S(1)}, u32[]{:S(2)}, u32[]{:S(2)}) collective-permute-start(bf16[784,128]{1,0:T(8,128)(2,1)S(1)} %get-tuple-element.73), channel_id=1, source_target_pairs={{0,16},{4,20},{8,24},{12,28},{16,0},{20,4},{24,8},{28,12},{1,17},{... | collective-permute-start | bytes 602120 | tf_op jit(solution)/shard_map/ppermute | solution.py:383
  55.6 7.6 %collective-permute-start.22 = (bf16[784,128]{1,0:T(8,128)(2,1)S(1)}, bf16[784,128]{1,0:T(8,128)(2,1)S(1)}, u32[]{:S(2)}, u32[]{:S(2)}) collective-permute-start(bf16[784,128]{1,0:T(8,128)(2,1)S(1)} %get-tuple-element.74), channel_id=1, source_target_pairs={{0,24},{4,28},{8,16},{12,20},{16,8},{20,12},{24,0},{28,4},{1,25},{... | collective-permute-start | bytes 602120 | tf_op jit(solution)/shard_map/ppermute | solution.py:383
  59.6 13.3 %collective-permute-start.15 = (bf16[1568,128]{1,0:T(8,128)(2,1)S(1)}, bf16[1568,128]{1,0:T(8,128)(2,1)S(1)}, u32[]{:S(2)}, u32[]{:S(2)}) collective-permute-start(bf16[1568,128]{1,0:T(8,128)(2,1)S(1)} %get-tuple-element.67), channel_id=1, source_target_pairs={{0,1},{1,0},{2,3},{3,2},{4,5},{5,4},{6,7},{7,6},{8,9},{9,8},{10,11... | collective-permute-start | bytes 1204232 | tf_op jit(solution)/shard_map/ppermute | solution.py:389
  63.9 17.6 %collective-permute-start.23 = (bf16[1568,128]{1,0:T(8,128)(2,1)S(1)}, bf16[1568,128]{1,0:T(8,128)(2,1)S(1)}, u32[]{:S(2)}, u32[]{:S(2)}) collective-permute-start(bf16[1568,128]{1,0:T(8,128)(2,1)S(1)} %get-tuple-element.77), channel_id=1, source_target_pairs={{0,1},{1,0},{2,3},{3,2},{4,5},{5,4},{6,7},{7,6},{8,9},{9,8},{10,11... | collective-permute-start | bytes 1204232 | tf_op jit(solution)/shard_map/ppermute | solution.py:389
  73.8 8.7 %collective-permute-start.16 = (bf16[784,128]{1,0:T(8,128)(2,1)S(1)}, bf16[784,128]{1,0:T(8,128)(2,1)S(1)}, u32[]{:S(2)}, u32[]{:S(2)}) collective-permute-start(bf16[784,128]{1,0:T(8,128)(2,1)S(1)} %get-tuple-element.69), channel_id=1, source_target_pairs={{0,2},{1,3},{2,0},{3,1},{4,6},{5,7},{6,4},{7,5},{8,10},{9,11},{10,... | collective-permute-start | bytes 602120 | tf_op jit(solution)/shard_map/ppermute | solution.py:389
  82.4 7.9 %collective-permute-start.24 = (bf16[784,128]{1,0:T(8,128)(2,1)S(1)}, bf16[784,128]{1,0:T(8,128)(2,1)S(1)}, u32[]{:S(2)}, u32[]{:S(2)}) collective-permute-start(bf16[784,128]{1,0:T(8,128)(2,1)S(1)} %get-tuple-element.79), channel_id=1, source_target_pairs={{0,2},{1,3},{2,0},{3,1},{4,6},{5,7},{6,4},{7,5},{8,10},{9,11},{10,... | collective-permute-start | bytes 602120 | tf_op jit(solution)/shard_map/ppermute | solution.py:389
  83.3 9.8 %collective-permute-start.17 = (bf16[784,128]{1,0:T(8,128)(2,1)S(1)}, bf16[784,128]{1,0:T(8,128)(2,1)S(1)}, u32[]{:S(2)}, u32[]{:S(2)}) collective-permute-start(bf16[784,128]{1,0:T(8,128)(2,1)S(1)} %sum_inner.2.refs_0_), channel_id=1, source_target_pairs={{0,8},{4,12},{8,0},{12,4},{16,24},{20,28},{24,16},{28,20},{1,9},{5... | collective-permute-start | bytes 602120 | tf_op jit(solution)/shard_map/ppermute | solution.py:383
  83.5 11.1 %collective-permute-start.18 = (bf16[784,128]{1,0:T(8,128)(2,1)S(1)}, bf16[784,128]{1,0:T(8,128)(2,1)S(1)}, u32[]{:S(2)}, u32[]{:S(2)}) collective-permute-start(bf16[784,128]{1,0:T(8,128)(2,1)S(1)} %sum_inner.2.refs_0_), channel_id=1, source_target_pairs={{0,16},{4,20},{8,24},{12,28},{16,0},{20,4},{24,8},{28,12},{1,17},{... | collective-permute-start | bytes 602120 | tf_op jit(solution)/shard_map/ppermute | solution.py:383
  85.4 9.3 %collective-permute-start.19 = (bf16[784,128]{1,0:T(8,128)(2,1)S(1)}, bf16[784,128]{1,0:T(8,128)(2,1)S(1)}, u32[]{:S(2)}, u32[]{:S(2)}) collective-permute-start(bf16[784,128]{1,0:T(8,128)(2,1)S(1)} %sum_inner.2.refs_0_), channel_id=1, source_target_pairs={{0,24},{4,28},{8,16},{12,20},{16,8},{20,12},{24,0},{28,4},{1,25},{... | collective-permute-start | bytes 602120 | tf_op jit(solution)/shard_map/ppermute | solution.py:383
  91.1 6.5 %collective-permute-start.25 = (bf16[784,128]{1,0:T(8,128)(2,1)S(1)}, bf16[784,128]{1,0:T(8,128)(2,1)S(1)}, u32[]{:S(2)}, u32[]{:S(2)}) collective-permute-start(bf16[784,128]{1,0:T(8,128)(2,1)S(1)} %sum_inner.3.refs_0_), channel_id=1, source_target_pairs={{0,8},{4,12},{8,0},{12,4},{16,24},{20,28},{24,16},{28,20},{1,9},{5... | collective-permute-start | bytes 602120 | tf_op jit(solution)/shard_map/ppermute | solution.py:383
  91.3 7.3 %collective-permute-start.26 = (bf16[784,128]{1,0:T(8,128)(2,1)S(1)}, bf16[784,128]{1,0:T(8,128)(2,1)S(1)}, u32[]{:S(2)}, u32[]{:S(2)}) collective-permute-start(bf16[784,128]{1,0:T(8,128)(2,1)S(1)} %sum_inner.3.refs_0_), channel_id=1, source_target_pairs={{0,16},{4,20},{8,24},{12,28},{16,0},{20,4},{24,8},{28,12},{1,17},{... | collective-permute-start | bytes 602120 | tf_op jit(solution)/shard_map/ppermute | solution.py:383
  93.1 6.6 %collective-permute-start.27 = (bf16[784,128]{1,0:T(8,128)(2,1)S(1)}, bf16[784,128]{1,0:T(8,128)(2,1)S(1)}, u32[]{:S(2)}, u32[]{:S(2)}) collective-permute-start(bf16[784,128]{1,0:T(8,128)(2,1)S(1)} %sum_inner.3.refs_0_), channel_id=1, source_target_pairs={{0,24},{4,28},{8,16},{12,20},{16,8},{20,12},{24,0},{28,4},{1,25},{... | collective-permute-start | bytes 602120 | tf_op jit(solution)/shard_map/ppermute | solution.py:383
  102.6 6.6 %collective-permute-start.28 = (bf16[544,128]{1,0:T(8,128)(2,1)S(1)}, bf16[544,128]{1,0:T(8,128)(2,1)S(1)}, u32[]{:S(2)}, u32[]{:S(2)}) collective-permute-start(bf16[544,128]{1,0:T(8,128)(2,1)S(1)} %get-tuple-element.84), channel_id=1, source_target_pairs={{0,1},{1,0},{2,3},{3,2},{4,5},{5,4},{6,7},{7,6},{8,9},{9,8},{10,11... | collective-permute-start | bytes 417800 | tf_op jit(solution)/shard_map/ppermute | solution.py:389
  102.7 7.6 %collective-permute-start.29 = (bf16[544,128]{1,0:T(8,128)(2,1)S(1)}, bf16[544,128]{1,0:T(8,128)(2,1)S(1)}, u32[]{:S(2)}, u32[]{:S(2)}) collective-permute-start(bf16[544,128]{1,0:T(8,128)(2,1)S(1)} %get-tuple-element.85), channel_id=1, source_target_pairs={{0,2},{1,3},{2,0},{3,1},{4,6},{5,7},{6,4},{7,5},{8,10},{9,11},{10,... | collective-permute-start | bytes 417800 | tf_op jit(solution)/shard_map/ppermute | solution.py:389
  105.2 6.9 %collective-permute-start.30 = (bf16[544,128]{1,0:T(8,128)(2,1)S(1)}, bf16[544,128]{1,0:T(8,128)(2,1)S(1)}, u32[]{:S(2)}, u32[]{:S(2)}) collective-permute-start(bf16[544,128]{1,0:T(8,128)(2,1)S(1)} %get-tuple-element.86), channel_id=1, source_target_pairs={{0,3},{1,2},{2,1},{3,0},{4,7},{5,6},{6,5},{7,4},{8,11},{9,10},{10,... | collective-permute-start | bytes 417800 | tf_op jit(solution)/shard_map/ppermute | solution.py:389
  112.8 1.4 %collective-permute-start.31 = (f32[2,64,256]{2,1,0:T(8,128)S(1)}, f32[2,64,256]{2,1,0:T(8,128)S(1)}, u32[]{:S(2)}, u32[]{:S(2)}) collective-permute-start(f32[2,64,256]{2,1,0:T(8,128)S(1)} %get-tuple-element.88), channel_id=1, source_target_pairs={{0,4},{4,0},{8,12},{12,8},{16,20},{20,16},{24,28},{28,24},{1,5},{5... | collective-permute-start | bytes 393224 | tf_op jit(solution)/shard_map/sum_outer/ppermute | solution.py:386
  (3 other events, 45.9 us)

commit v5 on v4

--- a/solution.py
+++ b/solution.py
@@ -9,14 +9,10 @@
 
 LANES = 128
 HEAD = 16
+VMEM_LIMIT = 24 * 1024 * 1024
 SPAN = 126.0
 CHUNKS = 2
-MERGE = True
-CHAIN = False
 BATCHES = ((0, 1, 2), (3,))
-ORDER = {}
-FORWARD = {"p3_0": False, "p3_1": False, "q3_0": False, "q3_1": False}
-HALVE = {"q2_0": True, "q2_1": True}
 BF = jnp.bfloat16
 F32 = jnp.float32
 
@@ -55,7 +51,7 @@
 
 def bound_of(top):
     top = jnp.max(top, axis=(0, 1), keepdims=True)
-    top = jnp.maximum(top, 1e-30) * (1.0 + 2.0**-7)
+    top = jnp.maximum(top, 2e-36) * (1.0 + 2.0**-7)
     return top.astype(BF).astype(F32)
 
 
@@ -83,18 +79,7 @@
     ref[0:HEAD, :] = spread_head(bound)
 
 
-COSTS = {"inner": 4.0, "outer": 3.0, "sum_inner": 0.8, "fold_inner": 0.9, "deal_inner": 0.7, "fetch": 0.9, "turn": 1.4}
-SCALE = None
-
-
-def guess(name):
-    if SCALE is None:
-        return None
-    flops = int(COSTS.get(name, 0.6) * SCALE * 1.1e9)
-    return pl.CostEstimate(flops=flops, bytes_accessed=0, transcendentals=0)
-
-
-def call(body, outs, scratch, name, args, flops=0, far=0):
+def call(body, outs, scratch, name, args, far=0):
     specs = (
         [pl.BlockSpec(memory_space=pltpu.SMEM)]
         + [pl.BlockSpec(memory_space=pltpu.HBM)] * far
@@ -106,8 +91,7 @@
         in_specs=specs,
         out_specs=[pl.BlockSpec(memory_space=pltpu.VMEM)] * len(outs),
         scratch_shapes=scratch,
-        compiler_params=pltpu.CompilerParams(vmem_limit_bytes=24 * 1024 * 1024),
-        cost_estimate=guess(name),
+        compiler_params=pltpu.CompilerParams(vmem_limit_bytes=VMEM_LIMIT),
         name=name,
     )(*args)
 
@@ -249,28 +233,6 @@
     for l in range(n_l):
         at = HEAD + l * group
         out_ref[at : at + group, :] = code(t_ref[l], bound)
-
-
-def add_body(parts, where_ref, *refs):
-    ins, out, t_ref = refs[:parts], refs[parts], refs[parts + 1]
-    n_l, group = t_ref.shape[0], t_ref.shape[1]
-    step = group // parts
-    top = jnp.zeros((8, LANES), F32)
-    bounds = [head_of(ins[d]) for d in range(parts)]
-    for l in range(n_l):
-        for s in range(parts):
-            total = None
-            for d in range(parts):
-                at = HEAD + l * group + (s ^ d) * step
-                term = decode(ins[d][at : at + step, :], bounds[d])
-                total = term if total is None else total + term
-            top = jnp.maximum(top, fold_top(total))
-            t_ref[l, s * step : (s + 1) * step, :] = total
-    bound = bound_of(top)
-    put_head(out, bound)
-    for l in range(n_l):
-        at = HEAD + l * group
-        out[at : at + group, :] = code(t_ref[l], bound)
 
 
 def outer_body(parts, rows, n_early, where_ref, a_own_ref, a_twin_ref, *refs):
@@ -419,11 +381,9 @@
         cut = alongs(route(planes(cut), "route_vv"))
         screened_own = fetch(late[0])
         cut = after(cut, screened_own, screened_twin, pair_cc_twin)
-        own = call(
+        (own,) = call(
             functools.partial(chunk_body, parts, chunks),
-            [shape((group * chunks, 2 * width), BF)]
-            if MERGE
-            else [shape((group, 2 * width), BF)] * chunks,
+            [shape((group * chunks, 2 * width), BF)],
             [],
             "chunk_vv",
             [where, *cut],
@@ -471,102 +431,23 @@
             [where, pair_cc, pair_cc_twin, *arrays, *early],
         )
 
-    done = {}
-
-    def step(name, arrays):
-        late = [a for other in ORDER.get(name, ()) for a in done[other]]
-        return after(arrays, *late) if late else tuple(arrays)
-
-    def tell(name, arrays):
-        done[name] = list(arrays)
-        return arrays
-
-    def gathered_of(x, forward):
-        if not forward:
-            return planes([x] * parts)
-        near = plane(x, 1)
-        return [x, near, plane(x, 2), plane(near, 2)]
-
-    def add(arrays):
-        body = functools.partial(add_body, parts)
-        return call(body, [coded], [summed], "add_inner", [where, *arrays])[0]
-
-    def gather_vv(e):
-        if MERGE and e:
-            return tell(f"p3_{e}", done["p3_0"])
-        (x,) = step(f"p3_{e}", [own[e]])
-        return tell(f"p3_{e}", gathered_of(x, FORWARD[f"p3_{e}"]))
-
-    def inner_step(e, groups):
-        if e == 0:
-            found = []
-            for batch in BATCHES:
-                picked = [groups[i] for i in batch]
-                if found and CHAIN:
-                    picked = after(picked, *found)
-                found += inner_of(picked)
-            tell("inner", found)
-        return done["inner"][e::chunks]
-
-    def spread_step(e, arrays):
-        mine, *sent = step(f"q1_{e}", arrays)
-        return tell(f"q1_{e}", planes([mine, *sent]))
-
-    def deal_step(e, arrays):
-        arrays = step(f"deal_{e}", arrays)
-        if HALVE[f"q2_{e}"]:
-            return tell(f"deal_{e}", deal(arrays))
-        return tell(f"deal_{e}", route(arrays, "route_inner"))
-
-    def move_step(e, arrays):
-        arrays = step(f"s1_{e}", arrays)
-        if not HALVE[f"q2_{e}"]:
-            got = tell(f"s1_{e}", alongs(arrays))
-            return tell(f"sum_{e}", [add(step(f"sum_{e}", got))])[0]
-        mine, far, sent = arrays
-        (got,) = tell(f"s1_{e}", [along(sent, 1)])
-        kept, sent = tell(f"fold_{e}", fold(*step(f"fold_{e}", [mine, far, got])))
-        (sent,) = step(f"s2_{e}", [sent])
-        (got,) = tell(f"s2_{e}", [along(sent, 2)])
-        return tell(f"sum_{e}", [sum_of(*step(f"sum_{e}", [kept, got]))])[0]
-
-    def gather_step(e, x):
-        (x,) = step(f"q3_{e}", [x])
-        return tell(f"q3_{e}", gathered_of(x, FORWARD[f"q3_{e}"]))
-
-    def outer_step(e, arrays):
-        early = done["out_0"][1:] if e else []
-        return tell(f"out_{e}", outer_of(step(f"out_{e}", arrays), early))
-
-    state = [None] * chunks
-    stages = (
-        lambda e, x: gather_vv(e),
-        inner_step,
-        spread_step,
-        deal_step,
-        move_step,
-        gather_step,
-        outer_step,
-    )
-    names = ("p3", "in", "q1", "deal", "s1", "q3", "out")
-    pending = [0] * chunks
-    while min(pending) < len(stages):
-        moved = False
-        for e in range(chunks):
-            n = pending[e]
-            if n == len(stages):
-                continue
-            needs = [f"{names[n]}_{e}"]
-            if names[n] == "s1":
-                needs += [f"fold_{e}", f"s2_{e}", f"sum_{e}"]
-            wanted = [o for name in needs for o in ORDER.get(name, ())]
-            if any(o not in done and not o.endswith(f"_{e}") for o in wanted):
-                continue
-            state[e] = stages[n](e, state[e])
-            pending[e] += 1
-            moved = True
-        assert moved
-    finals = [x[0] for x in state] + alongs(state[-1])[1:]
+    with jax.named_scope("inner"):
+        groups = planes([own] * parts)
+        inner = []
+        for batch in BATCHES:
+            inner += inner_of([groups[i] for i in batch])
+    totals = []
+    for e in range(chunks):
+        with jax.named_scope("move_inner"):
+            mine, far, sent = deal(planes(inner[e::chunks]))
+            kept, sent = fold(mine, far, along(sent, 1))
+            totals.append(sum_of(kept, along(sent, 2)))
+    finals, early = [], []
+    with jax.named_scope("outer"):
+        for total in totals:
+            kept, *early = outer_of(planes([total] * parts), early)
+            finals.append(kept)
+        finals += [along(x, d) for d, x in enumerate(early, 1)]
     with jax.named_scope("sum_outer"):
         own, theirs = call(
             functools.partial(last_body, parts, chunks, rows),

time: 116 us -> 116 us (level)
  no operation moved by 1% of the time
where the time goes in v5:
time: 116 us
  waiting for transfers between devices  45.5 us (39%)
  starting transfers between devices  41.9 us (36%)
  Pallas kernels  24.6 us (21%)
  local copies, waits for them, and re-layouts  3.34 us (3%)
    pallas_call x17, Pallas kernels, call(): pl.pallas_call(body, out_shape=outs, in_specs=specs, out_specs=[pl.BlockS...  24.6 us
    ppermute x10, waiting for transfers between devices, along(): return lax.ppermute(x, 'col', [(a, a ^ d) for a in range(parts)])  22.2 us
    ppermute x18, starting transfers between devices, plane(): return lax.ppermute(x, 'row', pairs)  22 us
    ppermute x18, waiting for transfers between devices, plane(): return lax.ppermute(x, 'row', pairs)  22 us
    ppermute x10, starting transfers between devices, along(): return lax.ppermute(x, 'col', [(a, a ^ d) for a in range(parts)])  18.8 us
    unnamed x6, local copies, waits for them, and re-layouts  3.34 us
  transfers between devices with their start and end apart: 32, of which 16 were waited for; matrix products, arithmetic and copies ran while one was open for 0% of the time, Pallas kernels for 16%

profile of v5, /device:TPU:0, one launch (start us, length us, event | category | flops | bytes accessed | tf_op | source)
XLA Modules:
  0.0 115.6 jit_solution(13473516610197667794)
XLA Ops:
  3.4 2.6 %collective-permute-start.3 = (bf16[32,1536]{1,0:T(8,128)(2,1)S(1)}, bf16[32,1536]{1,0:T(8,128)(2,1)S(1)}, u32[]{:S(2)}, u32[]{:S(2)}) collective-permute-start(bf16[32,1536]{1,0:T(8,128)(2,1)S(1)} %get-tuple-element.48), channel_id=1, source_target_pairs={{0,8},{4,12},{8,0},{12,4},{16,24},{20,28},{24,16},{28,20},{1,9},{5... | collective-permute-start | bytes 294920 | tf_op jit(solution)/shard_map/spread_vv/ppermute | solution.py:345
  6.0 1.5 %collective-permute-start.4 = (bf16[32,1536]{1,0:T(8,128)(2,1)S(1)}, bf16[32,1536]{1,0:T(8,128)(2,1)S(1)}, u32[]{:S(2)}, u32[]{:S(2)}) collective-permute-start(bf16[32,1536]{1,0:T(8,128)(2,1)S(1)} %get-tuple-element.49), channel_id=1, source_target_pairs={{0,16},{4,20},{8,24},{12,28},{16,0},{20,4},{24,8},{28,12},{1,17},{... | collective-permute-start | bytes 294920 | tf_op jit(solution)/shard_map/spread_vv/ppermute | solution.py:345
  7.6 1.8 %collective-permute-done.3.refs_1_ = bf16[32,1536]{1,0:T(8,128)(2,1)S(1)} collective-permute-done((bf16[32,1536]{1,0:T(8,128)(2,1)S(1)}, bf16[32,1536]{1,0:T(8,128)(2,1)S(1)}, u32[]{:S(2)}, u32[]{:S(2)}) %collective-permute-start.3) | collective-permute-done | bytes 98336 | tf_op jit(solution)/shard_map/spread_vv/ppermute | solution.py:345
  9.4 2.6 %collective-permute-done.4.refs_2_ = bf16[32,1536]{1,0:T(8,128)(2,1)S(1)} collective-permute-done((bf16[32,1536]{1,0:T(8,128)(2,1)S(1)}, bf16[32,1536]{1,0:T(8,128)(2,1)S(1)}, u32[]{:S(2)}, u32[]{:S(2)}) %collective-permute-start.4) | collective-permute-done | bytes 98336 | tf_op jit(solution)/shard_map/spread_vv/ppermute | solution.py:345
  13.7 1.6 %collective-permute-start.6 = (bf16[32,1536]{1,0:T(8,128)(2,1)S(1)}, bf16[32,1536]{1,0:T(8,128)(2,1)S(1)}, u32[]{:S(2)}, u32[]{:S(2)}) collective-permute-start(bf16[32,1536]{1,0:T(8,128)(2,1)S(1)} %get-tuple-element.54), channel_id=1, source_target_pairs={{0,1},{1,0},{2,3},{3,2},{4,5},{5,4},{6,7},{7,6},{8,9},{9,8},{10,11... | collective-permute-start | bytes 294920 | tf_op jit(solution)/shard_map/spread_vv/ppermute | solution.py:351
  15.3 2.6 %collective-permute-start.7 = (bf16[32,1536]{1,0:T(8,128)(2,1)S(1)}, bf16[32,1536]{1,0:T(8,128)(2,1)S(1)}, u32[]{:S(2)}, u32[]{:S(2)}) collective-permute-start(bf16[32,1536]{1,0:T(8,128)(2,1)S(1)} %get-tuple-element.55), channel_id=1, source_target_pairs={{0,2},{1,3},{2,0},{3,1},{4,6},{5,7},{6,4},{7,5},{8,10},{9,11},{10,... | collective-permute-start | bytes 294920 | tf_op jit(solution)/shard_map/spread_vv/ppermute | solution.py:351
  18.1 2.3 %copy-done.1 = bf16[2,768,1536]{2,1,0:T(8,128)(2,1)S(1)} copy-done((bf16[2,768,1536]{2,1,0:T(8,128)(2,1)S(1)}, bf16[2,768,1536]{2,1,0:T(8,128)(2,1)}, u32[]{:S(2)}) %copy-start.1) | copy-done | bytes 4718616
  21.3 3.3 %collective-permute-done.7.refs_2_ = bf16[32,1536]{1,0:T(8,128)(2,1)S(1)} collective-permute-done((bf16[32,1536]{1,0:T(8,128)(2,1)S(1)}, bf16[32,1536]{1,0:T(8,128)(2,1)S(1)}, u32[]{:S(2)}, u32[]{:S(2)}) %collective-permute-start.7) | collective-permute-done | bytes 98336 | tf_op jit(solution)/shard_map/spread_vv/ppermute | solution.py:351
  25.2 2.1 %collective-permute-start.9 = (bf16[128,1536]{1,0:T(8,128)(2,1)S(1)}, bf16[128,1536]{1,0:T(8,128)(2,1)S(1)}, u32[]{:S(2)}, u32[]{:S(2)}) collective-permute-start(bf16[128,1536]{1,0:T(8,128)(2,1)S(1)} %chunk_vv.1.refs_0_), channel_id=1, source_target_pairs={{0,8},{4,12},{8,0},{12,4},{16,24},{20,28},{24,16},{28,20},{1,9},{5... | collective-permute-start | bytes 1179656 | tf_op jit(solution)/shard_map/inner/ppermute | solution.py:345
  28.9 8.5 %collective-permute-done.9.refs_1_ = bf16[128,1536]{1,0:T(8,128)(2,1)S(1)} collective-permute-done((bf16[128,1536]{1,0:T(8,128)(2,1)S(1)}, bf16[128,1536]{1,0:T(8,128)(2,1)S(1)}, u32[]{:S(2)}, u32[]{:S(2)}) %collective-permute-start.9) | collective-permute-done | bytes 393248 | tf_op jit(solution)/shard_map/inner/ppermute | solution.py:345
  37.4 3.5 %collective-permute-done.10.refs_2_ = bf16[128,1536]{1,0:T(8,128)(2,1)S(1)} collective-permute-done((bf16[128,1536]{1,0:T(8,128)(2,1)S(1)}, bf16[128,1536]{1,0:T(8,128)(2,1)S(1)}, u32[]{:S(2)}, u32[]{:S(2)}) %collective-permute-start.10) | collective-permute-done | bytes 393248 | tf_op jit(solution)/shard_map/inner/ppermute | solution.py:345
  40.9 4.8 %inner.2 = (bf16[784,128]{1,0:T(8,128)(2,1)S(1)}, bf16[784,128]{1,0:T(8,128)(2,1)S(1)}, bf16[784,128]{1,0:T(8,128)(2,1)S(1)}, bf16[784,128]{1,0:T(8,128)(2,1)S(1...) custom-call(s32[3]{0:T(128)S(1)} %pad_add_fusion.where_ref, bf16[2,768,1536]{2,1,0:T(8,128)(2,1)S(1)} %fetch.3.w_own_ref, ...), custom_call_target="tpu_custom_call" | custom-call | tf_op jit(solution)/shard_map/inner/inner/pallas_call | solution.py:88
  45.8 2.4 %collective-permute-start.12 = (bf16[784,128]{1,0:T(8,128)(2,1)S(1)}, bf16[784,128]{1,0:T(8,128)(2,1)S(1)}, u32[]{:S(2)}, u32[]{:S(2)}) collective-permute-start(bf16[784,128]{1,0:T(8,128)(2,1)S(1)} %get-tuple-element.63), channel_id=1, source_target_pairs={{0,16},{4,20},{8,24},{12,28},{16,0},{20,4},{24,8},{28,12},{1,17},{... | collective-permute-start | bytes 602120 | tf_op jit(solution)/shard_map/move_inner/ppermute | solution.py:345
  48.2 3.9 %inner.3 = (bf16[784,128]{1,0:T(8,128)(2,1)S(1)}, bf16[784,128]{1,0:T(8,128)(2,1)S(1)}) custom-call(s32[3]{0:T(128)S(1)} %pad_add_fusion.where_ref, bf16[2,768,1536]{2,1,0:T(8,128)(2,1)S(1)} %fetch.3.w_own_ref, bf16[2,768,1536]{2,1,0:T(8,128)(2,1)S(1)} %collective-permute-done.2.w_twin_ref, bf16[128,1536]{1,0:T(8,128)(2,1)S(1)} %collective-permute-done.13.refs_0_), custom_call_target="tpu_custom_call" | custom-call | tf_op jit(solution)/shard_map/inner/inner/pallas_call | solution.py:88
  53.6 2.0 %collective-permute-start.21 = (bf16[784,128]{1,0:T(8,128)(2,1)S(1)}, bf16[784,128]{1,0:T(8,128)(2,1)S(1)}, u32[]{:S(2)}, u32[]{:S(2)}) collective-permute-start(bf16[784,128]{1,0:T(8,128)(2,1)S(1)} %get-tuple-element.73), channel_id=1, source_target_pairs={{0,16},{4,20},{8,24},{12,28},{16,0},{20,4},{24,8},{28,12},{1,17},{... | collective-permute-start | bytes 602120 | tf_op jit(solution)/shard_map/move_inner/ppermute | solution.py:345
  56.7 2.2 %collective-permute-done.14.refs_3_ = bf16[784,128]{1,0:T(8,128)(2,1)S(1)} collective-permute-done((bf16[784,128]{1,0:T(8,128)(2,1)S(1)}, bf16[784,128]{1,0:T(8,128)(2,1)S(1)}, u32[]{:S(2)}, u32[]{:S(2)}) %collective-permute-start.14) | collective-permute-done | bytes 200736 | tf_op jit(solution)/shard_map/move_inner/ppermute | solution.py:345
  59.6 3.7 %collective-permute-start.15 = (bf16[1568,128]{1,0:T(8,128)(2,1)S(1)}, bf16[1568,128]{1,0:T(8,128)(2,1)S(1)}, u32[]{:S(2)}, u32[]{:S(2)}) collective-permute-start(bf16[1568,128]{1,0:T(8,128)(2,1)S(1)} %get-tuple-element.67), channel_id=1, source_target_pairs={{0,1},{1,0},{2,3},{3,2},{4,5},{5,4},{6,7},{7,6},{8,9},{9,8},{10,11... | collective-permute-start | bytes 1204232 | tf_op jit(solution)/shard_map/move_inner/ppermute | solution.py:351
  63.9 3.6 %collective-permute-start.23 = (bf16[1568,128]{1,0:T(8,128)(2,1)S(1)}, bf16[1568,128]{1,0:T(8,128)(2,1)S(1)}, u32[]{:S(2)}, u32[]{:S(2)}) collective-permute-start(bf16[1568,128]{1,0:T(8,128)(2,1)S(1)} %get-tuple-element.77), channel_id=1, source_target_pairs={{0,1},{1,0},{2,3},{3,2},{4,5},{5,4},{6,7},{7,6},{8,9},{9,8},{10,11... | collective-permute-start | bytes 1204232 | tf_op jit(solution)/shard_map/move_inner/ppermute | solution.py:351
  67.5 5.4 %collective-permute-done.15.got_ref = bf16[1568,128]{1,0:T(8,128)(2,1)S(1)} collective-permute-done((bf16[1568,128]{1,0:T(8,128)(2,1)S(1)}, bf16[1568,128]{1,0:T(8,128)(2,1)S(1)}, u32[]{:S(2)}, u32[]{:S(2)}) %collective-permute-start.15) | collective-permute-done | bytes 401440 | tf_op jit(solution)/shard_map/move_inner/ppermute | solution.py:351
  73.8 2.5 %collective-permute-start.16 = (bf16[784,128]{1,0:T(8,128)(2,1)S(1)}, bf16[784,128]{1,0:T(8,128)(2,1)S(1)}, u32[]{:S(2)}, u32[]{:S(2)}) collective-permute-start(bf16[784,128]{1,0:T(8,128)(2,1)S(1)} %get-tuple-element.69), channel_id=1, source_target_pairs={{0,2},{1,3},{2,0},{3,1},{4,6},{5,7},{6,4},{7,5},{8,10},{9,11},{10,... | collective-permute-start | bytes 602120 | tf_op jit(solution)/shard_map/move_inner/ppermute | solution.py:351
  76.4 5.1 %collective-permute-done.23.got_ref = bf16[1568,128]{1,0:T(8,128)(2,1)S(1)} collective-permute-done((bf16[1568,128]{1,0:T(8,128)(2,1)S(1)}, bf16[1568,128]{1,0:T(8,128)(2,1)S(1)}, u32[]{:S(2)}, u32[]{:S(2)}) %collective-permute-start.23) | collective-permute-done | bytes 401440 | tf_op jit(solution)/shard_map/move_inner/ppermute | solution.py:351
  83.5 1.9 %collective-permute-start.18 = (bf16[784,128]{1,0:T(8,128)(2,1)S(1)}, bf16[784,128]{1,0:T(8,128)(2,1)S(1)}, u32[]{:S(2)}, u32[]{:S(2)}) collective-permute-start(bf16[784,128]{1,0:T(8,128)(2,1)S(1)} %sum_inner.2.refs_0_), channel_id=1, source_target_pairs={{0,16},{4,20},{8,24},{12,28},{16,0},{20,4},{24,8},{28,12},{1,17},{... | collective-permute-start | bytes 602120 | tf_op jit(solution)/shard_map/outer/ppermute | solution.py:345
  85.4 1.5 %collective-permute-start.19 = (bf16[784,128]{1,0:T(8,128)(2,1)S(1)}, bf16[784,128]{1,0:T(8,128)(2,1)S(1)}, u32[]{:S(2)}, u32[]{:S(2)}) collective-permute-start(bf16[784,128]{1,0:T(8,128)(2,1)S(1)} %sum_inner.2.refs_0_), channel_id=1, source_target_pairs={{0,24},{4,28},{8,16},{12,20},{16,8},{20,12},{24,0},{28,4},{1,25},{... | collective-permute-start | bytes 602120 | tf_op jit(solution)/shard_map/outer/ppermute | solution.py:345
  86.9 3.4 %collective-permute-done.24.got_ref = bf16[784,128]{1,0:T(8,128)(2,1)S(1)} collective-permute-done((bf16[784,128]{1,0:T(8,128)(2,1)S(1)}, bf16[784,128]{1,0:T(8,128)(2,1)S(1)}, u32[]{:S(2)}, u32[]{:S(2)}) %collective-permute-start.24) | collective-permute-done | bytes 200736 | tf_op jit(solution)/shard_map/move_inner/ppermute | solution.py:351
  91.3 1.8 %collective-permute-start.26 = (bf16[784,128]{1,0:T(8,128)(2,1)S(1)}, bf16[784,128]{1,0:T(8,128)(2,1)S(1)}, u32[]{:S(2)}, u32[]{:S(2)}) collective-permute-start(bf16[784,128]{1,0:T(8,128)(2,1)S(1)} %sum_inner.3.refs_0_), channel_id=1, source_target_pairs={{0,16},{4,20},{8,24},{12,28},{16,0},{20,4},{24,8},{28,12},{1,17},{... | collective-permute-start | bytes 602120 | tf_op jit(solution)/shard_map/outer/ppermute | solution.py:345
  93.1 1.5 %collective-permute-start.27 = (bf16[784,128]{1,0:T(8,128)(2,1)S(1)}, bf16[784,128]{1,0:T(8,128)(2,1)S(1)}, u32[]{:S(2)}, u32[]{:S(2)}) collective-permute-start(bf16[784,128]{1,0:T(8,128)(2,1)S(1)} %sum_inner.3.refs_0_), channel_id=1, source_target_pairs={{0,24},{4,28},{8,16},{12,20},{16,8},{20,12},{24,0},{28,4},{1,25},{... | collective-permute-start | bytes 602120 | tf_op jit(solution)/shard_map/outer/ppermute | solution.py:345
  94.7 2.9 %outer.2 = (f32[256,128]{1,0:T(8,128)S(1)}, bf16[272,128]{1,0:T(8,128)(2,1)S(1)}, bf16[272,128]{1,0:T(8,128)(2,1)S(1)}, bf16[272,128]{1,0:T(8,128)(2,1)S(1)}) custom-call(s32[3]{0:T(128)S(1)} %pad_add_fusion.where_ref, bf16[2,256,1536]{2,1,0:T(8,128)(2,1)S(1)} %copy-done, bf16[2,256,1536]{2,1,0:T(8,128)(2,1)S(1)} %collective-permute-done.1.a_twin_ref, ...), custom_call_target="tpu_custom_call" | custom-call | tf_op jit(solution)/shard_map/outer/outer/pallas_call | solution.py:88
  99.7 2.9 %outer.3 = (f32[256,128]{1,0:T(8,128)S(1)}, bf16[544,128]{1,0:T(8,128)(2,1)S(1)}, bf16[544,128]{1,0:T(8,128)(2,1)S(1)}, bf16[544,128]{1,0:T(8,128)(2,1)S(1)}) custom-call(s32[3]{0:T(128)S(1)} %pad_add_fusion.where_ref, bf16[2,256,1536]{2,1,0:T(8,128)(2,1)S(1)} %copy-done, bf16[2,256,1536]{2,1,0:T(8,128)(2,1)S(1)} %collective-permute-done.1.a_twin_ref, ...), custom_call_target="tpu_custom_call" | custom-call | tf_op jit(solution)/shard_map/outer/outer/pallas_call | solution.py:88
  102.7 2.5 %collective-permute-start.29 = (bf16[544,128]{1,0:T(8,128)(2,1)S(1)}, bf16[544,128]{1,0:T(8,128)(2,1)S(1)}, u32[]{:S(2)}, u32[]{:S(2)}) collective-permute-start(bf16[544,128]{1,0:T(8,128)(2,1)S(1)} %get-tuple-element.85), channel_id=1, source_target_pairs={{0,2},{1,3},{2,0},{3,1},{4,6},{5,7},{6,4},{7,5},{8,10},{9,11},{10,... | collective-permute-start | bytes 417800 | tf_op jit(solution)/shard_map/outer/ppermute | solution.py:351
  105.2 1.9 %collective-permute-start.30 = (bf16[544,128]{1,0:T(8,128)(2,1)S(1)}, bf16[544,128]{1,0:T(8,128)(2,1)S(1)}, u32[]{:S(2)}, u32[]{:S(2)}) collective-permute-start(bf16[544,128]{1,0:T(8,128)(2,1)S(1)} %get-tuple-element.86), channel_id=1, source_target_pairs={{0,3},{1,2},{2,1},{3,0},{4,7},{5,6},{6,5},{7,4},{8,11},{9,10},{10,... | collective-permute-start | bytes 417800 | tf_op jit(solution)/shard_map/outer/ppermute | solution.py:351
  107.1 2.1 %collective-permute-done.28.refs_2_ = bf16[544,128]{1,0:T(8,128)(2,1)S(1)} collective-permute-done((bf16[544,128]{1,0:T(8,128)(2,1)S(1)}, bf16[544,128]{1,0:T(8,128)(2,1)S(1)}, u32[]{:S(2)}, u32[]{:S(2)}) %collective-permute-start.28) | collective-permute-done | bytes 139296 | tf_op jit(solution)/shard_map/outer/ppermute | solution.py:351
  110.3 1.8 %collective-permute-done.30.refs_4_ = bf16[544,128]{1,0:T(8,128)(2,1)S(1)} collective-permute-done((bf16[544,128]{1,0:T(8,128)(2,1)S(1)}, bf16[544,128]{1,0:T(8,128)(2,1)S(1)}, u32[]{:S(2)}, u32[]{:S(2)}) %collective-permute-start.30) | collective-permute-done | bytes 139296 | tf_op jit(solution)/shard_map/outer/ppermute | solution.py:351
  (56 shorter events, 22.8 us)
Async XLA Ops:
  0.0 2.3 %collective-permute-start = (bf16[2,128,768]{2,1,0:T(8,128)(2,1)}, bf16[2,128,768]{2,1,0:T(8,128)(2,1)S(1)}, u32[]{:S(2)}, u32[]{:S(2)}) collective-permute-start(bf16[2,128,768]{2,1,0:T(8,128)(2,1)} %far_ref.1), channel_id=1, source_target_pairs={{0,4},{4,0},{8,12},{12,8},{16,20},{20,16},{24,28},{28,24},{1,5},{5... | collective-permute-start | bytes 1179656 | tf_op jit(solution)/shard_map/spread_vv/ppermute | solution.py:348
  2.9 21.7 %collective-permute-start.2 = (bf16[2,768,1536]{2,1,0:T(8,128)(2,1)}, bf16[2,768,1536]{2,1,0:T(8,128)(2,1)S(1)}, u32[]{:S(2)}, u32[]{:S(2)}) collective-permute-start(bf16[2,768,1536]{2,1,0:T(8,128)(2,1)} %far_ref.2), channel_id=1, source_target_pairs={{0,4},{4,0},{8,12},{12,8},{16,20},{20,16},{24,28},{28,24},{1,5},{5... | collective-permute-start | bytes 14155784 | tf_op jit(solution)/shard_map/spread_vv/ppermute | solution.py:348
  3.0 21.6 %collective-permute-start.1 = (bf16[2,256,1536]{2,1,0:T(8,128)(2,1)}, bf16[2,256,1536]{2,1,0:T(8,128)(2,1)S(1)}, u32[]{:S(2)}, u32[]{:S(2)}) collective-permute-start(bf16[2,256,1536]{2,1,0:T(8,128)(2,1)} %a_own_ref.3), channel_id=1, source_target_pairs={{0,4},{4,0},{8,12},{12,8},{16,20},{20,16},{24,28},{28,24},{1,5},{5... | collective-permute-start | bytes 4718600 | tf_op jit(solution)/shard_map/spread_vv/ppermute | solution.py:348
  3.4 6.0 %collective-permute-start.3 = (bf16[32,1536]{1,0:T(8,128)(2,1)S(1)}, bf16[32,1536]{1,0:T(8,128)(2,1)S(1)}, u32[]{:S(2)}, u32[]{:S(2)}) collective-permute-start(bf16[32,1536]{1,0:T(8,128)(2,1)S(1)} %get-tuple-element.48), channel_id=1, source_target_pairs={{0,8},{4,12},{8,0},{12,4},{16,24},{20,28},{24,16},{28,20},{1,9},{5... | collective-permute-start | bytes 294920 | tf_op jit(solution)/shard_map/spread_vv/ppermute | solution.py:345
  6.0 6.0 %collective-permute-start.4 = (bf16[32,1536]{1,0:T(8,128)(2,1)S(1)}, bf16[32,1536]{1,0:T(8,128)(2,1)S(1)}, u32[]{:S(2)}, u32[]{:S(2)}) collective-permute-start(bf16[32,1536]{1,0:T(8,128)(2,1)S(1)} %get-tuple-element.49), channel_id=1, source_target_pairs={{0,16},{4,20},{8,24},{12,28},{16,0},{20,4},{24,8},{28,12},{1,17},{... | collective-permute-start | bytes 294920 | tf_op jit(solution)/shard_map/spread_vv/ppermute | solution.py:345
  7.6 5.5 %collective-permute-start.5 = (bf16[32,1536]{1,0:T(8,128)(2,1)S(1)}, bf16[32,1536]{1,0:T(8,128)(2,1)S(1)}, u32[]{:S(2)}, u32[]{:S(2)}) collective-permute-start(bf16[32,1536]{1,0:T(8,128)(2,1)S(1)} %get-tuple-element.50), channel_id=1, source_target_pairs={{0,24},{4,28},{8,16},{12,20},{16,8},{20,12},{24,0},{28,4},{1,25},{... | collective-permute-start | bytes 294920 | tf_op jit(solution)/shard_map/spread_vv/ppermute | solution.py:345
  13.7 7.7 %collective-permute-start.6 = (bf16[32,1536]{1,0:T(8,128)(2,1)S(1)}, bf16[32,1536]{1,0:T(8,128)(2,1)S(1)}, u32[]{:S(2)}, u32[]{:S(2)}) collective-permute-start(bf16[32,1536]{1,0:T(8,128)(2,1)S(1)} %get-tuple-element.54), channel_id=1, source_target_pairs={{0,1},{1,0},{2,3},{3,2},{4,5},{5,4},{6,7},{7,6},{8,9},{9,8},{10,11... | collective-permute-start | bytes 294920 | tf_op jit(solution)/shard_map/spread_vv/ppermute | solution.py:351
  15.3 9.3 %collective-permute-start.7 = (bf16[32,1536]{1,0:T(8,128)(2,1)S(1)}, bf16[32,1536]{1,0:T(8,128)(2,1)S(1)}, u32[]{:S(2)}, u32[]{:S(2)}) collective-permute-start(bf16[32,1536]{1,0:T(8,128)(2,1)S(1)} %get-tuple-element.55), channel_id=1, source_target_pairs={{0,2},{1,3},{2,0},{3,1},{4,6},{5,7},{6,4},{7,5},{8,10},{9,11},{10,... | collective-permute-start | bytes 294920 | tf_op jit(solution)/shard_map/spread_vv/ppermute | solution.py:351
  17.9 6.7 %collective-permute-start.8 = (bf16[32,1536]{1,0:T(8,128)(2,1)S(1)}, bf16[32,1536]{1,0:T(8,128)(2,1)S(1)}, u32[]{:S(2)}, u32[]{:S(2)}) collective-permute-start(bf16[32,1536]{1,0:T(8,128)(2,1)S(1)} %get-tuple-element.56), channel_id=1, source_target_pairs={{0,3},{1,2},{2,1},{3,0},{4,7},{5,6},{6,5},{7,4},{8,11},{9,10},{10,... | collective-permute-start | bytes 294920 | tf_op jit(solution)/shard_map/spread_vv/ppermute | solution.py:351
  25.2 12.2 %collective-permute-start.9 = (bf16[128,1536]{1,0:T(8,128)(2,1)S(1)}, bf16[128,1536]{1,0:T(8,128)(2,1)S(1)}, u32[]{:S(2)}, u32[]{:S(2)}) collective-permute-start(bf16[128,1536]{1,0:T(8,128)(2,1)S(1)} %chunk_vv.1.refs_0_), channel_id=1, source_target_pairs={{0,8},{4,12},{8,0},{12,4},{16,24},{20,28},{24,16},{28,20},{1,9},{5... | collective-permute-start | bytes 1179656 | tf_op jit(solution)/shard_map/inner/ppermute | solution.py:345
  27.3 13.6 %collective-permute-start.10 = (bf16[128,1536]{1,0:T(8,128)(2,1)S(1)}, bf16[128,1536]{1,0:T(8,128)(2,1)S(1)}, u32[]{:S(2)}, u32[]{:S(2)}) collective-permute-start(bf16[128,1536]{1,0:T(8,128)(2,1)S(1)} %chunk_vv.1.refs_0_), channel_id=1, source_target_pairs={{0,16},{4,20},{8,24},{12,28},{16,0},{20,4},{24,8},{28,12},{1,17},{... | collective-permute-start | bytes 1179656 | tf_op jit(solution)/shard_map/inner/ppermute | solution.py:345
  27.9 20.3 %collective-permute-start.13 = (bf16[128,1536]{1,0:T(8,128)(2,1)S(1)}, bf16[128,1536]{1,0:T(8,128)(2,1)S(1)}, u32[]{:S(2)}, u32[]{:S(2)}) collective-permute-start(bf16[128,1536]{1,0:T(8,128)(2,1)S(1)} %chunk_vv.1.refs_0_), channel_id=1, source_target_pairs={{0,24},{4,28},{8,16},{12,20},{16,8},{20,12},{24,0},{28,4},{1,25},{... | collective-permute-start | bytes 1179656 | tf_op jit(solution)/shard_map/inner/ppermute | solution.py:345
  45.7 9.9 %collective-permute-start.11 = (bf16[784,128]{1,0:T(8,128)(2,1)S(1)}, bf16[784,128]{1,0:T(8,128)(2,1)S(1)}, u32[]{:S(2)}, u32[]{:S(2)}) collective-permute-start(bf16[784,128]{1,0:T(8,128)(2,1)S(1)} %get-tuple-element.62), channel_id=1, source_target_pairs={{0,8},{4,12},{8,0},{12,4},{16,24},{20,28},{24,16},{28,20},{1,9},{5... | collective-permute-start | bytes 602120 | tf_op jit(solution)/shard_map/move_inner/ppermute | solution.py:345
  45.8 10.9 %collective-permute-start.12 = (bf16[784,128]{1,0:T(8,128)(2,1)S(1)}, bf16[784,128]{1,0:T(8,128)(2,1)S(1)}, u32[]{:S(2)}, u32[]{:S(2)}) collective-permute-start(bf16[784,128]{1,0:T(8,128)(2,1)S(1)} %get-tuple-element.63), channel_id=1, source_target_pairs={{0,16},{4,20},{8,24},{12,28},{16,0},{20,4},{24,8},{28,12},{1,17},{... | collective-permute-start | bytes 602120 | tf_op jit(solution)/shard_map/move_inner/ppermute | solution.py:345
  52.1 6.8 %collective-permute-start.14 = (bf16[784,128]{1,0:T(8,128)(2,1)S(1)}, bf16[784,128]{1,0:T(8,128)(2,1)S(1)}, u32[]{:S(2)}, u32[]{:S(2)}) collective-permute-start(bf16[784,128]{1,0:T(8,128)(2,1)S(1)} %get-tuple-element.64), channel_id=1, source_target_pairs={{0,24},{4,28},{8,16},{12,20},{16,8},{20,12},{24,0},{28,4},{1,25},{... | collective-permute-start | bytes 602120 | tf_op jit(solution)/shard_map/move_inner/ppermute | solution.py:345
  53.2 10.1 %collective-permute-start.20 = (bf16[784,128]{1,0:T(8,128)(2,1)S(1)}, bf16[784,128]{1,0:T(8,128)(2,1)S(1)}, u32[]{:S(2)}, u32[]{:S(2)}) collective-permute-start(bf16[784,128]{1,0:T(8,128)(2,1)S(1)} %get-tuple-element.72), channel_id=1, source_target_pairs={{0,8},{4,12},{8,0},{12,4},{16,24},{20,28},{24,16},{28,20},{1,9},{5... | collective-permute-start | bytes 602120 | tf_op jit(solution)/shard_map/move_inner/ppermute | solution.py:345
  53.6 9.7 %collective-permute-start.21 = (bf16[784,128]{1,0:T(8,128)(2,1)S(1)}, bf16[784,128]{1,0:T(8,128)(2,1)S(1)}, u32[]{:S(2)}, u32[]{:S(2)}) collective-permute-start(bf16[784,128]{1,0:T(8,128)(2,1)S(1)} %get-tuple-element.73), channel_id=1, source_target_pairs={{0,16},{4,20},{8,24},{12,28},{16,0},{20,4},{24,8},{28,12},{1,17},{... | collective-permute-start | bytes 602120 | tf_op jit(solution)/shard_map/move_inner/ppermute | solution.py:345
  55.6 7.6 %collective-permute-start.22 = (bf16[784,128]{1,0:T(8,128)(2,1)S(1)}, bf16[784,128]{1,0:T(8,128)(2,1)S(1)}, u32[]{:S(2)}, u32[]{:S(2)}) collective-permute-start(bf16[784,128]{1,0:T(8,128)(2,1)S(1)} %get-tuple-element.74), channel_id=1, source_target_pairs={{0,24},{4,28},{8,16},{12,20},{16,8},{20,12},{24,0},{28,4},{1,25},{... | collective-permute-start | bytes 602120 | tf_op jit(solution)/shard_map/move_inner/ppermute | solution.py:345
  59.6 13.3 %collective-permute-start.15 = (bf16[1568,128]{1,0:T(8,128)(2,1)S(1)}, bf16[1568,128]{1,0:T(8,128)(2,1)S(1)}, u32[]{:S(2)}, u32[]{:S(2)}) collective-permute-start(bf16[1568,128]{1,0:T(8,128)(2,1)S(1)} %get-tuple-element.67), channel_id=1, source_target_pairs={{0,1},{1,0},{2,3},{3,2},{4,5},{5,4},{6,7},{7,6},{8,9},{9,8},{10,11... | collective-permute-start | bytes 1204232 | tf_op jit(solution)/shard_map/move_inner/ppermute | solution.py:351
  63.9 17.6 %collective-permute-start.23 = (bf16[1568,128]{1,0:T(8,128)(2,1)S(1)}, bf16[1568,128]{1,0:T(8,128)(2,1)S(1)}, u32[]{:S(2)}, u32[]{:S(2)}) collective-permute-start(bf16[1568,128]{1,0:T(8,128)(2,1)S(1)} %get-tuple-element.77), channel_id=1, source_target_pairs={{0,1},{1,0},{2,3},{3,2},{4,5},{5,4},{6,7},{7,6},{8,9},{9,8},{10,11... | collective-permute-start | bytes 1204232 | tf_op jit(solution)/shard_map/move_inner/ppermute | solution.py:351
  73.8 8.7 %collective-permute-start.16 = (bf16[784,128]{1,0:T(8,128)(2,1)S(1)}, bf16[784,128]{1,0:T(8,128)(2,1)S(1)}, u32[]{:S(2)}, u32[]{:S(2)}) collective-permute-start(bf16[784,128]{1,0:T(8,128)(2,1)S(1)} %get-tuple-element.69), channel_id=1, source_target_pairs={{0,2},{1,3},{2,0},{3,1},{4,6},{5,7},{6,4},{7,5},{8,10},{9,11},{10,... | collective-permute-start | bytes 602120 | tf_op jit(solution)/shard_map/move_inner/ppermute | solution.py:351
  82.4 7.9 %collective-permute-start.24 = (bf16[784,128]{1,0:T(8,128)(2,1)S(1)}, bf16[784,128]{1,0:T(8,128)(2,1)S(1)}, u32[]{:S(2)}, u32[]{:S(2)}) collective-permute-start(bf16[784,128]{1,0:T(8,128)(2,1)S(1)} %get-tuple-element.79), channel_id=1, source_target_pairs={{0,2},{1,3},{2,0},{3,1},{4,6},{5,7},{6,4},{7,5},{8,10},{9,11},{10,... | collective-permute-start | bytes 602120 | tf_op jit(solution)/shard_map/move_inner/ppermute | solution.py:351
  83.3 9.8 %collective-permute-start.17 = (bf16[784,128]{1,0:T(8,128)(2,1)S(1)}, bf16[784,128]{1,0:T(8,128)(2,1)S(1)}, u32[]{:S(2)}, u32[]{:S(2)}) collective-permute-start(bf16[784,128]{1,0:T(8,128)(2,1)S(1)} %sum_inner.2.refs_0_), channel_id=1, source_target_pairs={{0,8},{4,12},{8,0},{12,4},{16,24},{20,28},{24,16},{28,20},{1,9},{5... | collective-permute-start | bytes 602120 | tf_op jit(solution)/shard_map/outer/ppermute | solution.py:345
  83.5 11.1 %collective-permute-start.18 = (bf16[784,128]{1,0:T(8,128)(2,1)S(1)}, bf16[784,128]{1,0:T(8,128)(2,1)S(1)}, u32[]{:S(2)}, u32[]{:S(2)}) collective-permute-start(bf16[784,128]{1,0:T(8,128)(2,1)S(1)} %sum_inner.2.refs_0_), channel_id=1, source_target_pairs={{0,16},{4,20},{8,24},{12,28},{16,0},{20,4},{24,8},{28,12},{1,17},{... | collective-permute-start | bytes 602120 | tf_op jit(solution)/shard_map/outer/ppermute | solution.py:345
  85.4 9.3 %collective-permute-start.19 = (bf16[784,128]{1,0:T(8,128)(2,1)S(1)}, bf16[784,128]{1,0:T(8,128)(2,1)S(1)}, u32[]{:S(2)}, u32[]{:S(2)}) collective-permute-start(bf16[784,128]{1,0:T(8,128)(2,1)S(1)} %sum_inner.2.refs_0_), channel_id=1, source_target_pairs={{0,24},{4,28},{8,16},{12,20},{16,8},{20,12},{24,0},{28,4},{1,25},{... | collective-permute-start | bytes 602120 | tf_op jit(solution)/shard_map/outer/ppermute | solution.py:345
  91.1 6.5 %collective-permute-start.25 = (bf16[784,128]{1,0:T(8,128)(2,1)S(1)}, bf16[784,128]{1,0:T(8,128)(2,1)S(1)}, u32[]{:S(2)}, u32[]{:S(2)}) collective-permute-start(bf16[784,128]{1,0:T(8,128)(2,1)S(1)} %sum_inner.3.refs_0_), channel_id=1, source_target_pairs={{0,8},{4,12},{8,0},{12,4},{16,24},{20,28},{24,16},{28,20},{1,9},{5... | collective-permute-start | bytes 602120 | tf_op jit(solution)/shard_map/outer/ppermute | solution.py:345
  91.3 7.3 %collective-permute-start.26 = (bf16[784,128]{1,0:T(8,128)(2,1)S(1)}, bf16[784,128]{1,0:T(8,128)(2,1)S(1)}, u32[]{:S(2)}, u32[]{:S(2)}) collective-permute-start(bf16[784,128]{1,0:T(8,128)(2,1)S(1)} %sum_inner.3.refs_0_), channel_id=1, source_target_pairs={{0,16},{4,20},{8,24},{12,28},{16,0},{20,4},{24,8},{28,12},{1,17},{... | collective-permute-start | bytes 602120 | tf_op jit(solution)/shard_map/outer/ppermute | solution.py:345
  93.1 6.6 %collective-permute-start.27 = (bf16[784,128]{1,0:T(8,128)(2,1)S(1)}, bf16[784,128]{1,0:T(8,128)(2,1)S(1)}, u32[]{:S(2)}, u32[]{:S(2)}) collective-permute-start(bf16[784,128]{1,0:T(8,128)(2,1)S(1)} %sum_inner.3.refs_0_), channel_id=1, source_target_pairs={{0,24},{4,28},{8,16},{12,20},{16,8},{20,12},{24,0},{28,4},{1,25},{... | collective-permute-start | bytes 602120 | tf_op jit(solution)/shard_map/outer/ppermute | solution.py:345
  102.6 6.6 %collective-permute-start.28 = (bf16[544,128]{1,0:T(8,128)(2,1)S(1)}, bf16[544,128]{1,0:T(8,128)(2,1)S(1)}, u32[]{:S(2)}, u32[]{:S(2)}) collective-permute-start(bf16[544,128]{1,0:T(8,128)(2,1)S(1)} %get-tuple-element.84), channel_id=1, source_target_pairs={{0,1},{1,0},{2,3},{3,2},{4,5},{5,4},{6,7},{7,6},{8,9},{9,8},{10,11... | collective-permute-start | bytes 417800 | tf_op jit(solution)/shard_map/outer/ppermute | solution.py:351
  102.7 7.6 %collective-permute-start.29 = (bf16[544,128]{1,0:T(8,128)(2,1)S(1)}, bf16[544,128]{1,0:T(8,128)(2,1)S(1)}, u32[]{:S(2)}, u32[]{:S(2)}) collective-permute-start(bf16[544,128]{1,0:T(8,128)(2,1)S(1)} %get-tuple-element.85), channel_id=1, source_target_pairs={{0,2},{1,3},{2,0},{3,1},{4,6},{5,7},{6,4},{7,5},{8,10},{9,11},{10,... | collective-permute-start | bytes 417800 | tf_op jit(solution)/shard_map/outer/ppermute | solution.py:351
  105.2 6.9 %collective-permute-start.30 = (bf16[544,128]{1,0:T(8,128)(2,1)S(1)}, bf16[544,128]{1,0:T(8,128)(2,1)S(1)}, u32[]{:S(2)}, u32[]{:S(2)}) collective-permute-start(bf16[544,128]{1,0:T(8,128)(2,1)S(1)} %get-tuple-element.86), channel_id=1, source_target_pairs={{0,3},{1,2},{2,1},{3,0},{4,7},{5,6},{6,5},{7,4},{8,11},{9,10},{10,... | collective-permute-start | bytes 417800 | tf_op jit(solution)/shard_map/outer/ppermute | solution.py:351
  112.8 1.4 %collective-permute-start.31 = (f32[2,64,256]{2,1,0:T(8,128)S(1)}, f32[2,64,256]{2,1,0:T(8,128)S(1)}, u32[]{:S(2)}, u32[]{:S(2)}) collective-permute-start(f32[2,64,256]{2,1,0:T(8,128)S(1)} %get-tuple-element.88), channel_id=1, source_target_pairs={{0,4},{4,0},{8,12},{12,8},{16,20},{20,16},{24,28},{28,24},{1,5},{5... | collective-permute-start | bytes 393224 | tf_op jit(solution)/shard_map/sum_outer/ppermute | solution.py:348
  (3 other events, 45.9 us)
